TPU v7x, 32 devices: a whole 2x2x4 slice. The times are simulated.
32 devices in a mesh: layer: 2 (over y), row: 8 (over z, core), col: 2 (over x).
Axes of the slice: x: 2, y: 2, z: 4, core: 2. Of those that a mesh axis runs over, the one named last changes fastest.
Arguments:
- a_val: float32 [2, 2, 8, 2, 64, 512], P('col', 'layer', 'row'), may hold values from -3 to 3
- a_rows: int32 [2, 2, 8, 2, 8], P('col', 'layer', 'row'), may hold values from 0 to 63, as said below
- b_val: float32 [8, 2, 2, 4, 2, 64, 512], P('row', 'layer', 'col'), may hold values from -3 to 3
- b_cols: int32 [8, 2, 2, 4, 2, 8], P('row', 'layer', 'col'), may hold values from 0 to 63, as said below
- pattern: int32 [2, 8, 256], P('col', 'row'), may hold values from 0 to 4095, as said below
- owners: int32 [2, 2048, 1], P('col', 'row'), may hold values from 0 to 15; in each aligned block of 256 rows (0 to 255, 256 to 511, ..., all dimensions but the last counted through in order) at most 16 rows name the same one
Outputs:
- owned: float32 [2048, 8192], P(('layer', 'row'), 'col')
Inputs may be any that keep to these rules, and one draw needn't show every extreme that they name: `a_rows`: for one k, the 8 block rows of A's block column k in a group are distinct and lie in s_k, s_k + 1, ..., s_k + 16 - 1 modulo 64, with s_k the same for every group and for B's block row k. `b_cols`: for one k, the 8 block columns of B's block row k in a group are distinct and lie in s_k, ..., s_k + 16 - 1 modulo 64, with the s_k of A. `pattern`: the 256 entries of one tile are distinct, and for each, (row - column) mod 64 is at most 4 or at least 60. `owners`: at most 16 kept blocks of one tile share an owner, and in every draw some tile has 16 with one owner.
All inputs are finite; a program needn't handle non-finite values.
Results may differ from a plain program's by a relative error of at most 0.0001.
Values sent between devices are 32-bit elements; how exact they have to be, the bound alone decides.
No kernel may reach another device: no remote copies, remote signals or barrier semaphores. Data moves between devices by JAX's collectives and lax.ppermute only.
A program may use at most 64 MiB of HBM per device.

v0:
```python
import jax
import jax.numpy as jnp
from jax import lax
from jax.sharding import PartitionSpec as P

TILE = 64
CAP = 16


def from_behind(block, axis, distance):
    devices = range(lax.axis_size(axis))
    route = [((i - distance) % len(devices), i) for i in devices]
    return lax.ppermute(block, axis, route)


def panel_products(total, a_panel, a_index, b_panel, b_index, table):
    count = a_panel.shape[0]
    block = a_panel.shape[1]
    many_a = a_index.shape[1]
    many_b = b_index.shape[1]
    kept_count = total.shape[0]
    a_four = a_panel.reshape(count, block, many_a, block)
    b_four = b_panel.reshape(count, block, many_b, block)
    prod = jnp.einsum(
        "kxap,kxbq->kabpq",
        a_four,
        b_four,
        precision=lax.Precision.HIGHEST,
        preferred_element_type=jnp.float32,
    )
    prod = prod.reshape(count * many_a * many_b, block * block)
    target = table[a_index[:, :, None] * TILE + b_index[:, None, :]].reshape(-1)
    selector = (target[:, None] == jnp.arange(kept_count, dtype=jnp.int32)[None, :]).astype(
        jnp.float32
    )
    return total + jnp.einsum(
        "sn,sd->nd",
        selector,
        prod,
        precision=lax.Precision.HIGHEST,
        preferred_element_type=jnp.float32,
    )


def body(a_val, a_rows, b_val, b_cols, pattern, owners):
    block = a_val.shape[4]
    span = block * block
    kept_count = pattern.shape[2]
    n_row = lax.axis_size("row")
    n_col = lax.axis_size("col")
    n_layer = lax.axis_size("layer")
    table = (
        jnp.full((TILE * TILE,), kept_count, jnp.int32)
        .at[pattern[0, 0]]
        .set(jnp.arange(kept_count, dtype=jnp.int32))
    )
    start_total = jnp.zeros((kept_count, span), jnp.float32)
    my_col = lax.axis_index("col")
    sets_count = b_val.shape[3]

    def pick_set(b_pair, step):
        which = (step + my_col) // n_col % sets_count
        vals = lax.dynamic_index_in_dim(b_pair[0][0, 0, 0], which, 0, keepdims=False)
        cols = lax.dynamic_index_in_dim(b_pair[1][0, 0, 0], which, 0, keepdims=False)
        return (vals, cols)

    def advance(step, state):
        total, a_pair, b_pair = state
        b_now, b_index = pick_set(b_pair, step)
        total = panel_products(total, a_pair[0][0, 0, 0], a_pair[1][0, 0, 0], b_now, b_index, table)
        a_pair = from_behind((a_pair[0], a_pair[1]), "row", -1)
        b_pair = from_behind((b_pair[0], b_pair[1]), "col", -1)
        return (total, a_pair, b_pair)

    total, a_pair, b_pair = lax.fori_loop(
        0, n_row - 1, advance, (start_total, (a_val, a_rows), (b_val, b_cols))
    )
    b_now, b_index = pick_set(b_pair, n_row - 1)
    total = panel_products(total, a_pair[0][0, 0, 0], a_pair[1][0, 0, 0], b_now, b_index, table)
    owner_list = owners[0, :, 0]
    n_owner = n_layer * n_row
    onehot = (owner_list[:, None] == jnp.arange(n_owner, dtype=jnp.int32)[None, :]).astype(
        jnp.int32
    )
    rank = jnp.sum((jnp.cumsum(onehot, axis=0) - onehot) * onehot, axis=1)
    outgoing = jnp.zeros((n_owner, CAP, span), jnp.float32).at[owner_list, rank].set(total)
    arrived = lax.all_to_all(outgoing, ("layer", "row"), split_axis=0, concat_axis=0, tiled=True)
    owned = jnp.sum(arrived.reshape(n_layer, n_row * CAP, span), axis=0)
    return owned


def solution(mesh):
    return jax.shard_map(
        body,
        mesh=mesh,
        in_specs=(
            P("col", "layer", "row", None, None, None),
            P("col", "layer", "row", None, None),
            P("row", "layer", "col", None, None, None, None),
            P("row", "layer", "col", None, None, None),
            P("col", "row", None),
            P("col", "row", None),
        ),
        out_specs=P(("layer", "row"), "col"),
        check_vma=False,
    )
```

profile of v0, /device:TPU:0, one launch (start us, length us, event | category | flops | bytes accessed | tf_op | source)
XLA Modules:
  0.0 388.1 jit_solution(16627375370125983639)
XLA Ops:
  7.5 192.2 %while.24 = (s32[]{:T(128)}, f32[256,4096]{1,0:T(8,128)}, f32[1,1,1,2,64,512]{5,4,3,2,1,0:T(8,128)}, s32[1,1,1,2,8]{4,3,2,1,0:T(2,128)S(1)}, f32[1,1,1,4,2,64,51...) while((s32[]{:T(128)}, f32[256,4096]{1,0:T(8,128)}, ...), condition=%wide.region_5.6_spmd.clone, body=%wide.region_4.5_spmd.clone.sunk | while | flops 2015397376 | bytes 30944096 | solution.py:75
  17.0 5.0 %convolution_bitcast_fusion.3 = f32[2,8,8,64,64]{3,4,1,2,0:T(8,128)} fusion(f32[2,64,8,64,1]{1,3,4,2,0:T(8,128)S(1)} %bitcast.90, f32[2,64,8,64,1]{3,2,1,0,4:T(8,128)S(1)} %bitcast.89), kind=kOutput, calls=%fused_computation.5.clone.1 | convolution fusion | flops 402653184 | bytes 2621440 | tf_op jit(solution)/shard_map/while/body/eval_jaxpr/kxap,kxbq->kabpq/dot_general | solution.py:24
  22.0 5.4 %copy.49 = f32[2,8,8,64,64]{4,3,2,1,0:T(8,128)} copy(f32[2,8,8,64,64]{3,4,1,2,0:T(8,128)} %convolution_bitcast_fusion.3) | data formatting | bytes 4194304 | tf_op jit(solution)/shard_map/while/body/eval_jaxpr/kxap,kxbq->kabpq/transpose | solution.py:24
  27.3 3.5 reshape.237
  32.2 4.1 %convolution_add_fusion.3 = f32[256,4096]{1,0:T(8,128)} fusion(f32[128,4096]{1,0:T(8,128)S(1)} %reshape.237, f32[256,4096]{1,0:T(8,128)} %get-tuple-element.337, pred[]{:T(512)S(6)} %compare.23, s32[128]{0:T(128)S(1)} %gather_fusion), kind=kOutput, calls=%fused_computation.4.clone.1 | convolution fusion | flops 1612742656 | bytes 10486273 | tf_op jit(solution)/shard_map/while/body/eval_jaxpr/sn,sd->nd/dot_general | solution.py:36
  43.3 5.0 %convolution_bitcast_fusion.3 = f32[2,8,8,64,64]{3,4,1,2,0:T(8,128)} fusion(f32[2,64,8,64,1]{1,3,4,2,0:T(8,128)S(1)} %bitcast.90, f32[2,64,8,64,1]{3,2,1,0,4:T(8,128)S(1)} %bitcast.89), kind=kOutput, calls=%fused_computation.5.clone.1 | convolution fusion | flops 402653184 | bytes 2621440 | tf_op jit(solution)/shard_map/while/body/eval_jaxpr/kxap,kxbq->kabpq/dot_general | solution.py:24
  48.2 5.4 %copy.49 = f32[2,8,8,64,64]{4,3,2,1,0:T(8,128)} copy(f32[2,8,8,64,64]{3,4,1,2,0:T(8,128)} %convolution_bitcast_fusion.3) | data formatting | bytes 4194304 | tf_op jit(solution)/shard_map/while/body/eval_jaxpr/kxap,kxbq->kabpq/transpose | solution.py:24
  53.6 3.5 reshape.237
  58.5 6.2 %convolution_add_fusion.3 = f32[256,4096]{1,0:T(8,128)} fusion(f32[128,4096]{1,0:T(8,128)S(1)} %reshape.237, f32[256,4096]{1,0:T(8,128)} %get-tuple-element.337, pred[]{:T(512)S(6)} %compare.23, s32[128]{0:T(128)S(1)} %gather_fusion), kind=kOutput, calls=%fused_computation.4.clone.1 | convolution fusion | flops 1612742656 | bytes 10486273 | tf_op jit(solution)/shard_map/while/body/eval_jaxpr/sn,sd->nd/dot_general | solution.py:36
  69.6 5.0 %convolution_bitcast_fusion.3 = f32[2,8,8,64,64]{3,4,1,2,0:T(8,128)} fusion(f32[2,64,8,64,1]{1,3,4,2,0:T(8,128)S(1)} %bitcast.90, f32[2,64,8,64,1]{3,2,1,0,4:T(8,128)S(1)} %bitcast.89), kind=kOutput, calls=%fused_computation.5.clone.1 | convolution fusion | flops 402653184 | bytes 2621440 | tf_op jit(solution)/shard_map/while/body/eval_jaxpr/kxap,kxbq->kabpq/dot_general | solution.py:24
  74.6 5.4 %copy.49 = f32[2,8,8,64,64]{4,3,2,1,0:T(8,128)} copy(f32[2,8,8,64,64]{3,4,1,2,0:T(8,128)} %convolution_bitcast_fusion.3) | data formatting | bytes 4194304 | tf_op jit(solution)/shard_map/while/body/eval_jaxpr/kxap,kxbq->kabpq/transpose | solution.py:24
  84.8 6.2 %convolution_add_fusion.3 = f32[256,4096]{1,0:T(8,128)} fusion(f32[128,4096]{1,0:T(8,128)S(1)} %reshape.237, f32[256,4096]{1,0:T(8,128)} %get-tuple-element.337, pred[]{:T(512)S(6)} %compare.23, s32[128]{0:T(128)S(1)} %gather_fusion), kind=kOutput, calls=%fused_computation.4.clone.1 | convolution fusion | flops 1612742656 | bytes 10486273 | tf_op jit(solution)/shard_map/while/body/eval_jaxpr/sn,sd->nd/dot_general | solution.py:36
  96.3 5.0 %convolution_bitcast_fusion.3 = f32[2,8,8,64,64]{3,4,1,2,0:T(8,128)} fusion(f32[2,64,8,64,1]{1,3,4,2,0:T(8,128)S(1)} %bitcast.90, f32[2,64,8,64,1]{3,2,1,0,4:T(8,128)S(1)} %bitcast.89), kind=kOutput, calls=%fused_computation.5.clone.1 | convolution fusion | flops 402653184 | bytes 2621440 | tf_op jit(solution)/shard_map/while/body/eval_jaxpr/kxap,kxbq->kabpq/dot_general | solution.py:24
  101.3 5.4 %copy.49 = f32[2,8,8,64,64]{4,3,2,1,0:T(8,128)} copy(f32[2,8,8,64,64]{3,4,1,2,0:T(8,128)} %convolution_bitcast_fusion.3) | data formatting | bytes 4194304 | tf_op jit(solution)/shard_map/while/body/eval_jaxpr/kxap,kxbq->kabpq/transpose | solution.py:24
  111.5 6.2 %convolution_add_fusion.3 = f32[256,4096]{1,0:T(8,128)} fusion(f32[128,4096]{1,0:T(8,128)S(1)} %reshape.237, f32[256,4096]{1,0:T(8,128)} %get-tuple-element.337, pred[]{:T(512)S(6)} %compare.23, s32[128]{0:T(128)S(1)} %gather_fusion), kind=kOutput, calls=%fused_computation.4.clone.1 | convolution fusion | flops 1612742656 | bytes 10486273 | tf_op jit(solution)/shard_map/while/body/eval_jaxpr/sn,sd->nd/dot_general | solution.py:36
  123.4 5.0 %convolution_bitcast_fusion.3 = f32[2,8,8,64,64]{3,4,1,2,0:T(8,128)} fusion(f32[2,64,8,64,1]{1,3,4,2,0:T(8,128)S(1)} %bitcast.90, f32[2,64,8,64,1]{3,2,1,0,4:T(8,128)S(1)} %bitcast.89), kind=kOutput, calls=%fused_computation.5.clone.1 | convolution fusion | flops 402653184 | bytes 2621440 | tf_op jit(solution)/shard_map/while/body/eval_jaxpr/kxap,kxbq->kabpq/dot_general | solution.py:24
  128.4 5.4 %copy.49 = f32[2,8,8,64,64]{4,3,2,1,0:T(8,128)} copy(f32[2,8,8,64,64]{3,4,1,2,0:T(8,128)} %convolution_bitcast_fusion.3) | data formatting | bytes 4194304 | tf_op jit(solution)/shard_map/while/body/eval_jaxpr/kxap,kxbq->kabpq/transpose | solution.py:24
  133.8 3.5 reshape.237
  138.6 6.2 %convolution_add_fusion.3 = f32[256,4096]{1,0:T(8,128)} fusion(f32[128,4096]{1,0:T(8,128)S(1)} %reshape.237, f32[256,4096]{1,0:T(8,128)} %get-tuple-element.337, pred[]{:T(512)S(6)} %compare.23, s32[128]{0:T(128)S(1)} %gather_fusion), kind=kOutput, calls=%fused_computation.4.clone.1 | convolution fusion | flops 1612742656 | bytes 10486273 | tf_op jit(solution)/shard_map/while/body/eval_jaxpr/sn,sd->nd/dot_general | solution.py:36
  151.9 5.0 %convolution_bitcast_fusion.3 = f32[2,8,8,64,64]{3,4,1,2,0:T(8,128)} fusion(f32[2,64,8,64,1]{1,3,4,2,0:T(8,128)S(1)} %bitcast.90, f32[2,64,8,64,1]{3,2,1,0,4:T(8,128)S(1)} %bitcast.89), kind=kOutput, calls=%fused_computation.5.clone.1 | convolution fusion | flops 402653184 | bytes 2621440 | tf_op jit(solution)/shard_map/while/body/eval_jaxpr/kxap,kxbq->kabpq/dot_general | solution.py:24
  156.9 5.4 %copy.49 = f32[2,8,8,64,64]{4,3,2,1,0:T(8,128)} copy(f32[2,8,8,64,64]{3,4,1,2,0:T(8,128)} %convolution_bitcast_fusion.3) | data formatting | bytes 4194304 | tf_op jit(solution)/shard_map/while/body/eval_jaxpr/kxap,kxbq->kabpq/transpose | solution.py:24
  167.1 6.2 %convolution_add_fusion.3 = f32[256,4096]{1,0:T(8,128)} fusion(f32[128,4096]{1,0:T(8,128)S(1)} %reshape.237, f32[256,4096]{1,0:T(8,128)} %get-tuple-element.337, pred[]{:T(512)S(6)} %compare.23, s32[128]{0:T(128)S(1)} %gather_fusion), kind=kOutput, calls=%fused_computation.4.clone.1 | convolution fusion | flops 1612742656 | bytes 10486273 | tf_op jit(solution)/shard_map/while/body/eval_jaxpr/sn,sd->nd/dot_general | solution.py:36
  178.3 5.0 %convolution_bitcast_fusion.3 = f32[2,8,8,64,64]{3,4,1,2,0:T(8,128)} fusion(f32[2,64,8,64,1]{1,3,4,2,0:T(8,128)S(1)} %bitcast.90, f32[2,64,8,64,1]{3,2,1,0,4:T(8,128)S(1)} %bitcast.89), kind=kOutput, calls=%fused_computation.5.clone.1 | convolution fusion | flops 402653184 | bytes 2621440 | tf_op jit(solution)/shard_map/while/body/eval_jaxpr/kxap,kxbq->kabpq/dot_general | solution.py:24
  183.2 5.4 %copy.49 = f32[2,8,8,64,64]{4,3,2,1,0:T(8,128)} copy(f32[2,8,8,64,64]{3,4,1,2,0:T(8,128)} %convolution_bitcast_fusion.3) | data formatting | bytes 4194304 | tf_op jit(solution)/shard_map/while/body/eval_jaxpr/kxap,kxbq->kabpq/transpose | solution.py:24
  188.6 3.5 reshape.237
  193.5 6.2 %convolution_add_fusion.3 = f32[256,4096]{1,0:T(8,128)} fusion(f32[128,4096]{1,0:T(8,128)S(1)} %reshape.237, f32[256,4096]{1,0:T(8,128)} %get-tuple-element.337, pred[]{:T(512)S(6)} %compare.23, s32[128]{0:T(128)S(1)} %gather_fusion), kind=kOutput, calls=%fused_computation.4.clone.1 | convolution fusion | flops 1612742656 | bytes 10486273 | tf_op jit(solution)/shard_map/while/body/eval_jaxpr/sn,sd->nd/dot_general | solution.py:36
  203.4 5.0 %convolution_bitcast_fusion.1 = f32[2,8,8,64,64]{3,4,1,2,0:T(8,128)} fusion(f32[2,64,8,64,1]{1,3,4,2,0:T(8,128)S(1)} %bitcast.93, f32[2,64,8,64,1]{3,2,1,0,4:T(8,128)S(1)} %bitcast.94), kind=kOutput, calls=%fused_computation.16 | convolution fusion | flops 402653184 | bytes 2621440 | tf_op jit(solution)/shard_map/kxap,kxbq->kabpq/dot_general | solution.py:24
  208.3 5.4 %copy.29 = f32[2,8,8,64,64]{4,3,2,1,0:T(8,128)} copy(f32[2,8,8,64,64]{3,4,1,2,0:T(8,128)} %convolution_bitcast_fusion.1) | data formatting | bytes 4194304 | tf_op jit(solution)/shard_map/kxap,kxbq->kabpq/transpose | solution.py:24
  213.7 3.5 reshape.183
  218.2 6.2 %convolution_add_fusion.1 = f32[256,4096]{1,0:T(8,128)} fusion(f32[256,4096]{1,0:T(8,128)} %get-tuple-element.210, f32[128,4096]{1,0:T(8,128)S(1)} %reshape.183, s32[128]{0:T(128)S(1)} %gather_fusion.1), kind=kOutput, calls=%fused_computation.14 | convolution fusion | flops 1611694080 | bytes 10486272 | tf_op jit(solution)/shard_map/sn,sd->nd/dot_general | solution.py:36
  226.8 63.3 %scatter_fusion = f32[16,16,4096]{2,1,0:T(8,128)} fusion(f32[16,16,4096]{2,1,0:T(8,128)} %broadcast_in_dim.15, s32[256]{0:T(256)S(1)} %bitcast.91, f32[256,4096]{1,0:T(8,128)} %convolution_add_fusion.1), kind=kCustom, calls=%fused_computation.3 | custom fusion | bytes 12584960 | tf_op jit(solution)/shard_map/scatter | solution.py:86
  290.1 96.4 %all_to_all.5 = f32[16,16,4096]{2,1,0:T(8,128)S(1)} all-to-all(f32[16,16,4096]{2,1,0:T(8,128)} %scatter_fusion), channel_id=1, replica_groups=mesh['layer'=2,'row'=8,'col'=2] {'layer','row'}, dimensions={0} | all-to-all | bytes 8388608 | tf_op jit(solution)/shard_map/all_to_all | solution.py:87
  (178 shorter events, 79.8 us)
Async XLA Ops:
  8.7 27.5 %collective-permute-start.2 = (f32[1,1,1,4,2,64,512]{6,5,4,3,2,1,0:T(8,128)S(1)}, f32[1,1,1,4,2,64,512]{6,5,4,3,2,1,0:T(8,128)}, u32[]{:S(2)}, u32[]{:S(2)}) collective-permute-start(f32[1,1,1,4,2,64,512]{6,5,4,3,2,1,0:T(8,128)S(1)} %copy.60), channel_id=1, source_target_pairs={{1,0},{0,1},{3,2},{2,3},{5,4},{4,5},{7,6},{6,7},{9,8},{8,9},{11,10... | collective-permute-start | bytes 3145736 | tf_op jit(solution)/shard_map/while/body/eval_jaxpr/ppermute | solution.py:13
  12.6 23.6 %collective-permute-start = (f32[1,1,1,2,64,512]{5,4,3,2,1,0:T(8,128)S(1)}, f32[1,1,1,2,64,512]{5,4,3,2,1,0:T(8,128)}, u32[]{:S(2)}, u32[]{:S(2)}) collective-permute-start(f32[1,1,1,2,64,512]{5,4,3,2,1,0:T(8,128)S(1)} %copy.58), channel_id=1, source_target_pairs={{2,0},{4,2},{6,4},{8,6},{10,8},{12,10},{14,12},{0,14},{3,1},{5,3},... | collective-permute-start | bytes 786440 | tf_op jit(solution)/shard_map/while/body/eval_jaxpr/ppermute | solution.py:13
  15.4 20.9 %collective-permute-start.3 = (s32[1,1,1,4,2,8]{5,4,3,2,1,0:T(2,128)S(1)}, s32[1,1,1,4,2,8]{5,4,3,2,1,0:T(2,128)S(1)}, u32[]{:S(2)}, u32[]{:S(2)}) collective-permute-start(s32[1,1,1,4,2,8]{5,4,3,2,1,0:T(2,128)S(1)} %copy.61), channel_id=1, source_target_pairs={{1,0},{0,1},{3,2},{2,3},{5,4},{4,5},{7,6},{6,7},{9,8},{8,9},{11,10... | collective-permute-start | bytes 776 | tf_op jit(solution)/shard_map/while/body/eval_jaxpr/ppermute | solution.py:13
  15.9 20.3 %collective-permute-start.1 = (s32[1,1,1,2,8]{4,3,2,1,0:T(2,128)S(1)}, s32[1,1,1,2,8]{4,3,2,1,0:T(2,128)S(1)}, u32[]{:S(2)}, u32[]{:S(2)}) collective-permute-start(s32[1,1,1,2,8]{4,3,2,1,0:T(2,128)S(1)} %copy.59), channel_id=1, source_target_pairs={{2,0},{4,2},{6,4},{8,6},{10,8},{12,10},{14,12},{0,14},{3,1},{5,3},... | collective-permute-start | bytes 200 | tf_op jit(solution)/shard_map/while/body/eval_jaxpr/ppermute | solution.py:13
  37.5 27.2 %collective-permute-start.2 = (f32[1,1,1,4,2,64,512]{6,5,4,3,2,1,0:T(8,128)S(1)}, f32[1,1,1,4,2,64,512]{6,5,4,3,2,1,0:T(8,128)}, u32[]{:S(2)}, u32[]{:S(2)}) collective-permute-start(f32[1,1,1,4,2,64,512]{6,5,4,3,2,1,0:T(8,128)S(1)} %copy.60), channel_id=1, source_target_pairs={{1,0},{0,1},{3,2},{2,3},{5,4},{4,5},{7,6},{6,7},{9,8},{8,9},{11,10... | collective-permute-start | bytes 3145736 | tf_op jit(solution)/shard_map/while/body/eval_jaxpr/ppermute | solution.py:13
  39.9 24.8 %collective-permute-start = (f32[1,1,1,2,64,512]{5,4,3,2,1,0:T(8,128)S(1)}, f32[1,1,1,2,64,512]{5,4,3,2,1,0:T(8,128)}, u32[]{:S(2)}, u32[]{:S(2)}) collective-permute-start(f32[1,1,1,2,64,512]{5,4,3,2,1,0:T(8,128)S(1)} %copy.58), channel_id=1, source_target_pairs={{2,0},{4,2},{6,4},{8,6},{10,8},{12,10},{14,12},{0,14},{3,1},{5,3},... | collective-permute-start | bytes 786440 | tf_op jit(solution)/shard_map/while/body/eval_jaxpr/ppermute | solution.py:13
  40.8 23.9 %collective-permute-start.3 = (s32[1,1,1,4,2,8]{5,4,3,2,1,0:T(2,128)S(1)}, s32[1,1,1,4,2,8]{5,4,3,2,1,0:T(2,128)S(1)}, u32[]{:S(2)}, u32[]{:S(2)}) collective-permute-start(s32[1,1,1,4,2,8]{5,4,3,2,1,0:T(2,128)S(1)} %copy.61), channel_id=1, source_target_pairs={{1,0},{0,1},{3,2},{2,3},{5,4},{4,5},{7,6},{6,7},{9,8},{8,9},{11,10... | collective-permute-start | bytes 776 | tf_op jit(solution)/shard_map/while/body/eval_jaxpr/ppermute | solution.py:13
  41.4 23.3 %collective-permute-start.1 = (s32[1,1,1,2,8]{4,3,2,1,0:T(2,128)S(1)}, s32[1,1,1,2,8]{4,3,2,1,0:T(2,128)S(1)}, u32[]{:S(2)}, u32[]{:S(2)}) collective-permute-start(s32[1,1,1,2,8]{4,3,2,1,0:T(2,128)S(1)} %copy.59), channel_id=1, source_target_pairs={{2,0},{4,2},{6,4},{8,6},{10,8},{12,10},{14,12},{0,14},{3,1},{5,3},... | collective-permute-start | bytes 200 | tf_op jit(solution)/shard_map/while/body/eval_jaxpr/ppermute | solution.py:13
  66.0 25.1 %collective-permute-start.2 = (f32[1,1,1,4,2,64,512]{6,5,4,3,2,1,0:T(8,128)S(1)}, f32[1,1,1,4,2,64,512]{6,5,4,3,2,1,0:T(8,128)}, u32[]{:S(2)}, u32[]{:S(2)}) collective-permute-start(f32[1,1,1,4,2,64,512]{6,5,4,3,2,1,0:T(8,128)S(1)} %copy.60), channel_id=1, source_target_pairs={{1,0},{0,1},{3,2},{2,3},{5,4},{4,5},{7,6},{6,7},{9,8},{8,9},{11,10... | collective-permute-start | bytes 3145736 | tf_op jit(solution)/shard_map/while/body/eval_jaxpr/ppermute | solution.py:13
  68.4 22.7 %collective-permute-start = (f32[1,1,1,2,64,512]{5,4,3,2,1,0:T(8,128)S(1)}, f32[1,1,1,2,64,512]{5,4,3,2,1,0:T(8,128)}, u32[]{:S(2)}, u32[]{:S(2)}) collective-permute-start(f32[1,1,1,2,64,512]{5,4,3,2,1,0:T(8,128)S(1)} %copy.58), channel_id=1, source_target_pairs={{2,0},{4,2},{6,4},{8,6},{10,8},{12,10},{14,12},{0,14},{3,1},{5,3},... | collective-permute-start | bytes 786440 | tf_op jit(solution)/shard_map/while/body/eval_jaxpr/ppermute | solution.py:13
  68.4 22.7 %collective-permute-start.3 = (s32[1,1,1,4,2,8]{5,4,3,2,1,0:T(2,128)S(1)}, s32[1,1,1,4,2,8]{5,4,3,2,1,0:T(2,128)S(1)}, u32[]{:S(2)}, u32[]{:S(2)}) collective-permute-start(s32[1,1,1,4,2,8]{5,4,3,2,1,0:T(2,128)S(1)} %copy.61), channel_id=1, source_target_pairs={{1,0},{0,1},{3,2},{2,3},{5,4},{4,5},{7,6},{6,7},{9,8},{8,9},{11,10... | collective-permute-start | bytes 776 | tf_op jit(solution)/shard_map/while/body/eval_jaxpr/ppermute | solution.py:13
  69.0 22.1 %collective-permute-start.1 = (s32[1,1,1,2,8]{4,3,2,1,0:T(2,128)S(1)}, s32[1,1,1,2,8]{4,3,2,1,0:T(2,128)S(1)}, u32[]{:S(2)}, u32[]{:S(2)}) collective-permute-start(s32[1,1,1,2,8]{4,3,2,1,0:T(2,128)S(1)} %copy.59), channel_id=1, source_target_pairs={{2,0},{4,2},{6,4},{8,6},{10,8},{12,10},{14,12},{0,14},{3,1},{5,3},... | collective-permute-start | bytes 200 | tf_op jit(solution)/shard_map/while/body/eval_jaxpr/ppermute | solution.py:13
  92.3 25.4 %collective-permute-start.2 = (f32[1,1,1,4,2,64,512]{6,5,4,3,2,1,0:T(8,128)S(1)}, f32[1,1,1,4,2,64,512]{6,5,4,3,2,1,0:T(8,128)}, u32[]{:S(2)}, u32[]{:S(2)}) collective-permute-start(f32[1,1,1,4,2,64,512]{6,5,4,3,2,1,0:T(8,128)S(1)} %copy.60), channel_id=1, source_target_pairs={{1,0},{0,1},{3,2},{2,3},{5,4},{4,5},{7,6},{6,7},{9,8},{8,9},{11,10... | collective-permute-start | bytes 3145736 | tf_op jit(solution)/shard_map/while/body/eval_jaxpr/ppermute | solution.py:13
  94.8 23.0 %collective-permute-start = (f32[1,1,1,2,64,512]{5,4,3,2,1,0:T(8,128)S(1)}, f32[1,1,1,2,64,512]{5,4,3,2,1,0:T(8,128)}, u32[]{:S(2)}, u32[]{:S(2)}) collective-permute-start(f32[1,1,1,2,64,512]{5,4,3,2,1,0:T(8,128)S(1)} %copy.58), channel_id=1, source_target_pairs={{2,0},{4,2},{6,4},{8,6},{10,8},{12,10},{14,12},{0,14},{3,1},{5,3},... | collective-permute-start | bytes 786440 | tf_op jit(solution)/shard_map/while/body/eval_jaxpr/ppermute | solution.py:13
  94.8 23.0 %collective-permute-start.3 = (s32[1,1,1,4,2,8]{5,4,3,2,1,0:T(2,128)S(1)}, s32[1,1,1,4,2,8]{5,4,3,2,1,0:T(2,128)S(1)}, u32[]{:S(2)}, u32[]{:S(2)}) collective-permute-start(s32[1,1,1,4,2,8]{5,4,3,2,1,0:T(2,128)S(1)} %copy.61), channel_id=1, source_target_pairs={{1,0},{0,1},{3,2},{2,3},{5,4},{4,5},{7,6},{6,7},{9,8},{8,9},{11,10... | collective-permute-start | bytes 776 | tf_op jit(solution)/shard_map/while/body/eval_jaxpr/ppermute | solution.py:13
  95.3 22.4 %collective-permute-start.1 = (s32[1,1,1,2,8]{4,3,2,1,0:T(2,128)S(1)}, s32[1,1,1,2,8]{4,3,2,1,0:T(2,128)S(1)}, u32[]{:S(2)}, u32[]{:S(2)}) collective-permute-start(s32[1,1,1,2,8]{4,3,2,1,0:T(2,128)S(1)} %copy.59), channel_id=1, source_target_pairs={{2,0},{4,2},{6,4},{8,6},{10,8},{12,10},{14,12},{0,14},{3,1},{5,3},... | collective-permute-start | bytes 200 | tf_op jit(solution)/shard_map/while/body/eval_jaxpr/ppermute | solution.py:13
  119.0 25.9 %collective-permute-start.2 = (f32[1,1,1,4,2,64,512]{6,5,4,3,2,1,0:T(8,128)S(1)}, f32[1,1,1,4,2,64,512]{6,5,4,3,2,1,0:T(8,128)}, u32[]{:S(2)}, u32[]{:S(2)}) collective-permute-start(f32[1,1,1,4,2,64,512]{6,5,4,3,2,1,0:T(8,128)S(1)} %copy.60), channel_id=1, source_target_pairs={{1,0},{0,1},{3,2},{2,3},{5,4},{4,5},{7,6},{6,7},{9,8},{8,9},{11,10... | collective-permute-start | bytes 3145736 | tf_op jit(solution)/shard_map/while/body/eval_jaxpr/ppermute | solution.py:13
  121.5 23.4 %collective-permute-start = (f32[1,1,1,2,64,512]{5,4,3,2,1,0:T(8,128)S(1)}, f32[1,1,1,2,64,512]{5,4,3,2,1,0:T(8,128)}, u32[]{:S(2)}, u32[]{:S(2)}) collective-permute-start(f32[1,1,1,2,64,512]{5,4,3,2,1,0:T(8,128)S(1)} %copy.58), channel_id=1, source_target_pairs={{2,0},{4,2},{6,4},{8,6},{10,8},{12,10},{14,12},{0,14},{3,1},{5,3},... | collective-permute-start | bytes 786440 | tf_op jit(solution)/shard_map/while/body/eval_jaxpr/ppermute | solution.py:13
  121.8 23.1 %collective-permute-start.3 = (s32[1,1,1,4,2,8]{5,4,3,2,1,0:T(2,128)S(1)}, s32[1,1,1,4,2,8]{5,4,3,2,1,0:T(2,128)S(1)}, u32[]{:S(2)}, u32[]{:S(2)}) collective-permute-start(s32[1,1,1,4,2,8]{5,4,3,2,1,0:T(2,128)S(1)} %copy.61), channel_id=1, source_target_pairs={{1,0},{0,1},{3,2},{2,3},{5,4},{4,5},{7,6},{6,7},{9,8},{8,9},{11,10... | collective-permute-start | bytes 776 | tf_op jit(solution)/shard_map/while/body/eval_jaxpr/ppermute | solution.py:13
  122.4 22.5 %collective-permute-start.1 = (s32[1,1,1,2,8]{4,3,2,1,0:T(2,128)S(1)}, s32[1,1,1,2,8]{4,3,2,1,0:T(2,128)S(1)}, u32[]{:S(2)}, u32[]{:S(2)}) collective-permute-start(s32[1,1,1,2,8]{4,3,2,1,0:T(2,128)S(1)} %copy.59), channel_id=1, source_target_pairs={{2,0},{4,2},{6,4},{8,6},{10,8},{12,10},{14,12},{0,14},{3,1},{5,3},... | collective-permute-start | bytes 200 | tf_op jit(solution)/shard_map/while/body/eval_jaxpr/ppermute | solution.py:13
  146.1 27.2 %collective-permute-start.2 = (f32[1,1,1,4,2,64,512]{6,5,4,3,2,1,0:T(8,128)S(1)}, f32[1,1,1,4,2,64,512]{6,5,4,3,2,1,0:T(8,128)}, u32[]{:S(2)}, u32[]{:S(2)}) collective-permute-start(f32[1,1,1,4,2,64,512]{6,5,4,3,2,1,0:T(8,128)S(1)} %copy.60), channel_id=1, source_target_pairs={{1,0},{0,1},{3,2},{2,3},{5,4},{4,5},{7,6},{6,7},{9,8},{8,9},{11,10... | collective-permute-start | bytes 3145736 | tf_op jit(solution)/shard_map/while/body/eval_jaxpr/ppermute | solution.py:13
  148.6 24.8 %collective-permute-start = (f32[1,1,1,2,64,512]{5,4,3,2,1,0:T(8,128)S(1)}, f32[1,1,1,2,64,512]{5,4,3,2,1,0:T(8,128)}, u32[]{:S(2)}, u32[]{:S(2)}) collective-permute-start(f32[1,1,1,2,64,512]{5,4,3,2,1,0:T(8,128)S(1)} %copy.58), channel_id=1, source_target_pairs={{2,0},{4,2},{6,4},{8,6},{10,8},{12,10},{14,12},{0,14},{3,1},{5,3},... | collective-permute-start | bytes 786440 | tf_op jit(solution)/shard_map/while/body/eval_jaxpr/ppermute | solution.py:13
  149.4 23.9 %collective-permute-start.3 = (s32[1,1,1,4,2,8]{5,4,3,2,1,0:T(2,128)S(1)}, s32[1,1,1,4,2,8]{5,4,3,2,1,0:T(2,128)S(1)}, u32[]{:S(2)}, u32[]{:S(2)}) collective-permute-start(s32[1,1,1,4,2,8]{5,4,3,2,1,0:T(2,128)S(1)} %copy.61), channel_id=1, source_target_pairs={{1,0},{0,1},{3,2},{2,3},{5,4},{4,5},{7,6},{6,7},{9,8},{8,9},{11,10... | collective-permute-start | bytes 776 | tf_op jit(solution)/shard_map/while/body/eval_jaxpr/ppermute | solution.py:13
  150.0 23.3 %collective-permute-start.1 = (s32[1,1,1,2,8]{4,3,2,1,0:T(2,128)S(1)}, s32[1,1,1,2,8]{4,3,2,1,0:T(2,128)S(1)}, u32[]{:S(2)}, u32[]{:S(2)}) collective-permute-start(s32[1,1,1,2,8]{4,3,2,1,0:T(2,128)S(1)} %copy.59), channel_id=1, source_target_pairs={{2,0},{4,2},{6,4},{8,6},{10,8},{12,10},{14,12},{0,14},{3,1},{5,3},... | collective-permute-start | bytes 200 | tf_op jit(solution)/shard_map/while/body/eval_jaxpr/ppermute | solution.py:13
  174.6 25.1 %collective-permute-start.2 = (f32[1,1,1,4,2,64,512]{6,5,4,3,2,1,0:T(8,128)S(1)}, f32[1,1,1,4,2,64,512]{6,5,4,3,2,1,0:T(8,128)}, u32[]{:S(2)}, u32[]{:S(2)}) collective-permute-start(f32[1,1,1,4,2,64,512]{6,5,4,3,2,1,0:T(8,128)S(1)} %copy.60), channel_id=1, source_target_pairs={{1,0},{0,1},{3,2},{2,3},{5,4},{4,5},{7,6},{6,7},{9,8},{8,9},{11,10... | collective-permute-start | bytes 3145736 | tf_op jit(solution)/shard_map/while/body/eval_jaxpr/ppermute | solution.py:13
  177.0 22.7 %collective-permute-start = (f32[1,1,1,2,64,512]{5,4,3,2,1,0:T(8,128)S(1)}, f32[1,1,1,2,64,512]{5,4,3,2,1,0:T(8,128)}, u32[]{:S(2)}, u32[]{:S(2)}) collective-permute-start(f32[1,1,1,2,64,512]{5,4,3,2,1,0:T(8,128)S(1)} %copy.58), channel_id=1, source_target_pairs={{2,0},{4,2},{6,4},{8,6},{10,8},{12,10},{14,12},{0,14},{3,1},{5,3},... | collective-permute-start | bytes 786440 | tf_op jit(solution)/shard_map/while/body/eval_jaxpr/ppermute | solution.py:13
  177.0 22.7 %collective-permute-start.3 = (s32[1,1,1,4,2,8]{5,4,3,2,1,0:T(2,128)S(1)}, s32[1,1,1,4,2,8]{5,4,3,2,1,0:T(2,128)S(1)}, u32[]{:S(2)}, u32[]{:S(2)}) collective-permute-start(s32[1,1,1,4,2,8]{5,4,3,2,1,0:T(2,128)S(1)} %copy.61), channel_id=1, source_target_pairs={{1,0},{0,1},{3,2},{2,3},{5,4},{4,5},{7,6},{6,7},{9,8},{8,9},{11,10... | collective-permute-start | bytes 776 | tf_op jit(solution)/shard_map/while/body/eval_jaxpr/ppermute | solution.py:13
  177.6 22.1 %collective-permute-start.1 = (s32[1,1,1,2,8]{4,3,2,1,0:T(2,128)S(1)}, s32[1,1,1,2,8]{4,3,2,1,0:T(2,128)S(1)}, u32[]{:S(2)}, u32[]{:S(2)}) collective-permute-start(s32[1,1,1,2,8]{4,3,2,1,0:T(2,128)S(1)} %copy.59), channel_id=1, source_target_pairs={{2,0},{4,2},{6,4},{8,6},{10,8},{12,10},{14,12},{0,14},{3,1},{5,3},... | collective-permute-start | bytes 200 | tf_op jit(solution)/shard_map/while/body/eval_jaxpr/ppermute | solution.py:13
  213.7 3.5 copy-start
where the time goes:
time: 391 us; the launch traced here: 388 us
  local copies, waits for them, and re-layouts  174 us (45%)
  blocking collectives  96.4 us (25%)
  matrix products  87.3 us (22%)
  starting transfers between devices  26 us (7%)
    all_to_all x1, blocking collectives, body(): lax.all_to_all(outgoing, ('layer', 'row'), split_axis=0, concat_axis=0, t...  96.4 us
    scatter x1, local copies, waits for them, and re-layouts, body(): jnp.zeros((n_owner, CAP, span), jnp.float32).at[owner_list, rank].set(total)  63.3 us
    dot_general x8, matrix products, panel_products(): jnp.einsum('sn,sd->nd', selector, prod, precision=lax.Precision.HIGHEST,...  47.6 us
    transpose x8, local copies, waits for them, and re-layouts, panel_products(): jnp.einsum('kxap,kxbq->kabpq', a_four, b_four, precision=lax.Precision.HI...  43 us
    dot_general x8, matrix products, panel_products(): jnp.einsum('kxap,kxbq->kabpq', a_four, b_four, precision=lax.Precision.HI...  39.7 us
    reshape x8, local copies, waits for them, and re-layouts, panel_products(): prod = prod.reshape(count * many_a * many_b, block * block)  28.1 us
    ppermute x28, starting transfers between devices, from_behind(): return lax.ppermute(block, axis, route)  26 us
    while x28, local copies, waits for them, and re-layouts  15.3 us
  transfers between devices with their start and end apart: 28, of which 0 were waited for; matrix products, arithmetic and copies ran while one was open for 40% of the time, Pallas kernels for 0%

commit v1 on v0

v1 whole, which is shorter than its diff:
```python
import functools
import jax
import jax.numpy as jnp
from jax import lax
from jax.experimental import pallas as pl
from jax.experimental.pallas import tpu as pltpu
from jax.sharding import PartitionSpec as P

TILE = 64
CAP = 16
LANES = 128
VMEM_BYTES = 56 * 2**20


def swap(block, axis, mask):
    return lax.ppermute(block, axis, [(i, i ^ mask) for i in range(lax.axis_size(axis))])


def gathered(block, axis, order):
    held = {0: block}
    for mask in order:
        held[mask] = jax.tree.map(
            lambda x, low=mask & -mask: swap(x, axis, low), held[mask & (mask - 1)]
        )
    return [held[mask] for mask in range(lax.axis_size(axis))]


def pack_kernel(a_ref, rows_ref, out_ref, flipped):
    panels, block, width = a_ref.shape
    half = width // 2
    for kk in range(panels):
        flipped[...] = a_ref[kk].T
        out_ref[pl.ds(kk * half, half), :block] = flipped[pl.ds(0, half, 2), :]
        out_ref[pl.ds(kk * half, half), block:] = flipped[pl.ds(1, half, 2), :]
    tail = panels * half
    out_ref[pl.ds(tail, 8), :] = jnp.zeros((8, LANES), jnp.float32)
    out_ref[pl.ds(tail, panels), : rows_ref.shape[1]] = rows_ref[...].astype(jnp.float32)


def product_kernel(n_layer, n_row, n_col, panels, sets, many, table_ref, *refs):
    a_refs, refs = refs[:n_row], refs[n_row:]
    b_refs, refs = refs[:n_col], refs[n_col:]
    c_refs, refs = refs[:n_col], refs[n_col:]
    n_unit = n_layer * n_row
    out_refs, refs = refs[:n_unit], refs[n_unit:]
    acc, left, right, prod, index, number, sem = refs
    block = b_refs[0].shape[1]
    half = many * block // 2
    pair = block // 2
    low = lax.broadcasted_iota(jnp.int32, (1, LANES), 1) < block

    for m in range(n_row):
        tail = a_refs[m][pl.ds(panels * half, panels), :]
        index[pl.ds(m * panels, panels), :] = tail.astype(jnp.int32)
    for m in range(n_col):
        index[pl.ds(n_row * panels + m, 1), : c_refs[m].shape[1]] = c_refs[m][...]
    copy = pltpu.make_async_copy(index, number, sem)
    copy.start()

    @pl.loop(0, acc.shape[0] // (8 * pair))
    def _(i):
        acc[pl.ds(pl.multiple_of(i * 8 * pair, 8), 8 * pair), :] = jnp.zeros(
            (8 * pair, LANES), jnp.float32
        )

    for m in range(n_col):

        @pl.loop(0, sets * panels)
        def _(i, m=m):
            b = b_refs[m][i]
            high = b.astype(jnp.bfloat16)
            rest = (b - high.astype(jnp.float32)).astype(jnp.bfloat16)
            at = m * sets * panels + i
            right[at, pl.ds(0, block), :] = high
            right[at, pl.ds(block, block), :] = rest
            right[at, pl.ds(2 * block, block), :] = high
            right[at, pl.ds(3 * block, block), :] = jnp.zeros_like(high)

    for m in range(n_row):

        @pl.loop(0, panels)
        def _(kk, m=m):
            a = a_refs[m][pl.ds(pl.multiple_of(kk * half, half), half), :]
            turned = pltpu.roll(a, block, 1)
            rest = a - a.astype(jnp.bfloat16).astype(jnp.float32)
            turned_rest = pltpu.roll(rest, block, 1)
            at = m * panels + kk
            left[at, pl.ds(0, half), pl.ds(0, LANES)] = jnp.where(low, a, turned).astype(jnp.bfloat16)
            left[at, pl.ds(0, half), pl.ds(LANES, LANES)] = rest.astype(jnp.bfloat16)
            left[at, pl.ds(half, half), pl.ds(0, LANES)] = jnp.where(low, turned, a).astype(jnp.bfloat16)
            left[at, pl.ds(half, half), pl.ds(LANES, LANES)] = turned_rest.astype(jnp.bfloat16)

    copy.wait()
    my_row, my_col = lax.axis_index("row"), lax.axis_index("col")

    def place_b(m):
        label = lax.rem(lax.bitwise_xor(my_row, m) + my_col, n_row)
        offset = lax.rem(label - my_row + n_row, n_row)
        mask = lax.bitwise_xor(lax.rem(offset, n_col), my_col)
        return mask, lax.div(offset, n_col)

    def multiply(m, kk):
        mask, which = place_b(m)
        prod[kk] = jnp.dot(
            left[m * panels + kk],
            right[(mask * sets + which) * panels + kk],
            preferred_element_type=jnp.float32,
        )

    def add(m, kk):
        mask, which = place_b(m)
        base = (which * panels + kk) * many
        cols = [number[n_row * panels + mask, base + b] for b in range(many)]
        for a in range(many):
            row = number[m * panels + kk, a]
            first, second = lax.shift_right_logical(row, 1), lax.bitwise_and(row, 1) * TILE
            places = [pl.multiple_of(table_ref[first, second + col], pair) for col in cols]
            even = prod[kk, pl.ds(a * pair, pair), :]
            odd = prod[kk, pl.ds(half + a * pair, pair), :]
            blocks = []
            for q in range(many // 2):
                e, o = even[:, q * LANES : (q + 1) * LANES], odd[:, q * LANES : (q + 1) * LANES]
                turned = pltpu.roll(jnp.where(low, o, e), block, 1)
                blocks += [jnp.where(low, e, turned), jnp.where(low, turned, o)]
            sums = [acc[pl.ds(at, pair), :] + new for at, new in zip(places, blocks)]
            for at, new in zip(places, sums):
                acc[pl.ds(at, pair), :] = new

    multiply(0, 0)

    @pl.loop(0, n_row)
    def _(m):
        for kk in range(panels):
            if kk + 1 < panels:
                multiply(m, kk + 1)
            else:
                multiply(lax.rem(m + 1, n_row), 0)
            add(m, kk)

    @pl.loop(0, pair)
    def _(j):
        for unit in range(n_unit):
            for eight in range(CAP // 8):
                first = (unit * CAP + eight * 8) * pair
                out_refs[unit][eight, j] = acc[pl.ds(first + j, 8, pair), :]


def place_kernel(n_row, own_ref, other_ref, *refs):
    units, out_ref, total, sems = refs[: n_row - 1], refs[n_row - 1], refs[n_row], refs[n_row + 1]
    my_row = lax.axis_index("row")
    size = own_ref.shape[0]

    def copy(m, source):
        at = pl.multiple_of(lax.bitwise_xor(my_row, m) * size, size)
        return pltpu.make_async_copy(source, out_ref.at[pl.ds(at, size)], sems.at[m])

    copies = [copy(m, units[m - 1]) for m in range(1, n_row)]
    for c in copies:
        c.start()
    total[...] = own_ref[...] + other_ref[...]
    mine = copy(0, total)
    mine.start()
    for c in (*copies, mine):
        c.wait()


def far_first(n):
    return [m for m in range(n // 2, n)] + [m for m in range(2, n // 2)] + [1, 0]


def body(a_val, a_rows, b_val, b_cols, pattern, owners):
    n_row, n_col, n_layer = (lax.axis_size(x) for x in ("row", "col", "layer"))
    panels, block, width = a_val.shape[3:]
    sets = b_val.shape[3]
    many = width // block
    pair = block // 2
    kept = pattern.shape[2]
    a_val, a_rows = a_val[0, 0, 0], a_rows[0, 0, 0]
    b_val = b_val[0, 0, 0].reshape(sets * panels, block, width)
    b_cols = b_cols[0, 0, 0].reshape(1, sets * panels * many)
    vmem, anywhere = pl.BlockSpec(memory_space=pltpu.VMEM), pl.BlockSpec(memory_space=pl.ANY)
    params = pltpu.CompilerParams(vmem_limit_bytes=VMEM_BYTES)
    rows = panels * width // 2 + 8

    packed = pl.pallas_call(
        pack_kernel,
        out_shape=jax.ShapeDtypeStruct((rows, LANES), jnp.float32),
        in_specs=[vmem, vmem],
        out_specs=vmem,
        scratch_shapes=[pltpu.VMEM((width, block), jnp.float32)],
        compiler_params=params,
    )(a_val, a_rows)
    b_held = gathered((b_val, b_cols), "col", range(1, n_col))
    high_first = [m for m in range(1, n_row)]
    high_first.sort(key=lambda m: (m & 1, bin(m).count("1"), -m))
    a_held = gathered(packed, "row", high_first)

    owner = owners[0, :, 0]
    my_row, my_layer = lax.axis_index("row"), lax.axis_index("layer")
    before = (owner[:, None] == owner[None, :]) & (
        jnp.arange(kept)[None, :] < jnp.arange(kept)[:, None]
    )
    rank = jnp.sum(before.astype(jnp.int32), axis=1)
    unit = ((owner // n_row) ^ my_layer) * n_row + ((owner % n_row) ^ my_row)
    slots = n_layer * n_row * CAP
    slot = unit * CAP + rank
    codes = jnp.arange(TILE * TILE, dtype=jnp.int32)
    hit = codes[:, None] == pattern[0, 0][None, :]
    table = slots + jnp.sum(jnp.where(hit, slot[None, :] - slots, 0), axis=1)
    table = (table * pair).reshape(TILE * TILE // LANES, LANES)

    unit_shape = (CAP // 8, pair, 8, LANES)
    n_unit = n_layer * n_row
    index_rows = -(-(n_row * panels + n_col) // 8) * 8
    parts = pl.pallas_call(
        functools.partial(product_kernel, n_layer, n_row, n_col, panels, sets, many),
        out_shape=[jax.ShapeDtypeStruct(unit_shape, jnp.float32)] * n_unit,
        in_specs=[pl.BlockSpec(memory_space=pltpu.SMEM)] + [vmem] * (n_row + 2 * n_col),
        out_specs=[vmem] * n_unit,
        scratch_shapes=[
            pltpu.VMEM(((slots + 8) * pair, LANES), jnp.float32),
            pltpu.VMEM((n_row * panels, width, 4 * block), jnp.bfloat16),
            pltpu.VMEM((n_col * sets * panels, 4 * block, width), jnp.bfloat16),
            pltpu.VMEM((panels, width, width), jnp.float32),
            pltpu.VMEM((index_rows, LANES), jnp.int32),
            pltpu.SMEM((index_rows, LANES), jnp.int32),
            pltpu.SemaphoreType.DMA,
        ],
        compiler_params=params,
    )(table, *a_held, *[b[0] for b in b_held], *[b[1] for b in b_held])

    arrived, others = {}, []
    order = far_first(n_row)
    for at, m in enumerate(order):
        gone = parts[n_row + m]
        if at > 1:
            gone, others[at - 2] = lax.optimization_barrier((gone, others[at - 2]))
        if at > 3 and order[at - 4] in arrived and at < n_row - 1:
            gone, arrived[order[at - 4]] = lax.optimization_barrier((gone, arrived[order[at - 4]]))
        other = swap(gone, "layer", 1)
        others.append(other)
        if m:
            arrived[m] = swap(parts[m] + other, "row", m)
    owned = pl.pallas_call(
        functools.partial(place_kernel, n_row),
        out_shape=jax.ShapeDtypeStruct((n_row * unit_shape[0], *unit_shape[1:]), jnp.float32),
        in_specs=[vmem] * (n_row + 1),
        out_specs=anywhere,
        scratch_shapes=[
            pltpu.VMEM(unit_shape, jnp.float32),
            pltpu.SemaphoreType.DMA((n_row,)),
        ],
        compiler_params=params,
    )(parts[0], other, *[arrived[m] for m in range(1, n_row)])
    return owned.transpose(0, 2, 1, 3).reshape(n_row * CAP, block * block)


def solution(mesh):
    return jax.shard_map(
        body,
        mesh=mesh,
        in_specs=(
            P("col", "layer", "row", None, None, None),
            P("col", "layer", "row", None, None),
            P("row", "layer", "col", None, None, None, None),
            P("row", "layer", "col", None, None, None),
            P("col", "row", None),
            P("col", "row", None),
        ),
        out_specs=P(("layer", "row"), "col"),
        check_vma=False,
    )
```

time: 391 us -> 124 us (0.32)
  local copies, waits for them, and re-layouts: 174 us -> 3.41 us
  blocking collectives: 96.4 us -> 0 us
  matrix products: 87.3 us -> 0 us
  waiting for transfers between devices: 0.1 us -> 51.5 us
  Pallas kernels: 0 us -> 21.8 us
  starting transfers between devices: 26 us -> 39.6 us
    all_to_all x1 -> x0, blocking collectives: 96.4 us -> none  [body(): lax.all_to_all(outgoing, ('layer', 'row'), split_axis=0, concat_axis=0, t...]
    dot_general x16 -> x0, matrix products: 87.3 us -> none  [the longest x8 47.6 us: panel_products(): jnp.einsum('sn,sd->nd', selector, prod, precision=lax.Precision.HIGHEST,...]
    scatter x2 -> x0, local copies, waits for them, and re-layouts: 64.7 us -> none  [the longest x1 63.3 us: body(): jnp.zeros((n_owner, CAP, span), jnp.float32).at[owner_list, rank].set(total)]
    ppermute x28 -> x24, waiting for transfers between devices: 0.1 us -> 51.5 us  [swap(): lax.ppermute(block, axis, [(i, i ^ mask) for i in range(lax.axis_size(axi...]
    transpose x8 -> x0, local copies, waits for them, and re-layouts: 43 us -> none  [panel_products(): jnp.einsum('kxap,kxbq->kabpq', a_four, b_four, precision=lax.Precision.HI...]
    reshape x8 -> x0, local copies, waits for them, and re-layouts: 28.1 us -> none  [panel_products(): prod = prod.reshape(count * many_a * many_b, block * block)]
    pallas_call x0 -> x3, Pallas kernels: none -> 21.8 us  [the longest x1 16.9 us: body(): pl.pallas_call(functools.partial(product_kernel, n_layer, n_row, n_col, p...]
    while x28 -> x0, local copies, waits for them, and re-layouts: 15.3 us -> none
  transfers between devices with their start and end apart: 28 -> 24, of which waited for: 0 -> 10; matrix products, arithmetic and copies ran while one was open for 40% -> 6% of each run, Pallas kernels for 0% -> 2%
where the time goes in v1:
time: 124 us; the launch traced here: 123 us
  waiting for transfers between devices  51.5 us (42%)
  starting transfers between devices  39.6 us (32%)
  Pallas kernels  21.8 us (18%)
  other arithmetic  6.64 us (5%)
  local copies, waits for them, and re-layouts  3.41 us (3%)
    ppermute x24, waiting for transfers between devices, swap(): lax.ppermute(block, axis, [(i, i ^ mask) for i in range(lax.axis_size(axi...  51.5 us
    ppermute x24, starting transfers between devices, swap(): lax.ppermute(block, axis, [(i, i ^ mask) for i in range(lax.axis_size(axi...  39.6 us
    pallas_call x1, Pallas kernels, body(): pl.pallas_call(functools.partial(product_kernel, n_layer, n_row, n_col, p...  16.9 us
    add x7, other arithmetic, body(): arrived[m] = swap(parts[m] + other, 'row', m)  3.09 us
    pallas_call x1, Pallas kernels, body(): pl.pallas_call(functools.partial(place_kernel, n_row), out_shape=jax.Shap...  2.97 us
    unnamed x50, local copies, waits for them, and re-layouts  2.64 us
  transfers between devices with their start and end apart: 24, of which 10 were waited for; matrix products, arithmetic and copies ran while one was open for 6% of the time, Pallas kernels for 2%

profile of v1, /device:TPU:0, one launch (start us, length us, event | category | flops | bytes accessed | tf_op | source)
XLA Modules:
  0.0 123.4 jit_solution(11645902308909961314)
XLA Ops:
  0.0 2.9 %collective-permute-start.7 = (f32[8,64,512]{2,1,0:T(8,128)}, f32[8,64,512]{2,1,0:T(8,128)S(1)}, u32[]{:S(2)}, u32[]{:S(2)}) collective-permute-start(f32[8,64,512]{2,1,0:T(8,128)} %bitcast.10), channel_id=1, source_target_pairs={{0,1},{1,0},{2,3},{3,2},{4,5},{5,4},{6,7},{7,6},{8,9},{9,8},{10,11... | collective-permute-start | bytes 3145736 | tf_op jit(solution)/shard_map/ppermute | solution.py:16
  2.9 2.0 %shard_map.64.refs_0_ = f32[520,128]{1,0:T(8,128)} custom-call(f32[2,64,512]{2,1,0:T(8,128)} %bitcast.12, s32[2,8]{1,0:T(2,128)} %bitcast.15), custom_call_target="tpu_custom_call" | custom-call | tf_op jit(solution)/shard_map/pallas_call | solution.py:185
  4.9 2.6 %collective-permute-start.3 = (f32[520,128]{1,0:T(8,128)}, f32[520,128]{1,0:T(8,128)S(1)}, u32[]{:S(2)}, u32[]{:S(2)}) collective-permute-start(f32[520,128]{1,0:T(8,128)} %shard_map.64.refs_0_), channel_id=1, source_target_pairs={{0,8},{2,10},{4,12},{6,14},{8,0},{10,2},{12,4},{14,6},{1,9},{3,11}... | collective-permute-start | bytes 798728 | tf_op jit(solution)/shard_map/ppermute | solution.py:16
  7.5 1.6 %collective-permute-start.1 = (f32[520,128]{1,0:T(8,128)}, f32[520,128]{1,0:T(8,128)S(1)}, u32[]{:S(2)}, u32[]{:S(2)}) collective-permute-start(f32[520,128]{1,0:T(8,128)} %shard_map.64.refs_0_), channel_id=1, source_target_pairs={{0,4},{2,6},{4,0},{6,2},{8,12},{10,14},{12,8},{14,10},{1,5},{3,7},... | collective-permute-start | bytes 798728 | tf_op jit(solution)/shard_map/ppermute | solution.py:16
  9.1 0.8 reshape_squeeze.7.refs_10_
  10.5 9.2 %collective-permute-done.3.refs_4_ = f32[520,128]{1,0:T(8,128)S(1)} collective-permute-done((f32[520,128]{1,0:T(8,128)}, f32[520,128]{1,0:T(8,128)S(1)}, u32[]{:S(2)}, u32[]{:S(2)}) %collective-permute-start.3) | collective-permute-done | bytes 266272 | tf_op jit(solution)/shard_map/ppermute | solution.py:16
  20.4 0.9 convert_reduce_fusion
  22.0 4.4 %collective-permute-done.8.refs_11_ = s32[1,64]{1,0:T(1,128)S(1)} collective-permute-done((s32[1,64]{1,0:T(1,128)S(1)}, s32[1,64]{1,0:T(1,128)S(1)}, u32[]{:S(2)}, u32[]{:S(2)}) %collective-permute-start.8) | collective-permute-done | bytes 288 | tf_op jit(solution)/shard_map/ppermute | solution.py:16
  27.0 1.3 %select_reduce_fusion = s32[4096]{0:T(1024)S(1)} fusion(s32[256]{0:T(256)S(1)} %add_add_fusion, s32[256]{0:T(256)} %bitcast.16), kind=kLoop, calls=%fused_computation | loop fusion | flops 3141632 | bytes 18432 | tf_op jit(solution)/shard_map/reduce_sum | solution.py:209
  29.9 1.0 copy-done
  30.9 16.9 %shard_map.65 = (f32[2,32,8,128]{3,2,1,0:T(8,128)}, f32[2,32,8,128]{3,2,1,0:T(8,128)}, f32[2,32,8,128]{3,2,1,0:T(8,128)}, f32[2,32,8,128]{3,2,1,0:T(8,128)}, f32...) custom-call(s32[32,128]{1,0:T(8,128)} %multiply_bitcast_fusion.table, ...), custom_call_target="tpu_custom_call" | custom-call | tf_op jit(solution)/shard_map/pallas_call | solution.py:215
  47.8 1.9 %collective-permute-start.14 = (f32[2,32,8,128]{3,2,1,0:T(8,128)}, f32[2,32,8,128]{3,2,1,0:T(8,128)S(1)}, u32[]{:S(2)}, u32[]{:S(2)}) collective-permute-start(f32[2,32,8,128]{3,2,1,0:T(8,128)} %get-tuple-element.47), channel_id=1, source_target_pairs={{0,16},{16,0},{1,17},{17,1},{2,18},{18,2},{3,19},{19,3},{4,20},{20... | collective-permute-start | bytes 786440 | tf_op jit(solution)/shard_map/ppermute | solution.py:16
  49.9 7.3 %collective-permute-done.14 = f32[2,32,8,128]{3,2,1,0:T(8,128)S(1)} collective-permute-done((f32[2,32,8,128]{3,2,1,0:T(8,128)}, f32[2,32,8,128]{3,2,1,0:T(8,128)S(1)}, u32[]{:S(2)}, u32[]{:S(2)}) %collective-permute-start.14) | collective-permute-done | bytes 262176 | tf_op jit(solution)/shard_map/ppermute | solution.py:16
  57.2 1.8 %collective-permute-start.15 = (f32[2,32,8,128]{3,2,1,0:T(8,128)}, f32[2,32,8,128]{3,2,1,0:T(8,128)S(1)}, u32[]{:S(2)}, u32[]{:S(2)}) collective-permute-start(f32[2,32,8,128]{3,2,1,0:T(8,128)} %get-tuple-element.48), channel_id=1, source_target_pairs={{0,16},{16,0},{1,17},{17,1},{2,18},{18,2},{3,19},{19,3},{4,20},{20... | collective-permute-start | bytes 786440 | tf_op jit(solution)/shard_map/ppermute | solution.py:16
  59.0 1.0 add.70
  60.0 3.0 %collective-permute-start.16 = (f32[2,32,8,128]{3,2,1,0:T(8,128)S(1)}, f32[2,32,8,128]{3,2,1,0:T(8,128)S(1)}, u32[]{:S(2)}, u32[]{:S(2)}) collective-permute-start(f32[2,32,8,128]{3,2,1,0:T(8,128)S(1)} %add.70), channel_id=1, source_target_pairs={{0,8},{2,10},{4,12},{6,14},{8,0},{10,2},{12,4},{14,6},{1,9},{3,11}... | collective-permute-start | bytes 786440 | tf_op jit(solution)/shard_map/ppermute | solution.py:16
  63.0 1.6 %collective-permute-start.10 = (f32[2,32,8,128]{3,2,1,0:T(8,128)}, f32[2,32,8,128]{3,2,1,0:T(8,128)S(1)}, u32[]{:S(2)}, u32[]{:S(2)}) collective-permute-start(f32[2,32,8,128]{3,2,1,0:T(8,128)} %get-tuple-element.38), channel_id=1, source_target_pairs={{0,16},{16,0},{1,17},{17,1},{2,18},{18,2},{3,19},{19,3},{4,20},{20... | collective-permute-start | bytes 786440 | tf_op jit(solution)/shard_map/ppermute | solution.py:16
  64.7 1.0 add.69
  65.7 1.6 %collective-permute-start.11 = (f32[2,32,8,128]{3,2,1,0:T(8,128)S(1)}, f32[2,32,8,128]{3,2,1,0:T(8,128)S(1)}, u32[]{:S(2)}, u32[]{:S(2)}) collective-permute-start(f32[2,32,8,128]{3,2,1,0:T(8,128)S(1)} %add.69), channel_id=1, source_target_pairs={{0,10},{2,8},{4,14},{6,12},{8,2},{10,0},{12,6},{14,4},{1,11},{3,9}... | collective-permute-start | bytes 786440 | tf_op jit(solution)/shard_map/ppermute | solution.py:16
  67.3 1.2 collective-permute-done.15
  68.5 12.6 %collective-permute-done.16.refs_3_ = f32[2,32,8,128]{3,2,1,0:T(8,128)S(1)} collective-permute-done((f32[2,32,8,128]{3,2,1,0:T(8,128)S(1)}, f32[2,32,8,128]{3,2,1,0:T(8,128)S(1)}, u32[]{:S(2)}, u32[]{:S(2)}) %collective-permute-start.16) | collective-permute-done | bytes 262176 | tf_op jit(solution)/shard_map/ppermute | solution.py:16
  81.6 1.0 add.71
  82.6 2.4 %collective-permute-start.18 = (f32[2,32,8,128]{3,2,1,0:T(8,128)S(1)}, f32[2,32,8,128]{3,2,1,0:T(8,128)S(1)}, u32[]{:S(2)}, u32[]{:S(2)}) collective-permute-start(f32[2,32,8,128]{3,2,1,0:T(8,128)S(1)} %add.71), channel_id=1, source_target_pairs={{0,12},{2,14},{4,8},{6,10},{8,4},{10,6},{12,0},{14,2},{1,13},{3,15... | collective-permute-start | bytes 786440 | tf_op jit(solution)/shard_map/ppermute | solution.py:16
  85.0 1.6 %collective-permute-start.12 = (f32[2,32,8,128]{3,2,1,0:T(8,128)S(1)}, f32[2,32,8,128]{3,2,1,0:T(8,128)S(1)}, u32[]{:S(2)}, u32[]{:S(2)}) collective-permute-start(f32[2,32,8,128]{3,2,1,0:T(8,128)S(1)} %copy-done.24), channel_id=1, source_target_pairs={{0,16},{16,0},{1,17},{17,1},{2,18},{18,2},{3,19},{19,3},{4,20},{20... | collective-permute-start | bytes 786440 | tf_op jit(solution)/shard_map/ppermute | solution.py:16
  86.6 1.1 collective-permute-done.17
  87.7 3.5 %collective-permute-done.18.refs_5_ = f32[2,32,8,128]{3,2,1,0:T(8,128)S(1)} collective-permute-done((f32[2,32,8,128]{3,2,1,0:T(8,128)S(1)}, f32[2,32,8,128]{3,2,1,0:T(8,128)S(1)}, u32[]{:S(2)}, u32[]{:S(2)}) %collective-permute-start.18) | collective-permute-done | bytes 262176 | tf_op jit(solution)/shard_map/ppermute | solution.py:16
  91.2 1.5 %collective-permute-start.19 = (f32[2,32,8,128]{3,2,1,0:T(8,128)S(1)}, f32[2,32,8,128]{3,2,1,0:T(8,128)S(1)}, u32[]{:S(2)}, u32[]{:S(2)}) collective-permute-start(f32[2,32,8,128]{3,2,1,0:T(8,128)S(1)} %copy-done.23), channel_id=1, source_target_pairs={{0,16},{16,0},{1,17},{17,1},{2,18},{18,2},{3,19},{19,3},{4,20},{20... | collective-permute-start | bytes 786440 | tf_op jit(solution)/shard_map/ppermute | solution.py:16
  92.7 1.7 %collective-permute-start.23 = (f32[2,32,8,128]{3,2,1,0:T(8,128)S(1)}, f32[2,32,8,128]{3,2,1,0:T(8,128)S(1)}, u32[]{:S(2)}, u32[]{:S(2)}) collective-permute-start(f32[2,32,8,128]{3,2,1,0:T(8,128)S(1)} %add.75), channel_id=1, source_target_pairs={{0,14},{2,12},{4,10},{6,8},{8,6},{10,4},{12,2},{14,0},{1,15},{3,13... | collective-permute-start | bytes 786440 | tf_op jit(solution)/shard_map/ppermute | solution.py:16
  94.9 12.2 %collective-permute-start.22 = (f32[2,32,8,128]{3,2,1,0:T(8,128)S(1)}, f32[2,32,8,128]{3,2,1,0:T(8,128)S(1)}, u32[]{:S(2)}, u32[]{:S(2)}) collective-permute-start(f32[2,32,8,128]{3,2,1,0:T(8,128)S(1)} %add.74), channel_id=1, source_target_pairs={{0,6},{2,4},{4,2},{6,0},{8,14},{10,12},{12,10},{14,8},{1,7},{3,5},... | collective-permute-start | bytes 786440 | tf_op jit(solution)/shard_map/ppermute | solution.py:16
  107.5 6.3 %collective-permute-done.22.refs_2_ = f32[2,32,8,128]{3,2,1,0:T(8,128)S(1)} collective-permute-done((f32[2,32,8,128]{3,2,1,0:T(8,128)S(1)}, f32[2,32,8,128]{3,2,1,0:T(8,128)S(1)}, u32[]{:S(2)}, u32[]{:S(2)}) %collective-permute-start.22) | collective-permute-done | bytes 262176 | tf_op jit(solution)/shard_map/ppermute | solution.py:16
  113.8 5.8 %collective-permute-done.21.refs_1_ = f32[2,32,8,128]{3,2,1,0:T(8,128)S(1)} collective-permute-done((f32[2,32,8,128]{3,2,1,0:T(8,128)S(1)}, f32[2,32,8,128]{3,2,1,0:T(8,128)S(1)}, u32[]{:S(2)}, u32[]{:S(2)}) %collective-permute-start.21) | collective-permute-done | bytes 262176 | tf_op jit(solution)/shard_map/ppermute | solution.py:16
  120.4 3.0 %shard_map.66 = f32[16,32,8,128]{3,2,1,0:T(8,128)} custom-call(f32[2,32,8,128]{3,2,1,0:T(8,128)} %get-tuple-element.33.own_ref, f32[2,32,8,128]{3,2,1,0:T(8,128)} %copy-done.16, f32[2,32,8,128]{3,2,1,0:T(8,128)} %copy-done.19, f32[2,32,8,128]{3,2,1,0:T(8,128)} %copy-done.18, f32[2,32,8,128]{3,2,1,0:T(8,128)} %copy-done.17, f32[2,32,8,128]{3,2,1,0:T(8,128)} %copy-done.10, ...), custom_call_target="tpu_custom_call" | custom-call | tf_op jit(solution)/shard_map/pallas_call | solution.py:244
  (81 shorter events, 6.4 us)
Async XLA Ops:
  0.0 29.0 %collective-permute-start.7 = (f32[8,64,512]{2,1,0:T(8,128)}, f32[8,64,512]{2,1,0:T(8,128)S(1)}, u32[]{:S(2)}, u32[]{:S(2)}) collective-permute-start(f32[8,64,512]{2,1,0:T(8,128)} %bitcast.10), channel_id=1, source_target_pairs={{0,1},{1,0},{2,3},{3,2},{4,5},{5,4},{6,7},{7,6},{8,9},{9,8},{10,11... | collective-permute-start | bytes 3145736 | tf_op jit(solution)/shard_map/ppermute | solution.py:16
  4.9 14.8 %collective-permute-start.3 = (f32[520,128]{1,0:T(8,128)}, f32[520,128]{1,0:T(8,128)S(1)}, u32[]{:S(2)}, u32[]{:S(2)}) collective-permute-start(f32[520,128]{1,0:T(8,128)} %shard_map.64.refs_0_), channel_id=1, source_target_pairs={{0,8},{2,10},{4,12},{6,14},{8,0},{10,2},{12,4},{14,6},{1,9},{3,11}... | collective-permute-start | bytes 798728 | tf_op jit(solution)/shard_map/ppermute | solution.py:16
  7.5 18.9 %collective-permute-start.1 = (f32[520,128]{1,0:T(8,128)}, f32[520,128]{1,0:T(8,128)S(1)}, u32[]{:S(2)}, u32[]{:S(2)}) collective-permute-start(f32[520,128]{1,0:T(8,128)} %shard_map.64.refs_0_), channel_id=1, source_target_pairs={{0,4},{2,6},{4,0},{6,2},{8,12},{10,14},{12,8},{14,10},{1,5},{3,7},... | collective-permute-start | bytes 798728 | tf_op jit(solution)/shard_map/ppermute | solution.py:16
  9.1 19.8 %collective-permute-start = (f32[520,128]{1,0:T(8,128)}, f32[520,128]{1,0:T(8,128)S(1)}, u32[]{:S(2)}, u32[]{:S(2)}) collective-permute-start(f32[520,128]{1,0:T(8,128)} %shard_map.64.refs_0_), channel_id=1, source_target_pairs={{0,2},{2,0},{4,6},{6,4},{8,10},{10,8},{12,14},{14,12},{1,3},{3,1},... | collective-permute-start | bytes 798728 | tf_op jit(solution)/shard_map/ppermute | solution.py:16
  9.9 16.5 %collective-permute-start.8 = (s32[1,64]{1,0:T(1,128)S(1)}, s32[1,64]{1,0:T(1,128)S(1)}, u32[]{:S(2)}, u32[]{:S(2)}) collective-permute-start(s32[1,64]{1,0:T(1,128)S(1)} %reshape_squeeze.7.refs_10_), channel_id=1, source_target_pairs={{0,1},{1,0},{2,3},{3,2},{4,5},{5,4},{6,7},{7,6},{8,9},{9,8},{10,11... | collective-permute-start | bytes 776 | tf_op jit(solution)/shard_map/ppermute | solution.py:16
  19.7 7.2 %collective-permute-start.5 = (f32[520,128]{1,0:T(8,128)S(1)}, f32[520,128]{1,0:T(8,128)S(1)}, u32[]{:S(2)}, u32[]{:S(2)}) collective-permute-start(f32[520,128]{1,0:T(8,128)S(1)} %collective-permute-done.3.refs_4_), channel_id=1, source_target_pairs={{0,4},{2,6},{4,0},{6,2},{8,12},{10,14},{12,8},{14,10},{1,5},{3,7},... | collective-permute-start | bytes 798728 | tf_op jit(solution)/shard_map/ppermute | solution.py:16
  26.4 2.5 %collective-permute-start.4 = (f32[520,128]{1,0:T(8,128)S(1)}, f32[520,128]{1,0:T(8,128)S(1)}, u32[]{:S(2)}, u32[]{:S(2)}) collective-permute-start(f32[520,128]{1,0:T(8,128)S(1)} %collective-permute-done.3.refs_4_), channel_id=1, source_target_pairs={{0,2},{2,0},{4,6},{6,4},{8,10},{10,8},{12,14},{14,12},{1,3},{3,1},... | collective-permute-start | bytes 798728 | tf_op jit(solution)/shard_map/ppermute | solution.py:16
  26.4 2.5 %collective-permute-start.2 = (f32[520,128]{1,0:T(8,128)S(1)}, f32[520,128]{1,0:T(8,128)S(1)}, u32[]{:S(2)}, u32[]{:S(2)}) collective-permute-start(f32[520,128]{1,0:T(8,128)S(1)} %collective-permute-done.1.refs_2_), channel_id=1, source_target_pairs={{0,2},{2,0},{4,6},{6,4},{8,10},{10,8},{12,14},{14,12},{1,3},{3,1},... | collective-permute-start | bytes 798728 | tf_op jit(solution)/shard_map/ppermute | solution.py:16
  26.9 2.0 %collective-permute-start.6 = (f32[520,128]{1,0:T(8,128)S(1)}, f32[520,128]{1,0:T(8,128)S(1)}, u32[]{:S(2)}, u32[]{:S(2)}) collective-permute-start(f32[520,128]{1,0:T(8,128)S(1)} %collective-permute-done.5.refs_6_), channel_id=1, source_target_pairs={{0,2},{2,0},{4,6},{6,4},{8,10},{10,8},{12,14},{14,12},{1,3},{3,1},... | collective-permute-start | bytes 798728 | tf_op jit(solution)/shard_map/ppermute | solution.py:16
  47.8 37.2 %copy-start.24 = (f32[2,32,8,128]{3,2,1,0:T(8,128)S(1)}, f32[2,32,8,128]{3,2,1,0:T(8,128)}, u32[]{:S(2)}) copy-start(f32[2,32,8,128]{3,2,1,0:T(8,128)} %get-tuple-element.41) | copy-start | bytes 786436
  47.8 43.4 %copy-start.23 = (f32[2,32,8,128]{3,2,1,0:T(8,128)S(1)}, f32[2,32,8,128]{3,2,1,0:T(8,128)}, u32[]{:S(2)}) copy-start(f32[2,32,8,128]{3,2,1,0:T(8,128)} %get-tuple-element.54) | copy-start | bytes 786436
  47.8 44.9 %copy-start.13 = (f32[2,32,8,128]{3,2,1,0:T(8,128)S(1)}, f32[2,32,8,128]{3,2,1,0:T(8,128)}, u32[]{:S(2)}) copy-start(f32[2,32,8,128]{3,2,1,0:T(8,128)} %get-tuple-element.60) | copy-start | bytes 786436
  47.8 46.6 %copy-start.22 = (f32[2,32,8,128]{3,2,1,0:T(8,128)S(1)}, f32[2,32,8,128]{3,2,1,0:T(8,128)}, u32[]{:S(2)}) copy-start(f32[2,32,8,128]{3,2,1,0:T(8,128)} %get-tuple-element.42) | copy-start | bytes 786436
  47.8 47.1 %copy-start.11 = (f32[2,32,8,128]{3,2,1,0:T(8,128)S(1)}, f32[2,32,8,128]{3,2,1,0:T(8,128)}, u32[]{:S(2)}) copy-start(f32[2,32,8,128]{3,2,1,0:T(8,128)} %get-tuple-element.56) | copy-start | bytes 786436
  47.8 59.3 %copy-start.9 = (f32[2,32,8,128]{3,2,1,0:T(8,128)S(1)}, f32[2,32,8,128]{3,2,1,0:T(8,128)}, u32[]{:S(2)}) copy-start(f32[2,32,8,128]{3,2,1,0:T(8,128)} %get-tuple-element.55) | copy-start | bytes 786436
  47.8 9.4 %collective-permute-start.14 = (f32[2,32,8,128]{3,2,1,0:T(8,128)}, f32[2,32,8,128]{3,2,1,0:T(8,128)S(1)}, u32[]{:S(2)}, u32[]{:S(2)}) collective-permute-start(f32[2,32,8,128]{3,2,1,0:T(8,128)} %get-tuple-element.47), channel_id=1, source_target_pairs={{0,16},{16,0},{1,17},{17,1},{2,18},{18,2},{3,19},{19,3},{4,20},{20... | collective-permute-start | bytes 786440 | tf_op jit(solution)/shard_map/ppermute | solution.py:16
  49.7 13.3 %collective-permute-start.9 = (f32[2,32,8,128]{3,2,1,0:T(8,128)}, f32[2,32,8,128]{3,2,1,0:T(8,128)S(1)}, u32[]{:S(2)}, u32[]{:S(2)}) collective-permute-start(f32[2,32,8,128]{3,2,1,0:T(8,128)} %get-tuple-element.37), channel_id=1, source_target_pairs={{0,16},{16,0},{1,17},{17,1},{2,18},{18,2},{3,19},{19,3},{4,20},{20... | collective-permute-start | bytes 786440 | tf_op jit(solution)/shard_map/ppermute | solution.py:16
  57.2 11.2 %collective-permute-start.15 = (f32[2,32,8,128]{3,2,1,0:T(8,128)}, f32[2,32,8,128]{3,2,1,0:T(8,128)S(1)}, u32[]{:S(2)}, u32[]{:S(2)}) collective-permute-start(f32[2,32,8,128]{3,2,1,0:T(8,128)} %get-tuple-element.48), channel_id=1, source_target_pairs={{0,16},{16,0},{1,17},{17,1},{2,18},{18,2},{3,19},{19,3},{4,20},{20... | collective-permute-start | bytes 786440 | tf_op jit(solution)/shard_map/ppermute | solution.py:16
  60.0 47.2 %copy-start.8 = (f32[2,32,8,128]{3,2,1,0:T(8,128)S(1)}, f32[2,32,8,128]{3,2,1,0:T(8,128)}, u32[]{:S(2)}) copy-start(f32[2,32,8,128]{3,2,1,0:T(8,128)} %get-tuple-element.43) | copy-start | bytes 786436
  60.0 21.0 %collective-permute-start.16 = (f32[2,32,8,128]{3,2,1,0:T(8,128)S(1)}, f32[2,32,8,128]{3,2,1,0:T(8,128)S(1)}, u32[]{:S(2)}, u32[]{:S(2)}) collective-permute-start(f32[2,32,8,128]{3,2,1,0:T(8,128)S(1)} %add.70), channel_id=1, source_target_pairs={{0,8},{2,10},{4,12},{6,14},{8,0},{10,2},{12,4},{14,6},{1,9},{3,11}... | collective-permute-start | bytes 786440 | tf_op jit(solution)/shard_map/ppermute | solution.py:16
  63.0 21.9 %collective-permute-start.10 = (f32[2,32,8,128]{3,2,1,0:T(8,128)}, f32[2,32,8,128]{3,2,1,0:T(8,128)S(1)}, u32[]{:S(2)}, u32[]{:S(2)}) collective-permute-start(f32[2,32,8,128]{3,2,1,0:T(8,128)} %get-tuple-element.38), channel_id=1, source_target_pairs={{0,16},{16,0},{1,17},{17,1},{2,18},{18,2},{3,19},{19,3},{4,20},{20... | collective-permute-start | bytes 786440 | tf_op jit(solution)/shard_map/ppermute | solution.py:16
  65.7 19.3 %collective-permute-start.11 = (f32[2,32,8,128]{3,2,1,0:T(8,128)S(1)}, f32[2,32,8,128]{3,2,1,0:T(8,128)S(1)}, u32[]{:S(2)}, u32[]{:S(2)}) collective-permute-start(f32[2,32,8,128]{3,2,1,0:T(8,128)S(1)} %add.69), channel_id=1, source_target_pairs={{0,10},{2,8},{4,14},{6,12},{8,2},{10,0},{12,6},{14,4},{1,11},{3,9}... | collective-permute-start | bytes 786440 | tf_op jit(solution)/shard_map/ppermute | solution.py:16
  81.1 38.5 %copy-start.10 = (f32[2,32,8,128]{3,2,1,0:T(8,128)}, f32[2,32,8,128]{3,2,1,0:T(8,128)S(1)}, u32[]{:S(2)}) copy-start(f32[2,32,8,128]{3,2,1,0:T(8,128)S(1)} %collective-permute-done.16.refs_3_) | copy-start | bytes 786436
  81.1 6.6 %collective-permute-start.17 = (f32[2,32,8,128]{3,2,1,0:T(8,128)}, f32[2,32,8,128]{3,2,1,0:T(8,128)S(1)}, u32[]{:S(2)}, u32[]{:S(2)}) collective-permute-start(f32[2,32,8,128]{3,2,1,0:T(8,128)} %get-tuple-element.51), channel_id=1, source_target_pairs={{0,16},{16,0},{1,17},{17,1},{2,18},{18,2},{3,19},{19,3},{4,20},{20... | collective-permute-start | bytes 786440 | tf_op jit(solution)/shard_map/ppermute | solution.py:16
  82.6 8.6 %collective-permute-start.18 = (f32[2,32,8,128]{3,2,1,0:T(8,128)S(1)}, f32[2,32,8,128]{3,2,1,0:T(8,128)S(1)}, u32[]{:S(2)}, u32[]{:S(2)}) collective-permute-start(f32[2,32,8,128]{3,2,1,0:T(8,128)S(1)} %add.71), channel_id=1, source_target_pairs={{0,12},{2,14},{4,8},{6,10},{8,4},{10,6},{12,0},{14,2},{1,13},{3,15... | collective-permute-start | bytes 786440 | tf_op jit(solution)/shard_map/ppermute | solution.py:16
  85.0 9.4 %collective-permute-start.12 = (f32[2,32,8,128]{3,2,1,0:T(8,128)S(1)}, f32[2,32,8,128]{3,2,1,0:T(8,128)S(1)}, u32[]{:S(2)}, u32[]{:S(2)}) collective-permute-start(f32[2,32,8,128]{3,2,1,0:T(8,128)S(1)} %copy-done.24), channel_id=1, source_target_pairs={{0,16},{16,0},{1,17},{17,1},{2,18},{18,2},{3,19},{19,3},{4,20},{20... | collective-permute-start | bytes 786440 | tf_op jit(solution)/shard_map/ppermute | solution.py:16
  91.2 16.1 %collective-permute-start.19 = (f32[2,32,8,128]{3,2,1,0:T(8,128)S(1)}, f32[2,32,8,128]{3,2,1,0:T(8,128)S(1)}, u32[]{:S(2)}, u32[]{:S(2)}) collective-permute-start(f32[2,32,8,128]{3,2,1,0:T(8,128)S(1)} %copy-done.23), channel_id=1, source_target_pairs={{0,16},{16,0},{1,17},{17,1},{2,18},{18,2},{3,19},{19,3},{4,20},{20... | collective-permute-start | bytes 786440 | tf_op jit(solution)/shard_map/ppermute | solution.py:16
  92.7 14.7 %collective-permute-start.23 = (f32[2,32,8,128]{3,2,1,0:T(8,128)S(1)}, f32[2,32,8,128]{3,2,1,0:T(8,128)S(1)}, u32[]{:S(2)}, u32[]{:S(2)}) collective-permute-start(f32[2,32,8,128]{3,2,1,0:T(8,128)S(1)} %add.75), channel_id=1, source_target_pairs={{0,14},{2,12},{4,10},{6,8},{8,6},{10,4},{12,2},{14,0},{1,15},{3,13... | collective-permute-start | bytes 786440 | tf_op jit(solution)/shard_map/ppermute | solution.py:16
  94.4 13.1 %collective-permute-start.13 = (f32[2,32,8,128]{3,2,1,0:T(8,128)S(1)}, f32[2,32,8,128]{3,2,1,0:T(8,128)S(1)}, u32[]{:S(2)}, u32[]{:S(2)}) collective-permute-start(f32[2,32,8,128]{3,2,1,0:T(8,128)S(1)} %copy-done.22), channel_id=1, source_target_pairs={{0,16},{16,0},{1,17},{17,1},{2,18},{18,2},{3,19},{19,3},{4,20},{20... | collective-permute-start | bytes 786440 | tf_op jit(solution)/shard_map/ppermute | solution.py:16
  94.9 18.9 %collective-permute-start.22 = (f32[2,32,8,128]{3,2,1,0:T(8,128)S(1)}, f32[2,32,8,128]{3,2,1,0:T(8,128)S(1)}, u32[]{:S(2)}, u32[]{:S(2)}) collective-permute-start(f32[2,32,8,128]{3,2,1,0:T(8,128)S(1)} %add.74), channel_id=1, source_target_pairs={{0,6},{2,4},{4,2},{6,0},{8,14},{10,12},{12,10},{14,8},{1,7},{3,5},... | collective-permute-start | bytes 786440 | tf_op jit(solution)/shard_map/ppermute | solution.py:16
  107.2 12.4 %collective-permute-start.21 = (f32[2,32,8,128]{3,2,1,0:T(8,128)S(1)}, f32[2,32,8,128]{3,2,1,0:T(8,128)S(1)}, u32[]{:S(2)}, u32[]{:S(2)}) collective-permute-start(f32[2,32,8,128]{3,2,1,0:T(8,128)S(1)} %add.73), channel_id=1, source_target_pairs={{0,4},{2,6},{4,0},{6,2},{8,12},{10,14},{12,8},{14,10},{1,5},{3,7},... | collective-permute-start | bytes 786440 | tf_op jit(solution)/shard_map/ppermute | solution.py:16
  107.3 12.3 %collective-permute-start.20 = (f32[2,32,8,128]{3,2,1,0:T(8,128)S(1)}, f32[2,32,8,128]{3,2,1,0:T(8,128)S(1)}, u32[]{:S(2)}, u32[]{:S(2)}) collective-permute-start(f32[2,32,8,128]{3,2,1,0:T(8,128)S(1)} %add.72), channel_id=1, source_target_pairs={{0,2},{2,0},{4,6},{6,4},{8,10},{10,8},{12,14},{14,12},{1,3},{3,1},... | collective-permute-start | bytes 786440 | tf_op jit(solution)/shard_map/ppermute | solution.py:16
  (17 other events, 135.0 us)

commit v2 on v1

v2 whole, which is shorter than its diff:
```python
import functools
import jax
import jax.numpy as jnp
from jax import lax
from jax.experimental import pallas as pl
from jax.experimental.pallas import tpu as pltpu
from jax.sharding import PartitionSpec as P

TILE = 64
CAP = 16
LANES = 128
MIB = 2**20
LAG_Y = 4
LAG_Z = 5


def swap(block, axis, mask):
    return lax.ppermute(block, axis, [(i, i ^ mask) for i in range(lax.axis_size(axis))])


def gathered(block, axis, order):
    held = {0: block}
    for mask in order:
        held[mask] = jax.tree.map(
            lambda x, low=mask & -mask: swap(x, axis, low), held[mask & (mask - 1)]
        )
    return [held[mask] for mask in range(lax.axis_size(axis))]


def gathered_with(block, axis, order, early):
    held = {0: block}
    for mask in order:
        source = held[mask & (mask - 1)]
        if mask == 3:
            source, early = lax.optimization_barrier((source, early))
            held[mask & (mask - 1)], done = source, early
        held[mask] = swap(source, axis, mask & -mask)
    return [held[mask] for mask in range(lax.axis_size(axis))], done


def parts_of(pair):
    return ((0, pair),)


def pack_a_kernel(a_ref, rows_ref, out_ref, flipped):
    panels, block, width = a_ref.shape
    half, pair, many = width // 2, block // 2, width // block
    for kk in range(panels):
        flipped[...] = a_ref[kk].T
        for first, last in parts_of(pair):
            long = last - first
            for a in range(many):
                at = kk * half + many * first + a * long
                for odd in range(2):
                    taken = flipped[pl.ds(a * block + 2 * first + odd, long, 2), :]
                    out_ref[pl.ds(at, long), odd * block : (odd + 1) * block] = taken
    out_ref[pl.ds(panels * half, 8), :] = jnp.zeros((8, LANES), jnp.float32)
    out_ref[pl.ds(panels * half, panels), :many] = rows_ref[...].astype(jnp.float32)


def pack_b_kernel(b_ref, cols_ref, out_ref):
    count, block, width = b_ref.shape

    @pl.loop(0, count)
    def _(i):
        out_ref[pl.ds(pl.multiple_of(i * block, block), block), :] = b_ref[i]

    out_ref[pl.ds(count * block, 8), :] = jnp.zeros((8, width), jnp.float32)
    out_ref[pl.ds(count * block, count), : cols_ref.shape[1]] = cols_ref[...].astype(jnp.float32)


def product_kernel(n_row, n_col, panels, sets, first, groups, table_ref, *refs):
    a_refs, refs = refs[:n_row], refs[n_row:]
    b_refs, refs = refs[:n_col], refs[n_col:]
    n_out = len(refs) - 8
    out_refs, refs = refs[:n_out], refs[n_out:]
    acc, left, right, prod, index, target, number, sem = refs
    block, width = right.shape[1] // 4, right.shape[2]
    many = width // block
    half = width // 2
    long = left.shape[1] // (2 * many)
    rows = many * long
    low = lax.broadcasted_iota(jnp.int32, (1, LANES), 1) < block

    my_row, my_col = lax.axis_index("row"), lax.axis_index("col")

    def place_b(m):
        label = lax.rem(lax.bitwise_xor(my_row, m) + my_col, n_row)
        offset = lax.rem(label - my_row + n_row, n_row)
        mask = lax.bitwise_xor(lax.rem(offset, n_col), my_col)
        return mask, lax.div(offset, n_col)

    count = n_row * panels
    for m in range(n_row):
        index[pl.ds(m * panels, panels), :] = a_refs[m][pl.ds(panels * half, panels), :]
    for m in range(n_col):
        tail = b_refs[m][pl.ds(sets * panels * block, sets * panels), pl.ds(0, LANES)]
        index[pl.ds(count + m * sets * panels, sets * panels), :] = tail
    down = index[pl.ds(0, count), :].T.astype(jnp.int32)
    across = lax.broadcasted_iota(jnp.int32, (many, LANES), 1)
    hot = [jnp.where(down[:many, k : k + 1] == across, 1.0, 0.0) for k in range(count)]
    hot = jnp.concatenate(hot, axis=0)[:, :TILE].astype(jnp.bfloat16)
    entries = table_ref[...]
    halves = [lax.shift_right_logical(entries, 4), lax.bitwise_and(entries, 15)]
    upper, lower = [
        jnp.dot(hot, x.astype(jnp.float32).astype(jnp.bfloat16), preferred_element_type=jnp.float32) for x in halves
    ]
    found = (upper * 16 + lower).astype(jnp.int32) * long
    per_row = LANES // many
    for k in range(count):
        mask, which = place_b(k // panels)
        at = count + (mask * sets + which) * panels + k % panels
        cols = jnp.broadcast_to(index[pl.ds(at, 1), :], (many, LANES)).astype(jnp.int32)
        picked = jnp.take_along_axis(found[k * many : (k + 1) * many, :], cols, axis=1)
        picked = jnp.where(across < many, picked, 0)
        shift = k % per_row * many
        picked = pltpu.roll(picked, shift, 1) if shift else picked
        group = pl.ds(k // per_row * many, many)
        target[group, :] = picked if shift == 0 else target[group, :] + picked
    copy = pltpu.make_async_copy(target, number, sem)
    copy.start()

    @pl.loop(0, acc.shape[0] // (8 * long))
    def _(i):
        acc[pl.ds(pl.multiple_of(i * 8 * long, 8), 8 * long), :] = jnp.zeros((8 * long, LANES), jnp.float32)

    for m in range(n_row):

        @pl.loop(0, panels)
        def _(kk, m=m):
            a = a_refs[m][pl.ds(pl.multiple_of(kk * half + many * first, 8), rows), :]
            turned = pltpu.roll(a, block, 1)
            rest = a - a.astype(jnp.bfloat16).astype(jnp.float32)
            turned_rest = pltpu.roll(rest, block, 1)
            at = m * panels + kk
            left[at, pl.ds(0, rows), pl.ds(0, LANES)] = jnp.where(low, a, turned).astype(jnp.bfloat16)
            left[at, pl.ds(0, rows), pl.ds(LANES, LANES)] = rest.astype(jnp.bfloat16)
            left[at, pl.ds(rows, rows), pl.ds(0, LANES)] = jnp.where(low, turned, a).astype(jnp.bfloat16)
            left[at, pl.ds(rows, rows), pl.ds(LANES, LANES)] = turned_rest.astype(jnp.bfloat16)

    for m in range(n_col):

        @pl.loop(0, sets * panels)
        def _(i, m=m):
            b = b_refs[m][pl.ds(pl.multiple_of(i * block, block), block), :]
            high = b.astype(jnp.bfloat16)
            rest = (b - high.astype(jnp.float32)).astype(jnp.bfloat16)
            at = m * sets * panels + i
            right[at, pl.ds(0, block), :] = high
            right[at, pl.ds(block, block), :] = rest
            right[at, pl.ds(2 * block, block), :] = high
            right[at, pl.ds(3 * block, block), :] = jnp.zeros_like(high)

    copy.wait()

    def multiply(m, kk):
        mask, which = place_b(m)
        prod[kk] = jnp.dot(
            left[m * panels + kk],
            right[(mask * sets + which) * panels + kk],
            preferred_element_type=jnp.float32,
        )

    def add(m, kk):
        k = m * panels + kk
        group, start = lax.div(k, per_row) * many, lax.rem(k, per_row) * many
        for a in range(many):
            places = [pl.multiple_of(number[group + a, start + b], 8) for b in range(many)]
            even = prod[kk, pl.ds(a * long, long), :]
            odd = prod[kk, pl.ds(rows + a * long, long), :]
            blocks = []
            for q in range(many // 2):
                e, o = even[:, q * LANES : (q + 1) * LANES], odd[:, q * LANES : (q + 1) * LANES]
                turned = pltpu.roll(jnp.where(low, o, e), block, 1)
                blocks += [jnp.where(low, e, turned), jnp.where(low, turned, o)]
            sums = [acc[pl.ds(at, long), :] + new for at, new in zip(places, blocks)]
            for at, new in zip(places, sums):
                acc[pl.ds(at, long), :] = new

    multiply(0, 0)

    @pl.loop(0, n_row)
    def _(m):
        for kk in range(panels):
            if kk + 1 < panels:
                multiply(m, kk + 1)
            else:
                multiply(lax.rem(m + 1, n_row), 0)
            add(m, kk)

    @pl.loop(0, long // 8)
    def _(j):
        at = pl.multiple_of(j * 8, 8)
        for out, out_ref in enumerate(out_refs):
            layer, group = divmod(out, len(groups))
            for i, m in enumerate(groups[group]):
                for eight in range(CAP // 8):
                    start = ((layer * n_row + m) * CAP + eight * 8) * long
                    taken = [acc[pl.ds(pl.multiple_of(start + s * long + at, 8), 8), :] for s in range(8)]
                    out_ref[i, eight, pl.ds(at, 8)] = jnp.swapaxes(jnp.stack(taken), 0, 1)


def place_kernel(pieces, *refs):
    sources, out_ref, sems = refs[: len(pieces)], refs[len(pieces)], refs[len(pieces) + 1]
    my_row = lax.axis_index("row")
    copies = []
    for i, (m, first) in enumerate(pieces):
        size, long = sources[i].shape[:2]
        at = pl.multiple_of(lax.bitwise_xor(my_row, m) * size, size)
        target = out_ref.at[pl.ds(at, size), pl.ds(first, long)]
        copies.append(pltpu.make_async_copy(sources[i], target, sems.at[i]))
    for copy in copies:
        copy.start()
    for copy in copies:
        copy.wait()


def body(a_val, a_rows, b_val, b_cols, pattern, owners):
    n_row, n_col, n_layer = (lax.axis_size(x) for x in ("row", "col", "layer"))
    panels, block, width = a_val.shape[3:]
    sets = b_val.shape[3]
    many = width // block
    pair = block // 2
    kept = pattern.shape[2]
    a_val, a_rows = a_val[0, 0, 0], a_rows[0, 0, 0]
    b_val = b_val[0, 0, 0].reshape(sets * panels, block, width)
    b_cols = b_cols[0, 0, 0].reshape(sets * panels, many)
    vmem, anywhere = pl.BlockSpec(memory_space=pltpu.VMEM), pl.BlockSpec(memory_space=pl.ANY)

    def room(*arrays):
        return pltpu.CompilerParams(vmem_limit_bytes=2 * MIB + sum(arrays))

    a_shape = (panels * width // 2 + 8, LANES)
    b_shape = (sets * panels * block + 8, width)

    a_packed = pl.pallas_call(
        pack_a_kernel,
        out_shape=jax.ShapeDtypeStruct(a_shape, jnp.float32),
        in_specs=[vmem] * 2,
        out_specs=vmem,
        scratch_shapes=[pltpu.VMEM((width, block), jnp.float32)],
        compiler_params=room(a_val.size * 8, width * LANES * 4),
    )(a_val, a_rows)
    b_packed = pl.pallas_call(
        pack_b_kernel,
        out_shape=jax.ShapeDtypeStruct(b_shape, jnp.float32),
        in_specs=[vmem] * 2,
        out_specs=vmem,
        compiler_params=room(b_val.size * 8),
    )(b_val, b_cols)
    b_held = gathered(b_packed, "col", range(1, n_col))

    owner = owners[0, :, 0]
    my_row, my_layer = lax.axis_index("row"), lax.axis_index("layer")
    before = (owner[:, None] == owner[None, :]) & (
        jnp.arange(kept)[None, :] < jnp.arange(kept)[:, None]
    )
    rank = jnp.sum(before.astype(jnp.int32), axis=1)
    unit = ((owner // n_row) ^ my_layer) * n_row + ((owner % n_row) ^ my_row)
    slots = n_layer * n_row * CAP
    slot = unit * CAP + rank
    codes = jnp.arange(TILE * TILE, dtype=jnp.int32)
    hit = codes[:, None] == pattern[0, 0][None, :]
    table = slots + jnp.sum(jnp.where(hit, slot[None, :] - slots, 0), axis=1)
    table = jnp.pad(table.reshape(TILE, TILE), ((0, 0), (0, LANES - TILE)))

    high_first = sorted(range(1, n_row), key=lambda m: (m & 1, m.bit_count(), -m))
    a_held, table = gathered_with(a_packed, "row", high_first, table)

    b_count = n_col * sets * panels
    held_bytes = n_row * a_shape[0] * LANES * 4 + n_col * b_shape[0] * width * 4
    far, near = list(range(n_row // 2, n_row)), [*range(2, n_row // 2), 1, 0]

    def products(first, last, groups, table):
        long = last - first
        shapes = [(len(g), CAP // 8, long, 8, LANES) for g in groups] * n_layer
        scratch_bytes = (
            (slots + 8) * long * LANES * 4
            + n_row * panels * many * long * block * 16
            + b_count * width * block * 8
            + panels * 2 * many * long * width * 4
        )
        made = pl.pallas_call(
            functools.partial(product_kernel, n_row, n_col, panels, sets, first, groups),
            out_shape=[jax.ShapeDtypeStruct(shape, jnp.float32) for shape in shapes],
            in_specs=[vmem] * (1 + n_row + n_col),
            out_specs=[vmem] * len(shapes),
            scratch_shapes=[
                pltpu.VMEM(((slots + 8) * long, LANES), jnp.float32),
                pltpu.VMEM((n_row * panels, 2 * many * long, 4 * block), jnp.bfloat16),
                pltpu.VMEM((b_count, 4 * block, width), jnp.bfloat16),
                pltpu.VMEM((panels, 2 * many * long, width), jnp.float32),
                pltpu.VMEM(((n_row + n_col * sets) * panels, LANES), jnp.float32),
                pltpu.VMEM((many * -(-n_row * panels * many // LANES), LANES), jnp.int32),
                pltpu.SMEM((many * -(-n_row * panels * many // LANES), LANES), jnp.int32),
                pltpu.SemaphoreType.DMA,
            ],
            compiler_params=room(held_bytes, scratch_bytes, slots * long * LANES * 4),
            cost_estimate=pl.CostEstimate(
                flops=n_row * panels * 2 * many * long * width * 4 * block * 2,
                bytes_accessed=held_bytes + slots * long * LANES * 4,
                transcendentals=0,
            ),
        )(table, *a_held, *b_held)
        return list(made[: len(groups)]), list(made[len(groups) :])

    order = far + near
    ((first, last),) = parts_of(pair)
    own, gone = products(first, last, [[m] for m in order], table)
    others, pieces = [], {}
    for at, m in enumerate(order):
        if at >= LAG_Y:
            gone[at], others[at - LAG_Y] = lax.optimization_barrier((gone[at], others[at - LAG_Y]))
        if at >= LAG_Z:
            key = order[at - LAG_Z], first
            gone[at], pieces[key] = lax.optimization_barrier((gone[at], pieces[key]))
        others.append(swap(gone[at], "layer", 1))
        total = own[at][0] + others[at][0]
        pieces[m, first] = swap(total, "row", m) if m else total
    keys = list(pieces)
    owned = pl.pallas_call(
        functools.partial(place_kernel, keys),
        out_shape=jax.ShapeDtypeStruct((n_row * CAP // 8, pair, 8, LANES), jnp.float32),
        in_specs=[vmem] * len(keys),
        out_specs=anywhere,
        scratch_shapes=[pltpu.SemaphoreType.DMA((len(keys),))],
        compiler_params=room(n_row * CAP * block * block * 4),
    )(*pieces.values())
    return owned.transpose(0, 2, 1, 3).reshape(n_row * CAP, block * block)


def solution(mesh):
    return jax.shard_map(
        body,
        mesh=mesh,
        in_specs=(
            P("col", "layer", "row", None, None, None),
            P("col", "layer", "row", None, None),
            P("row", "layer", "col", None, None, None, None),
            P("row", "layer", "col", None, None, None),
            P("col", "row", None),
            P("col", "row", None),
        ),
        out_specs=P(("layer", "row"), "col"),
        check_vma=False,
    )
```

time: 124 us -> 99.8 us (0.80); the launches traced: 123 us -> 97.8 us
  Pallas kernels: 21.8 us -> 11 us
  waiting for transfers between devices: 51.5 us -> 40.9 us
  other arithmetic: 6.64 us -> 1.08 us
  starting transfers between devices: 39.6 us -> 42.6 us
  local copies, waits for them, and re-layouts: 3.41 us -> 2.05 us
    pallas_call x3 -> x4, Pallas kernels: 21.8 us -> 11 us  [the longest x1 9.24 us: products(): pl.pallas_call(functools.partial(product_kernel, n_row, n_col, panels, se...]
    ppermute x24 -> x23, waiting for transfers between devices: 51.5 us -> 40.9 us  [swap(): lax.ppermute(block, axis, [(i, i ^ mask) for i in range(lax.axis_size(axi...]
    ppermute x24 -> x23, starting transfers between devices: 39.6 us -> 42.6 us  [swap(): lax.ppermute(block, axis, [(i, i ^ mask) for i in range(lax.axis_size(axi...]
    add x7 -> x9, other arithmetic: 3.09 us -> 0.27 us  [the longest x8 0.26 us: body(): total = own[at][0] + others[at][0]]
    unnamed x50 -> x12, local copies, waits for them, and re-layouts: 2.64 us -> 1.97 us
  transfers between devices with their start and end apart: 24 -> 23, of which waited for: 10 -> 9; matrix products, arithmetic and copies ran while one was open for 6% -> 1% of each run, Pallas kernels for 2% -> 0%
where the time goes in v2:
time: 99.8 us; the launch traced here: 97.8 us
  starting transfers between devices  42.6 us (43%)
  waiting for transfers between devices  40.9 us (41%)
  Pallas kernels  11 us (11%)
  local copies, waits for them, and re-layouts  2.05 us (2%)
  other arithmetic  1.08 us (1%)
    ppermute x23, starting transfers between devices, swap(): lax.ppermute(block, axis, [(i, i ^ mask) for i in range(lax.axis_size(axi...  42.6 us
    ppermute x23, waiting for transfers between devices, swap(): lax.ppermute(block, axis, [(i, i ^ mask) for i in range(lax.axis_size(axi...  40.9 us
    pallas_call x1, Pallas kernels, products(): pl.pallas_call(functools.partial(product_kernel, n_row, n_col, panels, se...  9.24 us
  transfers between devices with their start and end apart: 23, of which 9 were waited for; matrix products, arithmetic and copies ran while one was open for 1% of the time, Pallas kernels for 0%

profile of v2, /device:TPU:0, one launch (start us, length us, event | category | flops | bytes accessed | tf_op | source)
XLA Modules:
  0.0 97.8 jit_solution(5584976030514656216)
XLA Ops:
  0.0 1.3 %copy-done = f32[1,1,1,4,2,64,512]{6,5,4,3,2,1,0:T(8,128)S(1)} copy-done((f32[1,1,1,4,2,64,512]{6,5,4,3,2,1,0:T(8,128)S(1)}, f32[1,1,1,4,2,64,512]{6,5,4,3,2,1,0:T(8,128)}, u32[]{:S(2)}) %copy-start) | copy-done | bytes 1048600
  1.3 0.7 copy-done.2
  2.1 3.0 %collective-permute-start.7 = (f32[520,512]{1,0:T(8,128)S(1)}, f32[520,512]{1,0:T(8,128)S(1)}, u32[]{:S(2)}, u32[]{:S(2)}) collective-permute-start(f32[520,512]{1,0:T(8,128)S(1)} %shard_map.65.refs_8_), channel_id=1, source_target_pairs={{0,1},{1,0},{2,3},{3,2},{4,5},{5,4},{6,7},{7,6},{8,9},{9,8},{10,11... | collective-permute-start | bytes 3194888 | tf_op jit(solution)/shard_map/ppermute | solution.py:18
  5.4 2.7 %collective-permute-start.3 = (f32[520,128]{1,0:T(8,128)S(1)}, f32[520,128]{1,0:T(8,128)S(1)}, u32[]{:S(2)}, u32[]{:S(2)}) collective-permute-start(f32[520,128]{1,0:T(8,128)S(1)} %shard_map.64.refs_0_), channel_id=1, source_target_pairs={{0,8},{2,10},{4,12},{6,14},{8,0},{10,2},{12,4},{14,6},{1,9},{3,11}... | collective-permute-start | bytes 798728 | tf_op jit(solution)/shard_map/ppermute | solution.py:18
  8.1 1.6 %collective-permute-start = (f32[520,128]{1,0:T(8,128)S(1)}, f32[520,128]{1,0:T(8,128)S(1)}, u32[]{:S(2)}, u32[]{:S(2)}) collective-permute-start(f32[520,128]{1,0:T(8,128)S(1)} %shard_map.64.refs_0_), channel_id=1, source_target_pairs={{0,4},{2,6},{4,0},{6,2},{8,12},{10,14},{12,8},{14,10},{1,5},{3,7},... | collective-permute-start | bytes 798728 | tf_op jit(solution)/shard_map/ppermute | solution.py:18
  9.8 10.2 %collective-permute-done.3.refs_4_ = f32[520,128]{1,0:T(8,128)S(1)} collective-permute-done((f32[520,128]{1,0:T(8,128)S(1)}, f32[520,128]{1,0:T(8,128)S(1)}, u32[]{:S(2)}, u32[]{:S(2)}) %collective-permute-start.3) | collective-permute-done | bytes 266272 | tf_op jit(solution)/shard_map/ppermute | solution.py:18
  20.0 0.6 collective-permute-start.5
  20.6 0.6 select_reduce_fusion
  21.5 0.5 collective-permute-start.4
  22.0 5.2 %collective-permute-done.5.refs_6_ = f32[520,128]{1,0:T(8,128)S(1)} collective-permute-done((f32[520,128]{1,0:T(8,128)S(1)}, f32[520,128]{1,0:T(8,128)S(1)}, u32[]{:S(2)}, u32[]{:S(2)}) %collective-permute-start.5) | collective-permute-done | bytes 266272 | tf_op jit(solution)/shard_map/ppermute | solution.py:18
  27.2 1.5 %collective-permute-done.6.refs_7_ = f32[520,128]{1,0:T(8,128)S(1)} collective-permute-done((f32[520,128]{1,0:T(8,128)S(1)}, f32[520,128]{1,0:T(8,128)S(1)}, u32[]{:S(2)}, u32[]{:S(2)}) %collective-permute-start.6) | collective-permute-done | bytes 266272 | tf_op jit(solution)/shard_map/ppermute | solution.py:18
  28.8 9.2 %shard_map.66 = (f32[1,2,32,8,128]{4,3,2,1,0:T(8,128)S(1)}, f32[1,2,32,8,128]{4,3,2,1,0:T(8,128)S(1)}, f32[1,2,32,8,128]{4,3,2,1,0:T(8,128)S(1)}, f32[1,2,32,8,1...) custom-call(s32[64,128]{1,0:T(8,128)S(1)} %pad.4.table_ref, ...), custom_call_target="tpu_custom_call" | custom-call | flops 2147483648 | bytes 8454144 | tf_op jit(solution)/shard_map/pallas_call | solution.py:283
  38.0 1.6 %collective-permute-start.9 = (f32[1,2,32,8,128]{4,3,2,1,0:T(8,128)S(1)}, f32[1,2,32,8,128]{4,3,2,1,0:T(8,128)S(1)}, u32[]{:S(2)}, u32[]{:S(2)}) collective-permute-start(f32[1,2,32,8,128]{4,3,2,1,0:T(8,128)S(1)} %get-tuple-element.39), channel_id=1, source_target_pairs={{0,16},{16,0},{1,17},{17,1},{2,18},{18,2},{3,19},{19,3},{4,20},{20... | collective-permute-start | bytes 786440 | tf_op jit(solution)/shard_map/ppermute | solution.py:18
  39.6 0.5 collective-permute-start.8
  40.1 1.6 %collective-permute-start.11 = (f32[1,2,32,8,128]{4,3,2,1,0:T(8,128)S(1)}, f32[1,2,32,8,128]{4,3,2,1,0:T(8,128)S(1)}, u32[]{:S(2)}, u32[]{:S(2)}) collective-permute-start(f32[1,2,32,8,128]{4,3,2,1,0:T(8,128)S(1)} %get-tuple-element.42), channel_id=1, source_target_pairs={{0,16},{16,0},{1,17},{17,1},{2,18},{18,2},{3,19},{19,3},{4,20},{20... | collective-permute-start | bytes 786440 | tf_op jit(solution)/shard_map/ppermute | solution.py:18
  42.1 5.1 %collective-permute-done.9 = f32[1,2,32,8,128]{4,3,2,1,0:T(8,128)S(1)} collective-permute-done((f32[1,2,32,8,128]{4,3,2,1,0:T(8,128)S(1)}, f32[1,2,32,8,128]{4,3,2,1,0:T(8,128)S(1)}, u32[]{:S(2)}, u32[]{:S(2)}) %collective-permute-start.9) | collective-permute-done | bytes 262176 | tf_op jit(solution)/shard_map/ppermute | solution.py:18
  47.3 3.4 %collective-permute-start.10 = (f32[2,32,8,128]{3,2,1,0:T(8,128)S(1)}, f32[2,32,8,128]{3,2,1,0:T(8,128)S(1)}, u32[]{:S(2)}, u32[]{:S(2)}) collective-permute-start(f32[2,32,8,128]{3,2,1,0:T(8,128)S(1)} %add_bitcast_fusion.7), channel_id=1, source_target_pairs={{0,8},{2,10},{4,12},{6,14},{8,0},{10,2},{12,4},{14,6},{1,9},{3,11}... | collective-permute-start | bytes 786440 | tf_op jit(solution)/shard_map/ppermute | solution.py:18
  50.7 2.2 %collective-permute-done.8 = f32[1,2,32,8,128]{4,3,2,1,0:T(8,128)S(1)} collective-permute-done((f32[1,2,32,8,128]{4,3,2,1,0:T(8,128)S(1)}, f32[1,2,32,8,128]{4,3,2,1,0:T(8,128)S(1)}, u32[]{:S(2)}, u32[]{:S(2)}) %collective-permute-start.8) | collective-permute-done | bytes 262176 | tf_op jit(solution)/shard_map/ppermute | solution.py:18
  52.9 1.5 %collective-permute-start.12 = (f32[2,32,8,128]{3,2,1,0:T(8,128)S(1)}, f32[2,32,8,128]{3,2,1,0:T(8,128)S(1)}, u32[]{:S(2)}, u32[]{:S(2)}) collective-permute-start(f32[2,32,8,128]{3,2,1,0:T(8,128)S(1)} %add_bitcast_fusion.6), channel_id=1, source_target_pairs={{0,10},{2,8},{4,14},{6,12},{8,2},{10,0},{12,6},{14,4},{1,11},{3,9}... | collective-permute-start | bytes 786440 | tf_op jit(solution)/shard_map/ppermute | solution.py:18
  54.4 1.5 %collective-permute-start.16 = (f32[1,2,32,8,128]{4,3,2,1,0:T(8,128)S(1)}, f32[1,2,32,8,128]{4,3,2,1,0:T(8,128)S(1)}, u32[]{:S(2)}, u32[]{:S(2)}) collective-permute-start(f32[1,2,32,8,128]{4,3,2,1,0:T(8,128)S(1)} %get-tuple-element.54), channel_id=1, source_target_pairs={{0,16},{16,0},{1,17},{17,1},{2,18},{18,2},{3,19},{19,3},{4,20},{20... | collective-permute-start | bytes 786440 | tf_op jit(solution)/shard_map/ppermute | solution.py:18
  55.9 2.5 %collective-permute-done.11 = f32[1,2,32,8,128]{4,3,2,1,0:T(8,128)S(1)} collective-permute-done((f32[1,2,32,8,128]{4,3,2,1,0:T(8,128)S(1)}, f32[1,2,32,8,128]{4,3,2,1,0:T(8,128)S(1)}, u32[]{:S(2)}, u32[]{:S(2)}) %collective-permute-start.11) | collective-permute-done | bytes 262176 | tf_op jit(solution)/shard_map/ppermute | solution.py:18
  58.5 4.6 %collective-permute-start.14 = (f32[2,32,8,128]{3,2,1,0:T(8,128)S(1)}, f32[2,32,8,128]{3,2,1,0:T(8,128)S(1)}, u32[]{:S(2)}, u32[]{:S(2)}) collective-permute-start(f32[2,32,8,128]{3,2,1,0:T(8,128)S(1)} %add_bitcast_fusion.5), channel_id=1, source_target_pairs={{0,12},{2,14},{4,8},{6,10},{8,4},{10,6},{12,0},{14,2},{1,13},{3,15... | collective-permute-start | bytes 786440 | tf_op jit(solution)/shard_map/ppermute | solution.py:18
  63.1 10.7 %collective-permute-done.10.refs_0_ = f32[2,32,8,128]{3,2,1,0:T(8,128)S(1)} collective-permute-done((f32[2,32,8,128]{3,2,1,0:T(8,128)S(1)}, f32[2,32,8,128]{3,2,1,0:T(8,128)S(1)}, u32[]{:S(2)}, u32[]{:S(2)}) %collective-permute-start.10) | collective-permute-done | bytes 262176 | tf_op jit(solution)/shard_map/ppermute | solution.py:18
  73.8 1.5 %collective-permute-start.18 = (f32[1,2,32,8,128]{4,3,2,1,0:T(8,128)S(1)}, f32[1,2,32,8,128]{4,3,2,1,0:T(8,128)S(1)}, u32[]{:S(2)}, u32[]{:S(2)}) collective-permute-start(f32[1,2,32,8,128]{4,3,2,1,0:T(8,128)S(1)} %get-tuple-element.56), channel_id=1, source_target_pairs={{0,16},{16,0},{1,17},{17,1},{2,18},{18,2},{3,19},{19,3},{4,20},{20... | collective-permute-start | bytes 786440 | tf_op jit(solution)/shard_map/ppermute | solution.py:18
  75.4 1.6 %collective-permute-start.15 = (f32[2,32,8,128]{3,2,1,0:T(8,128)S(1)}, f32[2,32,8,128]{3,2,1,0:T(8,128)S(1)}, u32[]{:S(2)}, u32[]{:S(2)}) collective-permute-start(f32[2,32,8,128]{3,2,1,0:T(8,128)S(1)} %add_bitcast_fusion.4), channel_id=1, source_target_pairs={{0,14},{2,12},{4,10},{6,8},{8,6},{10,4},{12,2},{14,0},{1,15},{3,13... | collective-permute-start | bytes 786440 | tf_op jit(solution)/shard_map/ppermute | solution.py:18
  77.0 1.3 %collective-permute-start.20 = (f32[1,2,32,8,128]{4,3,2,1,0:T(8,128)S(1)}, f32[1,2,32,8,128]{4,3,2,1,0:T(8,128)S(1)}, u32[]{:S(2)}, u32[]{:S(2)}) collective-permute-start(f32[1,2,32,8,128]{4,3,2,1,0:T(8,128)S(1)} %get-tuple-element.58), channel_id=1, source_target_pairs={{0,16},{16,0},{1,17},{17,1},{2,18},{18,2},{3,19},{19,3},{4,20},{20... | collective-permute-start | bytes 786440 | tf_op jit(solution)/shard_map/ppermute | solution.py:18
  78.3 2.1 %collective-permute-start.17 = (f32[2,32,8,128]{3,2,1,0:T(8,128)S(1)}, f32[2,32,8,128]{3,2,1,0:T(8,128)S(1)}, u32[]{:S(2)}, u32[]{:S(2)}) collective-permute-start(f32[2,32,8,128]{3,2,1,0:T(8,128)S(1)} %add_bitcast_fusion.3), channel_id=1, source_target_pairs={{0,4},{2,6},{4,0},{6,2},{8,12},{10,14},{12,8},{14,10},{1,5},{3,7},... | collective-permute-start | bytes 786440 | tf_op jit(solution)/shard_map/ppermute | solution.py:18
  80.4 0.6 collective-permute-start.22
  81.1 9.9 %collective-permute-start.19 = (f32[2,32,8,128]{3,2,1,0:T(8,128)S(1)}, f32[2,32,8,128]{3,2,1,0:T(8,128)S(1)}, u32[]{:S(2)}, u32[]{:S(2)}) collective-permute-start(f32[2,32,8,128]{3,2,1,0:T(8,128)S(1)} %add_bitcast_fusion.2), channel_id=1, source_target_pairs={{0,6},{2,4},{4,2},{6,0},{8,14},{10,12},{12,10},{14,8},{1,7},{3,5},... | collective-permute-start | bytes 786440 | tf_op jit(solution)/shard_map/ppermute | solution.py:18
  91.1 2.0 %collective-permute-start.21 = (f32[2,32,8,128]{3,2,1,0:T(8,128)S(1)}, f32[2,32,8,128]{3,2,1,0:T(8,128)S(1)}, u32[]{:S(2)}, u32[]{:S(2)}) collective-permute-start(f32[2,32,8,128]{3,2,1,0:T(8,128)S(1)} %add_bitcast_fusion.1), channel_id=1, source_target_pairs={{0,2},{2,0},{4,6},{6,4},{8,10},{10,8},{12,14},{14,12},{1,3},{3,1},... | collective-permute-start | bytes 786440 | tf_op jit(solution)/shard_map/ppermute | solution.py:18
  93.2 3.2 %collective-permute-done.19.refs_5_ = f32[2,32,8,128]{3,2,1,0:T(8,128)S(1)} collective-permute-done((f32[2,32,8,128]{3,2,1,0:T(8,128)S(1)}, f32[2,32,8,128]{3,2,1,0:T(8,128)S(1)}, u32[]{:S(2)}, u32[]{:S(2)}) %collective-permute-start.19) | collective-permute-done | bytes 262176 | tf_op jit(solution)/shard_map/ppermute | solution.py:18
  96.4 1.4 %shard_map.67 = f32[16,32,8,128]{3,2,1,0:T(8,128)} custom-call(f32[2,32,8,128]{3,2,1,0:T(8,128)S(1)} %collective-permute-done.10.refs_0_, f32[2,32,8,128]{3,2,1,0:T(8,128)S(1)} %collective-permute-done.12.refs_1_, f32[2,32,8,128]{3,2,1,0:T(8,128)S(1)} %collective-permute-done.14.refs_2_, f32[2,32,8,128]{3,2,1,0:T(8,128)S(1)} %collective-permute-done.15.refs_3_, ...), custom_call_target="tpu_custom_call" | custom-call | tf_op jit(solution)/shard_map/pallas_call | solution.py:321
  (44 shorter events, 1.6 us)
Async XLA Ops:
  0.0 5.1 %copy-start.3 = (s32[1,1,1,2,8]{4,3,2,1,0:T(2,128)S(1)}, s32[1,1,1,2,8]{4,3,2,1,0:T(2,128)}, u32[]{:S(2)}) copy-start(s32[1,1,1,2,8]{4,3,2,1,0:T(2,128)} %param.7) | copy-start | bytes 196
  0.0 9.6 %copy-start.4 = (s32[1,256,1]{1,2,0:T(1,128)S(1)}, s32[1,256,1]{1,2,0:T(1,128)}, u32[]{:S(2)}) copy-start(s32[1,256,1]{1,2,0:T(1,128)} %param.11) | copy-start | bytes 3076
  0.0 20.6 %copy-start.5 = (s32[1,1,256]{2,1,0:T(1,128)S(1)}, s32[1,1,256]{2,1,0:T(1,128)}, u32[]{:S(2)}) copy-start(s32[1,1,256]{2,1,0:T(1,128)} %param.10) | copy-start | bytes 3076
  0.0 1.3 %copy-start = (f32[1,1,1,4,2,64,512]{6,5,4,3,2,1,0:T(8,128)S(1)}, f32[1,1,1,4,2,64,512]{6,5,4,3,2,1,0:T(8,128)}, u32[]{:S(2)}) copy-start(f32[1,1,1,4,2,64,512]{6,5,4,3,2,1,0:T(8,128)} %param.8) | copy-start | bytes 3145732
  1.3 0.7 copy-start.2
  2.0 3.1 %copy-start.1 = (f32[1,1,1,2,64,512]{5,4,3,2,1,0:T(8,128)S(1)}, f32[1,1,1,2,64,512]{5,4,3,2,1,0:T(8,128)}, u32[]{:S(2)}) copy-start(f32[1,1,1,2,64,512]{5,4,3,2,1,0:T(8,128)} %param.6) | copy-start | bytes 786436
  2.1 26.7 %collective-permute-start.7 = (f32[520,512]{1,0:T(8,128)S(1)}, f32[520,512]{1,0:T(8,128)S(1)}, u32[]{:S(2)}, u32[]{:S(2)}) collective-permute-start(f32[520,512]{1,0:T(8,128)S(1)} %shard_map.65.refs_8_), channel_id=1, source_target_pairs={{0,1},{1,0},{2,3},{3,2},{4,5},{5,4},{6,7},{7,6},{8,9},{9,8},{10,11... | collective-permute-start | bytes 3194888 | tf_op jit(solution)/shard_map/ppermute | solution.py:18
  5.4 14.6 %collective-permute-start.3 = (f32[520,128]{1,0:T(8,128)S(1)}, f32[520,128]{1,0:T(8,128)S(1)}, u32[]{:S(2)}, u32[]{:S(2)}) collective-permute-start(f32[520,128]{1,0:T(8,128)S(1)} %shard_map.64.refs_0_), channel_id=1, source_target_pairs={{0,8},{2,10},{4,12},{6,14},{8,0},{10,2},{12,4},{14,6},{1,9},{3,11}... | collective-permute-start | bytes 798728 | tf_op jit(solution)/shard_map/ppermute | solution.py:18
  8.1 19.2 %collective-permute-start.1 = (f32[520,128]{1,0:T(8,128)S(1)}, f32[520,128]{1,0:T(8,128)S(1)}, u32[]{:S(2)}, u32[]{:S(2)}) collective-permute-start(f32[520,128]{1,0:T(8,128)S(1)} %shard_map.64.refs_0_), channel_id=1, source_target_pairs={{0,2},{2,0},{4,6},{6,4},{8,10},{10,8},{12,14},{14,12},{1,3},{3,1},... | collective-permute-start | bytes 798728 | tf_op jit(solution)/shard_map/ppermute | solution.py:18
  8.1 13.4 %collective-permute-start = (f32[520,128]{1,0:T(8,128)S(1)}, f32[520,128]{1,0:T(8,128)S(1)}, u32[]{:S(2)}, u32[]{:S(2)}) collective-permute-start(f32[520,128]{1,0:T(8,128)S(1)} %shard_map.64.refs_0_), channel_id=1, source_target_pairs={{0,4},{2,6},{4,0},{6,2},{8,12},{10,14},{12,8},{14,10},{1,5},{3,7},... | collective-permute-start | bytes 798728 | tf_op jit(solution)/shard_map/ppermute | solution.py:18
  20.0 7.2 %collective-permute-start.5 = (f32[520,128]{1,0:T(8,128)S(1)}, f32[520,128]{1,0:T(8,128)S(1)}, u32[]{:S(2)}, u32[]{:S(2)}) collective-permute-start(f32[520,128]{1,0:T(8,128)S(1)} %collective-permute-done.3.refs_4_), channel_id=1, source_target_pairs={{0,4},{2,6},{4,0},{6,2},{8,12},{10,14},{12,8},{14,10},{1,5},{3,7},... | collective-permute-start | bytes 798728 | tf_op jit(solution)/shard_map/ppermute | solution.py:18
  21.5 5.8 %collective-permute-start.2 = (f32[520,128]{1,0:T(8,128)S(1)}, f32[520,128]{1,0:T(8,128)S(1)}, u32[]{:S(2)}, u32[]{:S(2)}) collective-permute-start(f32[520,128]{1,0:T(8,128)S(1)} %collective-permute-done.refs_2_), channel_id=1, source_target_pairs={{0,2},{2,0},{4,6},{6,4},{8,10},{10,8},{12,14},{14,12},{1,3},{3,1},... | collective-permute-start | bytes 798728 | tf_op jit(solution)/shard_map/ppermute | solution.py:18
  21.5 5.8 %collective-permute-start.4 = (f32[520,128]{1,0:T(8,128)S(1)}, f32[520,128]{1,0:T(8,128)S(1)}, u32[]{:S(2)}, u32[]{:S(2)}) collective-permute-start(f32[520,128]{1,0:T(8,128)S(1)} %collective-permute-done.3.refs_4_), channel_id=1, source_target_pairs={{0,2},{2,0},{4,6},{6,4},{8,10},{10,8},{12,14},{14,12},{1,3},{3,1},... | collective-permute-start | bytes 798728 | tf_op jit(solution)/shard_map/ppermute | solution.py:18
  27.2 1.5 %collective-permute-start.6 = (f32[520,128]{1,0:T(8,128)S(1)}, f32[520,128]{1,0:T(8,128)S(1)}, u32[]{:S(2)}, u32[]{:S(2)}) collective-permute-start(f32[520,128]{1,0:T(8,128)S(1)} %collective-permute-done.5.refs_6_), channel_id=1, source_target_pairs={{0,2},{2,0},{4,6},{6,4},{8,10},{10,8},{12,14},{14,12},{1,3},{3,1},... | collective-permute-start | bytes 798728 | tf_op jit(solution)/shard_map/ppermute | solution.py:18
  38.0 9.2 %collective-permute-start.9 = (f32[1,2,32,8,128]{4,3,2,1,0:T(8,128)S(1)}, f32[1,2,32,8,128]{4,3,2,1,0:T(8,128)S(1)}, u32[]{:S(2)}, u32[]{:S(2)}) collective-permute-start(f32[1,2,32,8,128]{4,3,2,1,0:T(8,128)S(1)} %get-tuple-element.39), channel_id=1, source_target_pairs={{0,16},{16,0},{1,17},{17,1},{2,18},{18,2},{3,19},{19,3},{4,20},{20... | collective-permute-start | bytes 786440 | tf_op jit(solution)/shard_map/ppermute | solution.py:18
  39.6 13.2 %collective-permute-start.8 = (f32[1,2,32,8,128]{4,3,2,1,0:T(8,128)S(1)}, f32[1,2,32,8,128]{4,3,2,1,0:T(8,128)S(1)}, u32[]{:S(2)}, u32[]{:S(2)}) collective-permute-start(f32[1,2,32,8,128]{4,3,2,1,0:T(8,128)S(1)} %get-tuple-element.36), channel_id=1, source_target_pairs={{0,16},{16,0},{1,17},{17,1},{2,18},{18,2},{3,19},{19,3},{4,20},{20... | collective-permute-start | bytes 786440 | tf_op jit(solution)/shard_map/ppermute | solution.py:18
  40.1 18.4 %collective-permute-start.11 = (f32[1,2,32,8,128]{4,3,2,1,0:T(8,128)S(1)}, f32[1,2,32,8,128]{4,3,2,1,0:T(8,128)S(1)}, u32[]{:S(2)}, u32[]{:S(2)}) collective-permute-start(f32[1,2,32,8,128]{4,3,2,1,0:T(8,128)S(1)} %get-tuple-element.42), channel_id=1, source_target_pairs={{0,16},{16,0},{1,17},{17,1},{2,18},{18,2},{3,19},{19,3},{4,20},{20... | collective-permute-start | bytes 786440 | tf_op jit(solution)/shard_map/ppermute | solution.py:18
  41.7 33.7 %collective-permute-start.13 = (f32[1,2,32,8,128]{4,3,2,1,0:T(8,128)S(1)}, f32[1,2,32,8,128]{4,3,2,1,0:T(8,128)S(1)}, u32[]{:S(2)}, u32[]{:S(2)}) collective-permute-start(f32[1,2,32,8,128]{4,3,2,1,0:T(8,128)S(1)} %get-tuple-element.47), channel_id=1, source_target_pairs={{0,16},{16,0},{1,17},{17,1},{2,18},{18,2},{3,19},{19,3},{4,20},{20... | collective-permute-start | bytes 786440 | tf_op jit(solution)/shard_map/ppermute | solution.py:18
  47.3 26.6 %collective-permute-start.10 = (f32[2,32,8,128]{3,2,1,0:T(8,128)S(1)}, f32[2,32,8,128]{3,2,1,0:T(8,128)S(1)}, u32[]{:S(2)}, u32[]{:S(2)}) collective-permute-start(f32[2,32,8,128]{3,2,1,0:T(8,128)S(1)} %add_bitcast_fusion.7), channel_id=1, source_target_pairs={{0,8},{2,10},{4,12},{6,14},{8,0},{10,2},{12,4},{14,6},{1,9},{3,11}... | collective-permute-start | bytes 786440 | tf_op jit(solution)/shard_map/ppermute | solution.py:18
  52.9 24.1 %collective-permute-start.12 = (f32[2,32,8,128]{3,2,1,0:T(8,128)S(1)}, f32[2,32,8,128]{3,2,1,0:T(8,128)S(1)}, u32[]{:S(2)}, u32[]{:S(2)}) collective-permute-start(f32[2,32,8,128]{3,2,1,0:T(8,128)S(1)} %add_bitcast_fusion.6), channel_id=1, source_target_pairs={{0,10},{2,8},{4,14},{6,12},{8,2},{10,0},{12,6},{14,4},{1,11},{3,9}... | collective-permute-start | bytes 786440 | tf_op jit(solution)/shard_map/ppermute | solution.py:18
  54.4 23.9 %collective-permute-start.16 = (f32[1,2,32,8,128]{4,3,2,1,0:T(8,128)S(1)}, f32[1,2,32,8,128]{4,3,2,1,0:T(8,128)S(1)}, u32[]{:S(2)}, u32[]{:S(2)}) collective-permute-start(f32[1,2,32,8,128]{4,3,2,1,0:T(8,128)S(1)} %get-tuple-element.54), channel_id=1, source_target_pairs={{0,16},{16,0},{1,17},{17,1},{2,18},{18,2},{3,19},{19,3},{4,20},{20... | collective-permute-start | bytes 786440 | tf_op jit(solution)/shard_map/ppermute | solution.py:18
  58.5 21.9 %collective-permute-start.14 = (f32[2,32,8,128]{3,2,1,0:T(8,128)S(1)}, f32[2,32,8,128]{3,2,1,0:T(8,128)S(1)}, u32[]{:S(2)}, u32[]{:S(2)}) collective-permute-start(f32[2,32,8,128]{3,2,1,0:T(8,128)S(1)} %add_bitcast_fusion.5), channel_id=1, source_target_pairs={{0,12},{2,14},{4,8},{6,10},{8,4},{10,6},{12,0},{14,2},{1,13},{3,15... | collective-permute-start | bytes 786440 | tf_op jit(solution)/shard_map/ppermute | solution.py:18
  73.8 7.2 %collective-permute-start.18 = (f32[1,2,32,8,128]{4,3,2,1,0:T(8,128)S(1)}, f32[1,2,32,8,128]{4,3,2,1,0:T(8,128)S(1)}, u32[]{:S(2)}, u32[]{:S(2)}) collective-permute-start(f32[1,2,32,8,128]{4,3,2,1,0:T(8,128)S(1)} %get-tuple-element.56), channel_id=1, source_target_pairs={{0,16},{16,0},{1,17},{17,1},{2,18},{18,2},{3,19},{19,3},{4,20},{20... | collective-permute-start | bytes 786440 | tf_op jit(solution)/shard_map/ppermute | solution.py:18
  75.4 17.8 %collective-permute-start.15 = (f32[2,32,8,128]{3,2,1,0:T(8,128)S(1)}, f32[2,32,8,128]{3,2,1,0:T(8,128)S(1)}, u32[]{:S(2)}, u32[]{:S(2)}) collective-permute-start(f32[2,32,8,128]{3,2,1,0:T(8,128)S(1)} %add_bitcast_fusion.4), channel_id=1, source_target_pairs={{0,14},{2,12},{4,10},{6,8},{8,6},{10,4},{12,2},{14,0},{1,15},{3,13... | collective-permute-start | bytes 786440 | tf_op jit(solution)/shard_map/ppermute | solution.py:18
  77.0 14.0 %collective-permute-start.20 = (f32[1,2,32,8,128]{4,3,2,1,0:T(8,128)S(1)}, f32[1,2,32,8,128]{4,3,2,1,0:T(8,128)S(1)}, u32[]{:S(2)}, u32[]{:S(2)}) collective-permute-start(f32[1,2,32,8,128]{4,3,2,1,0:T(8,128)S(1)} %get-tuple-element.58), channel_id=1, source_target_pairs={{0,16},{16,0},{1,17},{17,1},{2,18},{18,2},{3,19},{19,3},{4,20},{20... | collective-permute-start | bytes 786440 | tf_op jit(solution)/shard_map/ppermute | solution.py:18
  78.3 14.8 %collective-permute-start.17 = (f32[2,32,8,128]{3,2,1,0:T(8,128)S(1)}, f32[2,32,8,128]{3,2,1,0:T(8,128)S(1)}, u32[]{:S(2)}, u32[]{:S(2)}) collective-permute-start(f32[2,32,8,128]{3,2,1,0:T(8,128)S(1)} %add_bitcast_fusion.3), channel_id=1, source_target_pairs={{0,4},{2,6},{4,0},{6,2},{8,12},{10,14},{12,8},{14,10},{1,5},{3,7},... | collective-permute-start | bytes 786440 | tf_op jit(solution)/shard_map/ppermute | solution.py:18
  80.4 12.7 %collective-permute-start.22 = (f32[1,2,32,8,128]{4,3,2,1,0:T(8,128)S(1)}, f32[1,2,32,8,128]{4,3,2,1,0:T(8,128)S(1)}, u32[]{:S(2)}, u32[]{:S(2)}) collective-permute-start(f32[1,2,32,8,128]{4,3,2,1,0:T(8,128)S(1)} %get-tuple-element.60), channel_id=1, source_target_pairs={{0,16},{16,0},{1,17},{17,1},{2,18},{18,2},{3,19},{19,3},{4,20},{20... | collective-permute-start | bytes 786440 | tf_op jit(solution)/shard_map/ppermute | solution.py:18
  81.1 15.3 %collective-permute-start.19 = (f32[2,32,8,128]{3,2,1,0:T(8,128)S(1)}, f32[2,32,8,128]{3,2,1,0:T(8,128)S(1)}, u32[]{:S(2)}, u32[]{:S(2)}) collective-permute-start(f32[2,32,8,128]{3,2,1,0:T(8,128)S(1)} %add_bitcast_fusion.2), channel_id=1, source_target_pairs={{0,6},{2,4},{4,2},{6,0},{8,14},{10,12},{12,10},{14,8},{1,7},{3,5},... | collective-permute-start | bytes 786440 | tf_op jit(solution)/shard_map/ppermute | solution.py:18
  91.1 5.3 %collective-permute-start.21 = (f32[2,32,8,128]{3,2,1,0:T(8,128)S(1)}, f32[2,32,8,128]{3,2,1,0:T(8,128)S(1)}, u32[]{:S(2)}, u32[]{:S(2)}) collective-permute-start(f32[2,32,8,128]{3,2,1,0:T(8,128)S(1)} %add_bitcast_fusion.1), channel_id=1, source_target_pairs={{0,2},{2,0},{4,6},{6,4},{8,10},{10,8},{12,14},{14,12},{1,3},{3,1},... | collective-permute-start | bytes 786440 | tf_op jit(solution)/shard_map/ppermute | solution.py:18

commit v3 on v2

--- a/solution.py
+++ b/solution.py
@@ -10,8 +10,10 @@
 CAP = 16
 LANES = 128
 MIB = 2**20
-LAG_Y = 4
-LAG_Z = 5
+
+
+def waits_of(at):
+    return at - 4 if at >= 4 else None, 0 if at == 4 else at - 5 if at >= 6 else None
 
 
 def swap(block, axis, mask):
@@ -126,7 +128,7 @@
 
     for m in range(n_row):
 
-        @pl.loop(0, panels)
+        @pl.loop(0, panels, unroll=True)
         def _(kk, m=m):
             a = a_refs[m][pl.ds(pl.multiple_of(kk * half + many * first, 8), rows), :]
             turned = pltpu.roll(a, block, 1)
@@ -140,7 +142,7 @@
 
     for m in range(n_col):
 
-        @pl.loop(0, sets * panels)
+        @pl.loop(0, sets * panels, unroll=True)
         def _(i, m=m):
             b = b_refs[m][pl.ds(pl.multiple_of(i * block, block), block), :]
             high = b.astype(jnp.bfloat16)
@@ -179,7 +181,7 @@
 
     multiply(0, 0)
 
-    @pl.loop(0, n_row)
+    @pl.loop(0, n_row, unroll=True)
     def _(m):
         for kk in range(panels):
             if kk + 1 < panels:
@@ -309,10 +311,11 @@
     own, gone = products(first, last, [[m] for m in order], table)
     others, pieces = [], {}
     for at, m in enumerate(order):
-        if at >= LAG_Y:
-            gone[at], others[at - LAG_Y] = lax.optimization_barrier((gone[at], others[at - LAG_Y]))
-        if at >= LAG_Z:
-            key = order[at - LAG_Z], first
+        layer_done, row_done = waits_of(at)
+        if layer_done is not None:
+            gone[at], others[layer_done] = lax.optimization_barrier((gone[at], others[layer_done]))
+        if row_done is not None:
+            key = order[row_done], first
             gone[at], pieces[key] = lax.optimization_barrier((gone[at], pieces[key]))
         others.append(swap(gone[at], "layer", 1))
         total = own[at][0] + others[at][0]

time: 99.8 us -> 97.7 us (0.979); the launches traced: 97.8 us -> 97.3 us
  waiting for transfers between devices: 40.9 us -> 43.1 us
  Pallas kernels: 11 us -> 8.97 us
    ppermute x23, waiting for transfers between devices: 40.9 us -> 43.1 us  [swap(): lax.ppermute(block, axis, [(i, i ^ mask) for i in range(lax.axis_size(axi...]
    pallas_call x1, Pallas kernels: 9.24 us -> 7.18 us  [products(): pl.pallas_call(functools.partial(product_kernel, n_row, n_col, panels, se...]
  transfers between devices with their start and end apart: 23 -> 23, of which waited for: 9 -> 10; matrix products, arithmetic and copies ran while one was open for 1% -> 1% of each run, Pallas kernels for 0% -> 0%
where the time goes in v3:
time: 97.7 us; the launch traced here: 97.3 us
  waiting for transfers between devices  43.1 us (44%)
  starting transfers between devices  42 us (43%)
  Pallas kernels  8.97 us (9%)
  local copies, waits for them, and re-layouts  2.05 us (2%)
  other arithmetic  1.07 us (1%)
    ppermute x23, waiting for transfers between devices, swap(): lax.ppermute(block, axis, [(i, i ^ mask) for i in range(lax.axis_size(axi...  43.1 us
    ppermute x23, starting transfers between devices, swap(): lax.ppermute(block, axis, [(i, i ^ mask) for i in range(lax.axis_size(axi...  42 us
    pallas_call x1, Pallas kernels, products(): pl.pallas_call(functools.partial(product_kernel, n_row, n_col, panels, se...  7.18 us
    unnamed x12, local copies, waits for them, and re-layouts  1.97 us
  transfers between devices with their start and end apart: 23, of which 10 were waited for; matrix products, arithmetic and copies ran while one was open for 1% of the time, Pallas kernels for 0%

profile of v3, /device:TPU:0, one launch (start us, length us, event | category | flops | bytes accessed | tf_op | source)
XLA Modules:
  0.0 97.3 jit_solution(6561564533265652263)
XLA Ops:
  0.0 1.3 %copy-done = f32[1,1,1,4,2,64,512]{6,5,4,3,2,1,0:T(8,128)S(1)} copy-done((f32[1,1,1,4,2,64,512]{6,5,4,3,2,1,0:T(8,128)S(1)}, f32[1,1,1,4,2,64,512]{6,5,4,3,2,1,0:T(8,128)}, u32[]{:S(2)}) %copy-start) | copy-done | bytes 1048600
  1.3 0.7 copy-done.2
  2.1 3.0 %collective-permute-start.7 = (f32[520,512]{1,0:T(8,128)S(1)}, f32[520,512]{1,0:T(8,128)S(1)}, u32[]{:S(2)}, u32[]{:S(2)}) collective-permute-start(f32[520,512]{1,0:T(8,128)S(1)} %shard_map.65.refs_8_), channel_id=1, source_target_pairs={{0,1},{1,0},{2,3},{3,2},{4,5},{5,4},{6,7},{7,6},{8,9},{9,8},{10,11... | collective-permute-start | bytes 3194888 | tf_op jit(solution)/shard_map/ppermute | solution.py:20
  5.4 2.7 %collective-permute-start.3 = (f32[520,128]{1,0:T(8,128)S(1)}, f32[520,128]{1,0:T(8,128)S(1)}, u32[]{:S(2)}, u32[]{:S(2)}) collective-permute-start(f32[520,128]{1,0:T(8,128)S(1)} %shard_map.64.refs_0_), channel_id=1, source_target_pairs={{0,8},{2,10},{4,12},{6,14},{8,0},{10,2},{12,4},{14,6},{1,9},{3,11}... | collective-permute-start | bytes 798728 | tf_op jit(solution)/shard_map/ppermute | solution.py:20
  8.1 1.6 %collective-permute-start = (f32[520,128]{1,0:T(8,128)S(1)}, f32[520,128]{1,0:T(8,128)S(1)}, u32[]{:S(2)}, u32[]{:S(2)}) collective-permute-start(f32[520,128]{1,0:T(8,128)S(1)} %shard_map.64.refs_0_), channel_id=1, source_target_pairs={{0,4},{2,6},{4,0},{6,2},{8,12},{10,14},{12,8},{14,10},{1,5},{3,7},... | collective-permute-start | bytes 798728 | tf_op jit(solution)/shard_map/ppermute | solution.py:20
  9.8 10.2 %collective-permute-done.3.refs_4_ = f32[520,128]{1,0:T(8,128)S(1)} collective-permute-done((f32[520,128]{1,0:T(8,128)S(1)}, f32[520,128]{1,0:T(8,128)S(1)}, u32[]{:S(2)}, u32[]{:S(2)}) %collective-permute-start.3) | collective-permute-done | bytes 266272 | tf_op jit(solution)/shard_map/ppermute | solution.py:20
  20.0 0.6 collective-permute-start.5
  20.6 0.6 select_reduce_fusion
  21.5 0.5 collective-permute-start.4
  22.0 5.2 %collective-permute-done.5.refs_6_ = f32[520,128]{1,0:T(8,128)S(1)} collective-permute-done((f32[520,128]{1,0:T(8,128)S(1)}, f32[520,128]{1,0:T(8,128)S(1)}, u32[]{:S(2)}, u32[]{:S(2)}) %collective-permute-start.5) | collective-permute-done | bytes 266272 | tf_op jit(solution)/shard_map/ppermute | solution.py:20
  27.2 1.5 %collective-permute-done.6.refs_7_ = f32[520,128]{1,0:T(8,128)S(1)} collective-permute-done((f32[520,128]{1,0:T(8,128)S(1)}, f32[520,128]{1,0:T(8,128)S(1)}, u32[]{:S(2)}, u32[]{:S(2)}) %collective-permute-start.6) | collective-permute-done | bytes 266272 | tf_op jit(solution)/shard_map/ppermute | solution.py:20
  28.8 7.2 %shard_map.66 = (f32[1,2,32,8,128]{4,3,2,1,0:T(8,128)S(1)}, f32[1,2,32,8,128]{4,3,2,1,0:T(8,128)S(1)}, f32[1,2,32,8,128]{4,3,2,1,0:T(8,128)S(1)}, f32[1,2,32,8,1...) custom-call(s32[64,128]{1,0:T(8,128)S(1)} %pad.4.table_ref, ...), custom_call_target="tpu_custom_call" | custom-call | flops 2147483648 | bytes 8454144 | tf_op jit(solution)/shard_map/pallas_call | solution.py:285
  36.0 1.7 %collective-permute-start.8 = (f32[1,2,32,8,128]{4,3,2,1,0:T(8,128)S(1)}, f32[1,2,32,8,128]{4,3,2,1,0:T(8,128)S(1)}, u32[]{:S(2)}, u32[]{:S(2)}) collective-permute-start(f32[1,2,32,8,128]{4,3,2,1,0:T(8,128)S(1)} %get-tuple-element.36), channel_id=1, source_target_pairs={{0,16},{16,0},{1,17},{17,1},{2,18},{18,2},{3,19},{19,3},{4,20},{20... | collective-permute-start | bytes 786440 | tf_op jit(solution)/shard_map/ppermute | solution.py:20
  37.6 0.4 collective-permute-start.11
  38.0 1.6 %collective-permute-start.10 = (f32[1,2,32,8,128]{4,3,2,1,0:T(8,128)S(1)}, f32[1,2,32,8,128]{4,3,2,1,0:T(8,128)S(1)}, u32[]{:S(2)}, u32[]{:S(2)}) collective-permute-start(f32[1,2,32,8,128]{4,3,2,1,0:T(8,128)S(1)} %get-tuple-element.41), channel_id=1, source_target_pairs={{0,16},{16,0},{1,17},{17,1},{2,18},{18,2},{3,19},{19,3},{4,20},{20... | collective-permute-start | bytes 786440 | tf_op jit(solution)/shard_map/ppermute | solution.py:20
  39.7 0.4 collective-permute-start.13
  40.1 5.1 %collective-permute-done.8 = f32[1,2,32,8,128]{4,3,2,1,0:T(8,128)S(1)} collective-permute-done((f32[1,2,32,8,128]{4,3,2,1,0:T(8,128)S(1)}, f32[1,2,32,8,128]{4,3,2,1,0:T(8,128)S(1)}, u32[]{:S(2)}, u32[]{:S(2)}) %collective-permute-start.8) | collective-permute-done | bytes 262176 | tf_op jit(solution)/shard_map/ppermute | solution.py:20
  45.2 3.4 %collective-permute-start.9 = (f32[2,32,8,128]{3,2,1,0:T(8,128)S(1)}, f32[2,32,8,128]{3,2,1,0:T(8,128)S(1)}, u32[]{:S(2)}, u32[]{:S(2)}) collective-permute-start(f32[2,32,8,128]{3,2,1,0:T(8,128)S(1)} %add_bitcast_fusion.7), channel_id=1, source_target_pairs={{0,8},{2,10},{4,12},{6,14},{8,0},{10,2},{12,4},{14,6},{1,9},{3,11}... | collective-permute-start | bytes 786440 | tf_op jit(solution)/shard_map/ppermute | solution.py:20
  48.6 2.2 %collective-permute-done.11 = f32[1,2,32,8,128]{4,3,2,1,0:T(8,128)S(1)} collective-permute-done((f32[1,2,32,8,128]{4,3,2,1,0:T(8,128)S(1)}, f32[1,2,32,8,128]{4,3,2,1,0:T(8,128)S(1)}, u32[]{:S(2)}, u32[]{:S(2)}) %collective-permute-start.11) | collective-permute-done | bytes 262176 | tf_op jit(solution)/shard_map/ppermute | solution.py:20
  50.8 1.6 %collective-permute-start.18 = (f32[1,2,32,8,128]{4,3,2,1,0:T(8,128)S(1)}, f32[1,2,32,8,128]{4,3,2,1,0:T(8,128)S(1)}, u32[]{:S(2)}, u32[]{:S(2)}) collective-permute-start(f32[1,2,32,8,128]{4,3,2,1,0:T(8,128)S(1)} %get-tuple-element.56), channel_id=1, source_target_pairs={{0,16},{16,0},{1,17},{17,1},{2,18},{18,2},{3,19},{19,3},{4,20},{20... | collective-permute-start | bytes 786440 | tf_op jit(solution)/shard_map/ppermute | solution.py:20
  52.4 1.2 %collective-permute-start.12 = (f32[2,32,8,128]{3,2,1,0:T(8,128)S(1)}, f32[2,32,8,128]{3,2,1,0:T(8,128)S(1)}, u32[]{:S(2)}, u32[]{:S(2)}) collective-permute-start(f32[2,32,8,128]{3,2,1,0:T(8,128)S(1)} %add_bitcast_fusion.6), channel_id=1, source_target_pairs={{0,10},{2,8},{4,14},{6,12},{8,2},{10,0},{12,6},{14,4},{1,11},{3,9}... | collective-permute-start | bytes 786440 | tf_op jit(solution)/shard_map/ppermute | solution.py:20
  53.7 2.7 %collective-permute-done.10 = f32[1,2,32,8,128]{4,3,2,1,0:T(8,128)S(1)} collective-permute-done((f32[1,2,32,8,128]{4,3,2,1,0:T(8,128)S(1)}, f32[1,2,32,8,128]{4,3,2,1,0:T(8,128)S(1)}, u32[]{:S(2)}, u32[]{:S(2)}) %collective-permute-start.10) | collective-permute-done | bytes 262176 | tf_op jit(solution)/shard_map/ppermute | solution.py:20
  56.4 4.6 %collective-permute-start.14 = (f32[2,32,8,128]{3,2,1,0:T(8,128)S(1)}, f32[2,32,8,128]{3,2,1,0:T(8,128)S(1)}, u32[]{:S(2)}, u32[]{:S(2)}) collective-permute-start(f32[2,32,8,128]{3,2,1,0:T(8,128)S(1)} %add_bitcast_fusion.5), channel_id=1, source_target_pairs={{0,12},{2,14},{4,8},{6,10},{8,4},{10,6},{12,0},{14,2},{1,13},{3,15... | collective-permute-start | bytes 786440 | tf_op jit(solution)/shard_map/ppermute | solution.py:20
  61.1 10.8 %collective-permute-done.9.refs_0_ = f32[2,32,8,128]{3,2,1,0:T(8,128)S(1)} collective-permute-done((f32[2,32,8,128]{3,2,1,0:T(8,128)S(1)}, f32[2,32,8,128]{3,2,1,0:T(8,128)S(1)}, u32[]{:S(2)}, u32[]{:S(2)}) %collective-permute-start.9) | collective-permute-done | bytes 262176 | tf_op jit(solution)/shard_map/ppermute | solution.py:20
  71.9 1.3 %collective-permute-start.16 = (f32[1,2,32,8,128]{4,3,2,1,0:T(8,128)S(1)}, f32[1,2,32,8,128]{4,3,2,1,0:T(8,128)S(1)}, u32[]{:S(2)}, u32[]{:S(2)}) collective-permute-start(f32[1,2,32,8,128]{4,3,2,1,0:T(8,128)S(1)} %get-tuple-element.53), channel_id=1, source_target_pairs={{0,16},{16,0},{1,17},{17,1},{2,18},{18,2},{3,19},{19,3},{4,20},{20... | collective-permute-start | bytes 786440 | tf_op jit(solution)/shard_map/ppermute | solution.py:20
  73.2 1.8 %collective-permute-start.15 = (f32[2,32,8,128]{3,2,1,0:T(8,128)S(1)}, f32[2,32,8,128]{3,2,1,0:T(8,128)S(1)}, u32[]{:S(2)}, u32[]{:S(2)}) collective-permute-start(f32[2,32,8,128]{3,2,1,0:T(8,128)S(1)} %add_bitcast_fusion.4), channel_id=1, source_target_pairs={{0,14},{2,12},{4,10},{6,8},{8,6},{10,4},{12,2},{14,0},{1,15},{3,13... | collective-permute-start | bytes 786440 | tf_op jit(solution)/shard_map/ppermute | solution.py:20
  75.2 1.3 %collective-permute-start.20 = (f32[1,2,32,8,128]{4,3,2,1,0:T(8,128)S(1)}, f32[1,2,32,8,128]{4,3,2,1,0:T(8,128)S(1)}, u32[]{:S(2)}, u32[]{:S(2)}) collective-permute-start(f32[1,2,32,8,128]{4,3,2,1,0:T(8,128)S(1)} %get-tuple-element.58), channel_id=1, source_target_pairs={{0,16},{16,0},{1,17},{17,1},{2,18},{18,2},{3,19},{19,3},{4,20},{20... | collective-permute-start | bytes 786440 | tf_op jit(solution)/shard_map/ppermute | solution.py:20
  76.5 1.3 %collective-permute-start.19 = (f32[2,32,8,128]{3,2,1,0:T(8,128)S(1)}, f32[2,32,8,128]{3,2,1,0:T(8,128)S(1)}, u32[]{:S(2)}, u32[]{:S(2)}) collective-permute-start(f32[2,32,8,128]{3,2,1,0:T(8,128)S(1)} %add_bitcast_fusion.2), channel_id=1, source_target_pairs={{0,6},{2,4},{4,2},{6,0},{8,14},{10,12},{12,10},{14,8},{1,7},{3,5},... | collective-permute-start | bytes 786440 | tf_op jit(solution)/shard_map/ppermute | solution.py:20
  77.8 0.7 collective-permute-start.22
  78.6 12.2 %collective-permute-start.17 = (f32[2,32,8,128]{3,2,1,0:T(8,128)S(1)}, f32[2,32,8,128]{3,2,1,0:T(8,128)S(1)}, u32[]{:S(2)}, u32[]{:S(2)}) collective-permute-start(f32[2,32,8,128]{3,2,1,0:T(8,128)S(1)} %add_bitcast_fusion.3), channel_id=1, source_target_pairs={{0,4},{2,6},{4,0},{6,2},{8,12},{10,14},{12,8},{14,10},{1,5},{3,7},... | collective-permute-start | bytes 786440 | tf_op jit(solution)/shard_map/ppermute | solution.py:20
  90.9 5.0 %collective-permute-done.17.refs_4_ = f32[2,32,8,128]{3,2,1,0:T(8,128)S(1)} collective-permute-done((f32[2,32,8,128]{3,2,1,0:T(8,128)S(1)}, f32[2,32,8,128]{3,2,1,0:T(8,128)S(1)}, u32[]{:S(2)}, u32[]{:S(2)}) %collective-permute-start.17) | collective-permute-done | bytes 262176 | tf_op jit(solution)/shard_map/ppermute | solution.py:20
  96.0 1.4 %shard_map.67 = f32[16,32,8,128]{3,2,1,0:T(8,128)} custom-call(f32[2,32,8,128]{3,2,1,0:T(8,128)S(1)} %collective-permute-done.9.refs_0_, f32[2,32,8,128]{3,2,1,0:T(8,128)S(1)} %collective-permute-done.12.refs_1_, f32[2,32,8,128]{3,2,1,0:T(8,128)S(1)} %collective-permute-done.14.refs_2_, f32[2,32,8,128]{3,2,1,0:T(8,128)S(1)} %collective-permute-done.15.refs_3_, ...), custom_call_target="tpu_custom_call" | custom-call | tf_op jit(solution)/shard_map/pallas_call | solution.py:324
  (44 shorter events, 1.4 us)
Async XLA Ops:
  0.0 5.1 %copy-start.3 = (s32[1,1,1,2,8]{4,3,2,1,0:T(2,128)S(1)}, s32[1,1,1,2,8]{4,3,2,1,0:T(2,128)}, u32[]{:S(2)}) copy-start(s32[1,1,1,2,8]{4,3,2,1,0:T(2,128)} %param.7) | copy-start | bytes 196
  0.0 9.6 %copy-start.4 = (s32[1,256,1]{1,2,0:T(1,128)S(1)}, s32[1,256,1]{1,2,0:T(1,128)}, u32[]{:S(2)}) copy-start(s32[1,256,1]{1,2,0:T(1,128)} %param.11) | copy-start | bytes 3076
  0.0 20.6 %copy-start.5 = (s32[1,1,256]{2,1,0:T(1,128)S(1)}, s32[1,1,256]{2,1,0:T(1,128)}, u32[]{:S(2)}) copy-start(s32[1,1,256]{2,1,0:T(1,128)} %param.10) | copy-start | bytes 3076
  0.0 1.3 %copy-start = (f32[1,1,1,4,2,64,512]{6,5,4,3,2,1,0:T(8,128)S(1)}, f32[1,1,1,4,2,64,512]{6,5,4,3,2,1,0:T(8,128)}, u32[]{:S(2)}) copy-start(f32[1,1,1,4,2,64,512]{6,5,4,3,2,1,0:T(8,128)} %param.8) | copy-start | bytes 3145732
  1.3 0.7 copy-start.2
  2.0 3.1 %copy-start.1 = (f32[1,1,1,2,64,512]{5,4,3,2,1,0:T(8,128)S(1)}, f32[1,1,1,2,64,512]{5,4,3,2,1,0:T(8,128)}, u32[]{:S(2)}) copy-start(f32[1,1,1,2,64,512]{5,4,3,2,1,0:T(8,128)} %param.6) | copy-start | bytes 786436
  2.1 26.7 %collective-permute-start.7 = (f32[520,512]{1,0:T(8,128)S(1)}, f32[520,512]{1,0:T(8,128)S(1)}, u32[]{:S(2)}, u32[]{:S(2)}) collective-permute-start(f32[520,512]{1,0:T(8,128)S(1)} %shard_map.65.refs_8_), channel_id=1, source_target_pairs={{0,1},{1,0},{2,3},{3,2},{4,5},{5,4},{6,7},{7,6},{8,9},{9,8},{10,11... | collective-permute-start | bytes 3194888 | tf_op jit(solution)/shard_map/ppermute | solution.py:20
  5.4 14.6 %collective-permute-start.3 = (f32[520,128]{1,0:T(8,128)S(1)}, f32[520,128]{1,0:T(8,128)S(1)}, u32[]{:S(2)}, u32[]{:S(2)}) collective-permute-start(f32[520,128]{1,0:T(8,128)S(1)} %shard_map.64.refs_0_), channel_id=1, source_target_pairs={{0,8},{2,10},{4,12},{6,14},{8,0},{10,2},{12,4},{14,6},{1,9},{3,11}... | collective-permute-start | bytes 798728 | tf_op jit(solution)/shard_map/ppermute | solution.py:20
  8.1 19.2 %collective-permute-start.1 = (f32[520,128]{1,0:T(8,128)S(1)}, f32[520,128]{1,0:T(8,128)S(1)}, u32[]{:S(2)}, u32[]{:S(2)}) collective-permute-start(f32[520,128]{1,0:T(8,128)S(1)} %shard_map.64.refs_0_), channel_id=1, source_target_pairs={{0,2},{2,0},{4,6},{6,4},{8,10},{10,8},{12,14},{14,12},{1,3},{3,1},... | collective-permute-start | bytes 798728 | tf_op jit(solution)/shard_map/ppermute | solution.py:20
  8.1 13.4 %collective-permute-start = (f32[520,128]{1,0:T(8,128)S(1)}, f32[520,128]{1,0:T(8,128)S(1)}, u32[]{:S(2)}, u32[]{:S(2)}) collective-permute-start(f32[520,128]{1,0:T(8,128)S(1)} %shard_map.64.refs_0_), channel_id=1, source_target_pairs={{0,4},{2,6},{4,0},{6,2},{8,12},{10,14},{12,8},{14,10},{1,5},{3,7},... | collective-permute-start | bytes 798728 | tf_op jit(solution)/shard_map/ppermute | solution.py:20
  20.0 7.2 %collective-permute-start.5 = (f32[520,128]{1,0:T(8,128)S(1)}, f32[520,128]{1,0:T(8,128)S(1)}, u32[]{:S(2)}, u32[]{:S(2)}) collective-permute-start(f32[520,128]{1,0:T(8,128)S(1)} %collective-permute-done.3.refs_4_), channel_id=1, source_target_pairs={{0,4},{2,6},{4,0},{6,2},{8,12},{10,14},{12,8},{14,10},{1,5},{3,7},... | collective-permute-start | bytes 798728 | tf_op jit(solution)/shard_map/ppermute | solution.py:20
  21.5 5.8 %collective-permute-start.2 = (f32[520,128]{1,0:T(8,128)S(1)}, f32[520,128]{1,0:T(8,128)S(1)}, u32[]{:S(2)}, u32[]{:S(2)}) collective-permute-start(f32[520,128]{1,0:T(8,128)S(1)} %collective-permute-done.refs_2_), channel_id=1, source_target_pairs={{0,2},{2,0},{4,6},{6,4},{8,10},{10,8},{12,14},{14,12},{1,3},{3,1},... | collective-permute-start | bytes 798728 | tf_op jit(solution)/shard_map/ppermute | solution.py:20
  21.5 5.8 %collective-permute-start.4 = (f32[520,128]{1,0:T(8,128)S(1)}, f32[520,128]{1,0:T(8,128)S(1)}, u32[]{:S(2)}, u32[]{:S(2)}) collective-permute-start(f32[520,128]{1,0:T(8,128)S(1)} %collective-permute-done.3.refs_4_), channel_id=1, source_target_pairs={{0,2},{2,0},{4,6},{6,4},{8,10},{10,8},{12,14},{14,12},{1,3},{3,1},... | collective-permute-start | bytes 798728 | tf_op jit(solution)/shard_map/ppermute | solution.py:20
  27.2 1.5 %collective-permute-start.6 = (f32[520,128]{1,0:T(8,128)S(1)}, f32[520,128]{1,0:T(8,128)S(1)}, u32[]{:S(2)}, u32[]{:S(2)}) collective-permute-start(f32[520,128]{1,0:T(8,128)S(1)} %collective-permute-done.5.refs_6_), channel_id=1, source_target_pairs={{0,2},{2,0},{4,6},{6,4},{8,10},{10,8},{12,14},{14,12},{1,3},{3,1},... | collective-permute-start | bytes 798728 | tf_op jit(solution)/shard_map/ppermute | solution.py:20
  36.0 9.2 %collective-permute-start.8 = (f32[1,2,32,8,128]{4,3,2,1,0:T(8,128)S(1)}, f32[1,2,32,8,128]{4,3,2,1,0:T(8,128)S(1)}, u32[]{:S(2)}, u32[]{:S(2)}) collective-permute-start(f32[1,2,32,8,128]{4,3,2,1,0:T(8,128)S(1)} %get-tuple-element.36), channel_id=1, source_target_pairs={{0,16},{16,0},{1,17},{17,1},{2,18},{18,2},{3,19},{19,3},{4,20},{20... | collective-permute-start | bytes 786440 | tf_op jit(solution)/shard_map/ppermute | solution.py:20
  37.6 13.1 %collective-permute-start.11 = (f32[1,2,32,8,128]{4,3,2,1,0:T(8,128)S(1)}, f32[1,2,32,8,128]{4,3,2,1,0:T(8,128)S(1)}, u32[]{:S(2)}, u32[]{:S(2)}) collective-permute-start(f32[1,2,32,8,128]{4,3,2,1,0:T(8,128)S(1)} %get-tuple-element.44), channel_id=1, source_target_pairs={{0,16},{16,0},{1,17},{17,1},{2,18},{18,2},{3,19},{19,3},{4,20},{20... | collective-permute-start | bytes 786440 | tf_op jit(solution)/shard_map/ppermute | solution.py:20
  38.0 18.4 %collective-permute-start.10 = (f32[1,2,32,8,128]{4,3,2,1,0:T(8,128)S(1)}, f32[1,2,32,8,128]{4,3,2,1,0:T(8,128)S(1)}, u32[]{:S(2)}, u32[]{:S(2)}) collective-permute-start(f32[1,2,32,8,128]{4,3,2,1,0:T(8,128)S(1)} %get-tuple-element.41), channel_id=1, source_target_pairs={{0,16},{16,0},{1,17},{17,1},{2,18},{18,2},{3,19},{19,3},{4,20},{20... | collective-permute-start | bytes 786440 | tf_op jit(solution)/shard_map/ppermute | solution.py:20
  39.7 33.5 %collective-permute-start.13 = (f32[1,2,32,8,128]{4,3,2,1,0:T(8,128)S(1)}, f32[1,2,32,8,128]{4,3,2,1,0:T(8,128)S(1)}, u32[]{:S(2)}, u32[]{:S(2)}) collective-permute-start(f32[1,2,32,8,128]{4,3,2,1,0:T(8,128)S(1)} %get-tuple-element.47), channel_id=1, source_target_pairs={{0,16},{16,0},{1,17},{17,1},{2,18},{18,2},{3,19},{19,3},{4,20},{20... | collective-permute-start | bytes 786440 | tf_op jit(solution)/shard_map/ppermute | solution.py:20
  45.2 26.7 %collective-permute-start.9 = (f32[2,32,8,128]{3,2,1,0:T(8,128)S(1)}, f32[2,32,8,128]{3,2,1,0:T(8,128)S(1)}, u32[]{:S(2)}, u32[]{:S(2)}) collective-permute-start(f32[2,32,8,128]{3,2,1,0:T(8,128)S(1)} %add_bitcast_fusion.7), channel_id=1, source_target_pairs={{0,8},{2,10},{4,12},{6,14},{8,0},{10,2},{12,4},{14,6},{1,9},{3,11}... | collective-permute-start | bytes 786440 | tf_op jit(solution)/shard_map/ppermute | solution.py:20
  50.8 25.7 %collective-permute-start.18 = (f32[1,2,32,8,128]{4,3,2,1,0:T(8,128)S(1)}, f32[1,2,32,8,128]{4,3,2,1,0:T(8,128)S(1)}, u32[]{:S(2)}, u32[]{:S(2)}) collective-permute-start(f32[1,2,32,8,128]{4,3,2,1,0:T(8,128)S(1)} %get-tuple-element.56), channel_id=1, source_target_pairs={{0,16},{16,0},{1,17},{17,1},{2,18},{18,2},{3,19},{19,3},{4,20},{20... | collective-permute-start | bytes 786440 | tf_op jit(solution)/shard_map/ppermute | solution.py:20
  52.4 22.8 %collective-permute-start.12 = (f32[2,32,8,128]{3,2,1,0:T(8,128)S(1)}, f32[2,32,8,128]{3,2,1,0:T(8,128)S(1)}, u32[]{:S(2)}, u32[]{:S(2)}) collective-permute-start(f32[2,32,8,128]{3,2,1,0:T(8,128)S(1)} %add_bitcast_fusion.6), channel_id=1, source_target_pairs={{0,10},{2,8},{4,14},{6,12},{8,2},{10,0},{12,6},{14,4},{1,11},{3,9}... | collective-permute-start | bytes 786440 | tf_op jit(solution)/shard_map/ppermute | solution.py:20
  56.4 21.4 %collective-permute-start.14 = (f32[2,32,8,128]{3,2,1,0:T(8,128)S(1)}, f32[2,32,8,128]{3,2,1,0:T(8,128)S(1)}, u32[]{:S(2)}, u32[]{:S(2)}) collective-permute-start(f32[2,32,8,128]{3,2,1,0:T(8,128)S(1)} %add_bitcast_fusion.5), channel_id=1, source_target_pairs={{0,12},{2,14},{4,8},{6,10},{8,4},{10,6},{12,0},{14,2},{1,13},{3,15... | collective-permute-start | bytes 786440 | tf_op jit(solution)/shard_map/ppermute | solution.py:20
  71.9 6.7 %collective-permute-start.16 = (f32[1,2,32,8,128]{4,3,2,1,0:T(8,128)S(1)}, f32[1,2,32,8,128]{4,3,2,1,0:T(8,128)S(1)}, u32[]{:S(2)}, u32[]{:S(2)}) collective-permute-start(f32[1,2,32,8,128]{4,3,2,1,0:T(8,128)S(1)} %get-tuple-element.53), channel_id=1, source_target_pairs={{0,16},{16,0},{1,17},{17,1},{2,18},{18,2},{3,19},{19,3},{4,20},{20... | collective-permute-start | bytes 786440 | tf_op jit(solution)/shard_map/ppermute | solution.py:20
  73.2 17.7 %collective-permute-start.15 = (f32[2,32,8,128]{3,2,1,0:T(8,128)S(1)}, f32[2,32,8,128]{3,2,1,0:T(8,128)S(1)}, u32[]{:S(2)}, u32[]{:S(2)}) collective-permute-start(f32[2,32,8,128]{3,2,1,0:T(8,128)S(1)} %add_bitcast_fusion.4), channel_id=1, source_target_pairs={{0,14},{2,12},{4,10},{6,8},{8,6},{10,4},{12,2},{14,0},{1,15},{3,13... | collective-permute-start | bytes 786440 | tf_op jit(solution)/shard_map/ppermute | solution.py:20
  75.2 15.5 %collective-permute-start.20 = (f32[1,2,32,8,128]{4,3,2,1,0:T(8,128)S(1)}, f32[1,2,32,8,128]{4,3,2,1,0:T(8,128)S(1)}, u32[]{:S(2)}, u32[]{:S(2)}) collective-permute-start(f32[1,2,32,8,128]{4,3,2,1,0:T(8,128)S(1)} %get-tuple-element.58), channel_id=1, source_target_pairs={{0,16},{16,0},{1,17},{17,1},{2,18},{18,2},{3,19},{19,3},{4,20},{20... | collective-permute-start | bytes 786440 | tf_op jit(solution)/shard_map/ppermute | solution.py:20
  76.5 14.4 %collective-permute-start.19 = (f32[2,32,8,128]{3,2,1,0:T(8,128)S(1)}, f32[2,32,8,128]{3,2,1,0:T(8,128)S(1)}, u32[]{:S(2)}, u32[]{:S(2)}) collective-permute-start(f32[2,32,8,128]{3,2,1,0:T(8,128)S(1)} %add_bitcast_fusion.2), channel_id=1, source_target_pairs={{0,6},{2,4},{4,2},{6,0},{8,14},{10,12},{12,10},{14,8},{1,7},{3,5},... | collective-permute-start | bytes 786440 | tf_op jit(solution)/shard_map/ppermute | solution.py:20
  77.8 13.1 %collective-permute-start.22 = (f32[1,2,32,8,128]{4,3,2,1,0:T(8,128)S(1)}, f32[1,2,32,8,128]{4,3,2,1,0:T(8,128)S(1)}, u32[]{:S(2)}, u32[]{:S(2)}) collective-permute-start(f32[1,2,32,8,128]{4,3,2,1,0:T(8,128)S(1)} %get-tuple-element.60), channel_id=1, source_target_pairs={{0,16},{16,0},{1,17},{17,1},{2,18},{18,2},{3,19},{19,3},{4,20},{20... | collective-permute-start | bytes 786440 | tf_op jit(solution)/shard_map/ppermute | solution.py:20
  78.6 17.4 %collective-permute-start.17 = (f32[2,32,8,128]{3,2,1,0:T(8,128)S(1)}, f32[2,32,8,128]{3,2,1,0:T(8,128)S(1)}, u32[]{:S(2)}, u32[]{:S(2)}) collective-permute-start(f32[2,32,8,128]{3,2,1,0:T(8,128)S(1)} %add_bitcast_fusion.3), channel_id=1, source_target_pairs={{0,4},{2,6},{4,0},{6,2},{8,12},{10,14},{12,8},{14,10},{1,5},{3,7},... | collective-permute-start | bytes 786440 | tf_op jit(solution)/shard_map/ppermute | solution.py:20
  90.8 5.2 %collective-permute-start.21 = (f32[2,32,8,128]{3,2,1,0:T(8,128)S(1)}, f32[2,32,8,128]{3,2,1,0:T(8,128)S(1)}, u32[]{:S(2)}, u32[]{:S(2)}) collective-permute-start(f32[2,32,8,128]{3,2,1,0:T(8,128)S(1)} %add_bitcast_fusion.1), channel_id=1, source_target_pairs={{0,2},{2,0},{4,6},{6,4},{8,10},{10,8},{12,14},{14,12},{1,3},{3,1},... | collective-permute-start | bytes 786440 | tf_op jit(solution)/shard_map/ppermute | solution.py:20

commit v4 on v3

--- a/solution.py
+++ b/solution.py
@@ -202,15 +202,14 @@
                     out_ref[i, eight, pl.ds(at, 8)] = jnp.swapaxes(jnp.stack(taken), 0, 1)
 
 
-def place_kernel(pieces, *refs):
-    sources, out_ref, sems = refs[: len(pieces)], refs[len(pieces)], refs[len(pieces) + 1]
+def place_kernel(masks, *refs):
+    sources, out_ref, sems = refs[: len(masks)], refs[-2], refs[-1]
     my_row = lax.axis_index("row")
     copies = []
-    for i, (m, first) in enumerate(pieces):
-        size, long = sources[i].shape[:2]
+    for i, m in enumerate(masks):
+        size = sources[i].shape[0]
         at = pl.multiple_of(lax.bitwise_xor(my_row, m) * size, size)
-        target = out_ref.at[pl.ds(at, size), pl.ds(first, long)]
-        copies.append(pltpu.make_async_copy(sources[i], target, sems.at[i]))
+        copies.append(pltpu.make_async_copy(sources[i], out_ref.at[pl.ds(at, size)], sems.at[i]))
     for copy in copies:
         copy.start()
     for copy in copies:
@@ -306,7 +305,7 @@
         )(table, *a_held, *b_held)
         return list(made[: len(groups)]), list(made[len(groups) :])
 
-    order = far + near
+    order = far[:-1] + near[:1] + far[-1:] + near[1:]
     ((first, last),) = parts_of(pair)
     own, gone = products(first, last, [[m] for m in order], table)
     others, pieces = [], {}
@@ -318,17 +317,21 @@
             key = order[row_done], first
             gone[at], pieces[key] = lax.optimization_barrier((gone[at], pieces[key]))
         others.append(swap(gone[at], "layer", 1))
-        total = own[at][0] + others[at][0]
+        total = (own[at] + others[at]).reshape(own[at].shape[1:])
         pieces[m, first] = swap(total, "row", m) if m else total
-    keys = list(pieces)
-    owned = pl.pallas_call(
-        functools.partial(place_kernel, keys),
-        out_shape=jax.ShapeDtypeStruct((n_row * CAP // 8, pair, 8, LANES), jnp.float32),
-        in_specs=[vmem] * len(keys),
-        out_specs=anywhere,
-        scratch_shapes=[pltpu.SemaphoreType.DMA((len(keys),))],
-        compiler_params=room(n_row * CAP * block * block * 4),
-    )(*pieces.values())
+    owned = []
+    for masks in (order[: n_row // 2] + [0], order[n_row // 2 : -1]):
+        placed = pl.pallas_call(
+            functools.partial(place_kernel, masks),
+            out_shape=jax.ShapeDtypeStruct((n_row * CAP // 8, pair, 8, LANES), jnp.float32),
+            in_specs=[vmem] * len(masks) + [anywhere] * len(owned),
+            out_specs=anywhere,
+            input_output_aliases={len(masks): 0} if owned else {},
+            scratch_shapes=[pltpu.SemaphoreType.DMA((len(masks),))],
+            compiler_params=room(len(masks) * CAP * block * block * 4),
+        )(*[pieces[m, first] for m in masks], *owned)
+        owned = [placed]
+    (owned,) = owned
     return owned.transpose(0, 2, 1, 3).reshape(n_row * CAP, block * block)
 
 

time: 97.7 us -> 96.5 us (0.988)
  the two profiles are of different devices: /device:TPU:0 before, /device:TPU:17 now
where the time goes in v4:
time: 96.5 us; the launch traced here: 96.4 us
  waiting for transfers between devices  50.5 us (52%)
  starting transfers between devices  33 us (34%)
  Pallas kernels  9.68 us (10%)
  local copies, waits for them, and re-layouts  2.04 us (2%)
  other arithmetic  1.11 us (1%)
    ppermute x23, waiting for transfers between devices, swap(): lax.ppermute(block, axis, [(i, i ^ mask) for i in range(lax.axis_size(axi...  50.5 us
    ppermute x23, starting transfers between devices, swap(): lax.ppermute(block, axis, [(i, i ^ mask) for i in range(lax.axis_size(axi...  33 us
    pallas_call x1, Pallas kernels, products(): pl.pallas_call(functools.partial(product_kernel, n_row, n_col, panels, se...  7.27 us
    pallas_call x2, Pallas kernels, body(): pl.pallas_call(functools.partial(place_kernel, masks), out_shape=jax.Shap...  2 us
    unnamed x12, local copies, waits for them, and re-layouts  1.96 us
  transfers between devices with their start and end apart: 23, of which 11 were waited for; matrix products, arithmetic and copies ran while one was open for 1% of the time, Pallas kernels for 1%

profile of v4, /device:TPU:17, one launch (start us, length us, event | category | flops | bytes accessed | tf_op | source)
XLA Modules:
  0.0 96.4 jit_solution(1698054569002831682)
XLA Ops:
  0.0 1.3 %copy-done = f32[1,1,1,4,2,64,512]{6,5,4,3,2,1,0:T(8,128)S(1)} copy-done((f32[1,1,1,4,2,64,512]{6,5,4,3,2,1,0:T(8,128)S(1)}, f32[1,1,1,4,2,64,512]{6,5,4,3,2,1,0:T(8,128)}, u32[]{:S(2)}) %copy-start) | copy-done | bytes 1048600
  1.3 0.7 copy-done.2
  2.1 1.3 %collective-permute-start.7 = (f32[520,512]{1,0:T(8,128)S(1)}, f32[520,512]{1,0:T(8,128)S(1)}, u32[]{:S(2)}, u32[]{:S(2)}) collective-permute-start(f32[520,512]{1,0:T(8,128)S(1)} %shard_map.65.refs_8_), channel_id=1, source_target_pairs={{0,1},{1,0},{2,3},{3,2},{4,5},{5,4},{6,7},{7,6},{8,9},{9,8},{10,11... | collective-permute-start | bytes 3194888 | tf_op jit(solution)/shard_map/ppermute | solution.py:20
  3.8 1.2 %collective-permute-start.1 = (f32[520,128]{1,0:T(8,128)S(1)}, f32[520,128]{1,0:T(8,128)S(1)}, u32[]{:S(2)}, u32[]{:S(2)}) collective-permute-start(f32[520,128]{1,0:T(8,128)S(1)} %shard_map.64.refs_0_), channel_id=1, source_target_pairs={{0,2},{2,0},{4,6},{6,4},{8,10},{10,8},{12,14},{14,12},{1,3},{3,1},... | collective-permute-start | bytes 798728 | tf_op jit(solution)/shard_map/ppermute | solution.py:20
  5.0 1.3 %collective-permute-start = (f32[520,128]{1,0:T(8,128)S(1)}, f32[520,128]{1,0:T(8,128)S(1)}, u32[]{:S(2)}, u32[]{:S(2)}) collective-permute-start(f32[520,128]{1,0:T(8,128)S(1)} %shard_map.64.refs_0_), channel_id=1, source_target_pairs={{0,4},{2,6},{4,0},{6,2},{8,12},{10,14},{12,8},{14,10},{1,5},{3,7},... | collective-permute-start | bytes 798728 | tf_op jit(solution)/shard_map/ppermute | solution.py:20
  6.5 8.1 %collective-permute-done.3.refs_4_ = f32[520,128]{1,0:T(8,128)S(1)} collective-permute-done((f32[520,128]{1,0:T(8,128)S(1)}, f32[520,128]{1,0:T(8,128)S(1)}, u32[]{:S(2)}, u32[]{:S(2)}) %collective-permute-start.3) | collective-permute-done | bytes 266272 | tf_op jit(solution)/shard_map/ppermute | solution.py:20
  14.6 5.3 %collective-permute-start.5 = (f32[520,128]{1,0:T(8,128)S(1)}, f32[520,128]{1,0:T(8,128)S(1)}, u32[]{:S(2)}, u32[]{:S(2)}) collective-permute-start(f32[520,128]{1,0:T(8,128)S(1)} %collective-permute-done.3.refs_4_), channel_id=1, source_target_pairs={{0,4},{2,6},{4,0},{6,2},{8,12},{10,14},{12,8},{14,10},{1,5},{3,7},... | collective-permute-start | bytes 798728 | tf_op jit(solution)/shard_map/ppermute | solution.py:20
  19.9 0.6 select_reduce_fusion
  20.6 0.9 collective-permute-start.2
  21.6 4.6 %collective-permute-done.5.refs_6_ = f32[520,128]{1,0:T(8,128)S(1)} collective-permute-done((f32[520,128]{1,0:T(8,128)S(1)}, f32[520,128]{1,0:T(8,128)S(1)}, u32[]{:S(2)}, u32[]{:S(2)}) %collective-permute-start.5) | collective-permute-done | bytes 266272 | tf_op jit(solution)/shard_map/ppermute | solution.py:20
  26.1 1.1 %collective-permute-start.6 = (f32[520,128]{1,0:T(8,128)S(1)}, f32[520,128]{1,0:T(8,128)S(1)}, u32[]{:S(2)}, u32[]{:S(2)}) collective-permute-start(f32[520,128]{1,0:T(8,128)S(1)} %collective-permute-done.5.refs_6_), channel_id=1, source_target_pairs={{0,2},{2,0},{4,6},{6,4},{8,10},{10,8},{12,14},{14,12},{1,3},{3,1},... | collective-permute-start | bytes 798728 | tf_op jit(solution)/shard_map/ppermute | solution.py:20
  27.2 1.2 %collective-permute-done.6.refs_7_ = f32[520,128]{1,0:T(8,128)S(1)} collective-permute-done((f32[520,128]{1,0:T(8,128)S(1)}, f32[520,128]{1,0:T(8,128)S(1)}, u32[]{:S(2)}, u32[]{:S(2)}) %collective-permute-start.6) | collective-permute-done | bytes 266272 | tf_op jit(solution)/shard_map/ppermute | solution.py:20
  28.4 7.3 %shard_map.66 = (f32[1,2,32,8,128]{4,3,2,1,0:T(8,128)S(1)}, f32[1,2,32,8,128]{4,3,2,1,0:T(8,128)S(1)}, f32[1,2,32,8,128]{4,3,2,1,0:T(8,128)S(1)}, f32[1,2,32,8,1...) custom-call(s32[64,128]{1,0:T(8,128)S(1)} %pad.4.table_ref, ...), custom_call_target="tpu_custom_call" | custom-call | flops 2147483648 | bytes 8454144 | tf_op jit(solution)/shard_map/pallas_call | solution.py:284
  35.7 1.3 %collective-permute-start.8 = (f32[1,2,32,8,128]{4,3,2,1,0:T(8,128)S(1)}, f32[1,2,32,8,128]{4,3,2,1,0:T(8,128)S(1)}, u32[]{:S(2)}, u32[]{:S(2)}) collective-permute-start(f32[1,2,32,8,128]{4,3,2,1,0:T(8,128)S(1)} %get-tuple-element.37), channel_id=1, source_target_pairs={{0,16},{16,0},{1,17},{17,1},{2,18},{18,2},{3,19},{19,3},{4,20},{20... | collective-permute-start | bytes 786440 | tf_op jit(solution)/shard_map/ppermute | solution.py:20
  37.2 1.2 %collective-permute-start.15 = (f32[1,2,32,8,128]{4,3,2,1,0:T(8,128)S(1)}, f32[1,2,32,8,128]{4,3,2,1,0:T(8,128)S(1)}, u32[]{:S(2)}, u32[]{:S(2)}) collective-permute-start(f32[1,2,32,8,128]{4,3,2,1,0:T(8,128)S(1)} %get-tuple-element.47), channel_id=1, source_target_pairs={{0,16},{16,0},{1,17},{17,1},{2,18},{18,2},{3,19},{19,3},{4,20},{20... | collective-permute-start | bytes 786440 | tf_op jit(solution)/shard_map/ppermute | solution.py:20
  38.7 4.6 %collective-permute-done.8 = f32[1,2,32,8,128]{4,3,2,1,0:T(8,128)S(1)} collective-permute-done((f32[1,2,32,8,128]{4,3,2,1,0:T(8,128)S(1)}, f32[1,2,32,8,128]{4,3,2,1,0:T(8,128)S(1)}, u32[]{:S(2)}, u32[]{:S(2)}) %collective-permute-start.8) | collective-permute-done | bytes 262176 | tf_op jit(solution)/shard_map/ppermute | solution.py:20
  43.4 5.5 %collective-permute-done.12 = f32[1,2,32,8,128]{4,3,2,1,0:T(8,128)S(1)} collective-permute-done((f32[1,2,32,8,128]{4,3,2,1,0:T(8,128)S(1)}, f32[1,2,32,8,128]{4,3,2,1,0:T(8,128)S(1)}, u32[]{:S(2)}, u32[]{:S(2)}) %collective-permute-start.12) | collective-permute-done | bytes 262176 | tf_op jit(solution)/shard_map/ppermute | solution.py:20
  48.9 1.2 %collective-permute-start.13 = (f32[1,2,32,8,128]{4,3,2,1,0:T(8,128)S(1)}, f32[1,2,32,8,128]{4,3,2,1,0:T(8,128)S(1)}, u32[]{:S(2)}, u32[]{:S(2)}) collective-permute-start(f32[1,2,32,8,128]{4,3,2,1,0:T(8,128)S(1)} %get-tuple-element.44), channel_id=1, source_target_pairs={{0,16},{16,0},{1,17},{17,1},{2,18},{18,2},{3,19},{19,3},{4,20},{20... | collective-permute-start | bytes 786440 | tf_op jit(solution)/shard_map/ppermute | solution.py:20
  50.2 1.5 %collective-permute-start.16 = (f32[2,32,8,128]{3,2,1,0:T(8,128)S(1)}, f32[2,32,8,128]{3,2,1,0:T(8,128)S(1)}, u32[]{:S(2)}, u32[]{:S(2)}) collective-permute-start(f32[2,32,8,128]{3,2,1,0:T(8,128)S(1)} %add_bitcast_fusion.4), channel_id=1, source_target_pairs={{0,10},{2,8},{4,14},{6,12},{8,2},{10,0},{12,6},{14,4},{1,11},{3,9}... | collective-permute-start | bytes 786440 | tf_op jit(solution)/shard_map/ppermute | solution.py:20
  51.7 2.8 %collective-permute-done.15 = f32[1,2,32,8,128]{4,3,2,1,0:T(8,128)S(1)} collective-permute-done((f32[1,2,32,8,128]{4,3,2,1,0:T(8,128)S(1)}, f32[1,2,32,8,128]{4,3,2,1,0:T(8,128)S(1)}, u32[]{:S(2)}, u32[]{:S(2)}) %collective-permute-start.15) | collective-permute-done | bytes 262176 | tf_op jit(solution)/shard_map/ppermute | solution.py:20
  55.1 9.9 %collective-permute-done.9.refs_0_ = f32[2,32,8,128]{3,2,1,0:T(8,128)S(1)} collective-permute-done((f32[2,32,8,128]{3,2,1,0:T(8,128)S(1)}, f32[2,32,8,128]{3,2,1,0:T(8,128)S(1)}, u32[]{:S(2)}, u32[]{:S(2)}) %collective-permute-start.9) | collective-permute-done | bytes 262176 | tf_op jit(solution)/shard_map/ppermute | solution.py:20
  65.0 1.5 %collective-permute-start.10 = (f32[1,2,32,8,128]{4,3,2,1,0:T(8,128)S(1)}, f32[1,2,32,8,128]{4,3,2,1,0:T(8,128)S(1)}, u32[]{:S(2)}, u32[]{:S(2)}) collective-permute-start(f32[1,2,32,8,128]{4,3,2,1,0:T(8,128)S(1)} %get-tuple-element.40), channel_id=1, source_target_pairs={{0,16},{16,0},{1,17},{17,1},{2,18},{18,2},{3,19},{19,3},{4,20},{20... | collective-permute-start | bytes 786440 | tf_op jit(solution)/shard_map/ppermute | solution.py:20
  66.5 5.4 %collective-permute-start.21 = (f32[2,32,8,128]{3,2,1,0:T(8,128)S(1)}, f32[2,32,8,128]{3,2,1,0:T(8,128)S(1)}, u32[]{:S(2)}, u32[]{:S(2)}) collective-permute-start(f32[2,32,8,128]{3,2,1,0:T(8,128)S(1)} %add_bitcast_fusion.1), channel_id=1, source_target_pairs={{0,4},{2,6},{4,0},{6,2},{8,12},{10,14},{12,8},{14,10},{1,5},{3,7},... | collective-permute-start | bytes 786440 | tf_op jit(solution)/shard_map/ppermute | solution.py:20
  72.2 6.0 %collective-permute-start.14 = (f32[2,32,8,128]{3,2,1,0:T(8,128)S(1)}, f32[2,32,8,128]{3,2,1,0:T(8,128)S(1)}, u32[]{:S(2)}, u32[]{:S(2)}) collective-permute-start(f32[2,32,8,128]{3,2,1,0:T(8,128)S(1)} %add_bitcast_fusion.5), channel_id=1, source_target_pairs={{0,6},{2,4},{4,2},{6,0},{8,14},{10,12},{12,10},{14,8},{1,7},{3,5},... | collective-permute-start | bytes 786440 | tf_op jit(solution)/shard_map/ppermute | solution.py:20
  78.2 2.4 %collective-permute-done.20.refs_2_ = f32[2,32,8,128]{3,2,1,0:T(8,128)S(1)} collective-permute-done((f32[2,32,8,128]{3,2,1,0:T(8,128)S(1)}, f32[2,32,8,128]{3,2,1,0:T(8,128)S(1)}, u32[]{:S(2)}, u32[]{:S(2)}) %collective-permute-start.20) | collective-permute-done | bytes 262176 | tf_op jit(solution)/shard_map/ppermute | solution.py:20
  80.6 1.3 %collective-permute-start.22 = (f32[1,2,32,8,128]{4,3,2,1,0:T(8,128)S(1)}, f32[1,2,32,8,128]{4,3,2,1,0:T(8,128)S(1)}, u32[]{:S(2)}, u32[]{:S(2)}) collective-permute-start(f32[1,2,32,8,128]{4,3,2,1,0:T(8,128)S(1)} %get-tuple-element.60), channel_id=1, source_target_pairs={{0,16},{16,0},{1,17},{17,1},{2,18},{18,2},{3,19},{19,3},{4,20},{20... | collective-permute-start | bytes 786440 | tf_op jit(solution)/shard_map/ppermute | solution.py:20
  82.1 0.8 collective-permute-start.18
  82.9 5.1 %collective-permute-done.22 = f32[1,2,32,8,128]{4,3,2,1,0:T(8,128)S(1)} collective-permute-done((f32[1,2,32,8,128]{4,3,2,1,0:T(8,128)S(1)}, f32[1,2,32,8,128]{4,3,2,1,0:T(8,128)S(1)}, u32[]{:S(2)}, u32[]{:S(2)}) %collective-permute-start.22) | collective-permute-done | bytes 262176 | tf_op jit(solution)/shard_map/ppermute | solution.py:20
  88.0 1.1 %shard_map.67.refs_3_ = f32[16,32,8,128]{3,2,1,0:T(8,128)} custom-call(f32[2,32,8,128]{3,2,1,0:T(8,128)S(1)} %collective-permute-done.9.refs_0_, f32[2,32,8,128]{3,2,1,0:T(8,128)S(1)} %collective-permute-done.16.refs_1_, f32[2,32,8,128]{3,2,1,0:T(8,128)S(1)} %collective-permute-done.20.refs_2_, f32[2,32,8,128]{3,2,1,0:T(8,128)S(1)} %collective-permute-done.21.refs_3_, ...), custom_call_target="tpu_custom_call" | custom-call | tf_op jit(solution)/shard_map/pallas_call | solution.py:324
  89.2 1.7 %collective-permute-done.14.refs_1_ = f32[2,32,8,128]{3,2,1,0:T(8,128)S(1)} collective-permute-done((f32[2,32,8,128]{3,2,1,0:T(8,128)S(1)}, f32[2,32,8,128]{3,2,1,0:T(8,128)S(1)}, u32[]{:S(2)}, u32[]{:S(2)}) %collective-permute-start.14) | collective-permute-done | bytes 262176 | tf_op jit(solution)/shard_map/ppermute | solution.py:20
  90.8 4.7 %collective-permute-done.11.refs_0_ = f32[2,32,8,128]{3,2,1,0:T(8,128)S(1)} collective-permute-done((f32[2,32,8,128]{3,2,1,0:T(8,128)S(1)}, f32[2,32,8,128]{3,2,1,0:T(8,128)S(1)}, u32[]{:S(2)}, u32[]{:S(2)}) %collective-permute-start.11) | collective-permute-done | bytes 262176 | tf_op jit(solution)/shard_map/ppermute | solution.py:20
  95.5 0.9 shard_map.68
  (45 shorter events, 2.7 us)
Async XLA Ops:
  0.0 3.3 %copy-start.3 = (s32[1,1,1,2,8]{4,3,2,1,0:T(2,128)S(1)}, s32[1,1,1,2,8]{4,3,2,1,0:T(2,128)}, u32[]{:S(2)}) copy-start(s32[1,1,1,2,8]{4,3,2,1,0:T(2,128)} %param.7) | copy-start | bytes 196
  0.0 6.3 %copy-start.4 = (s32[1,256,1]{1,2,0:T(1,128)S(1)}, s32[1,256,1]{1,2,0:T(1,128)}, u32[]{:S(2)}) copy-start(s32[1,256,1]{1,2,0:T(1,128)} %param.11) | copy-start | bytes 3076
  0.0 19.9 %copy-start.5 = (s32[1,1,256]{2,1,0:T(1,128)S(1)}, s32[1,1,256]{2,1,0:T(1,128)}, u32[]{:S(2)}) copy-start(s32[1,1,256]{2,1,0:T(1,128)} %param.10) | copy-start | bytes 3076
  0.0 1.3 %copy-start = (f32[1,1,1,4,2,64,512]{6,5,4,3,2,1,0:T(8,128)S(1)}, f32[1,1,1,4,2,64,512]{6,5,4,3,2,1,0:T(8,128)}, u32[]{:S(2)}) copy-start(f32[1,1,1,4,2,64,512]{6,5,4,3,2,1,0:T(8,128)} %param.8) | copy-start | bytes 3145732
  1.3 0.7 copy-start.2
  2.0 1.4 %copy-start.1 = (f32[1,1,1,2,64,512]{5,4,3,2,1,0:T(8,128)S(1)}, f32[1,1,1,2,64,512]{5,4,3,2,1,0:T(8,128)}, u32[]{:S(2)}) copy-start(f32[1,1,1,2,64,512]{5,4,3,2,1,0:T(8,128)} %param.6) | copy-start | bytes 786436
  2.1 26.4 %collective-permute-start.7 = (f32[520,512]{1,0:T(8,128)S(1)}, f32[520,512]{1,0:T(8,128)S(1)}, u32[]{:S(2)}, u32[]{:S(2)}) collective-permute-start(f32[520,512]{1,0:T(8,128)S(1)} %shard_map.65.refs_8_), channel_id=1, source_target_pairs={{0,1},{1,0},{2,3},{3,2},{4,5},{5,4},{6,7},{7,6},{8,9},{9,8},{10,11... | collective-permute-start | bytes 3194888 | tf_op jit(solution)/shard_map/ppermute | solution.py:20
  3.7 10.9 %collective-permute-start.3 = (f32[520,128]{1,0:T(8,128)S(1)}, f32[520,128]{1,0:T(8,128)S(1)}, u32[]{:S(2)}, u32[]{:S(2)}) collective-permute-start(f32[520,128]{1,0:T(8,128)S(1)} %shard_map.64.refs_0_), channel_id=1, source_target_pairs={{0,8},{2,10},{4,12},{6,14},{8,0},{10,2},{12,4},{14,6},{1,9},{3,11}... | collective-permute-start | bytes 798728 | tf_op jit(solution)/shard_map/ppermute | solution.py:20
  3.8 23.4 %collective-permute-start.1 = (f32[520,128]{1,0:T(8,128)S(1)}, f32[520,128]{1,0:T(8,128)S(1)}, u32[]{:S(2)}, u32[]{:S(2)}) collective-permute-start(f32[520,128]{1,0:T(8,128)S(1)} %shard_map.64.refs_0_), channel_id=1, source_target_pairs={{0,2},{2,0},{4,6},{6,4},{8,10},{10,8},{12,14},{14,12},{1,3},{3,1},... | collective-permute-start | bytes 798728 | tf_op jit(solution)/shard_map/ppermute | solution.py:20
  5.0 15.6 %collective-permute-start = (f32[520,128]{1,0:T(8,128)S(1)}, f32[520,128]{1,0:T(8,128)S(1)}, u32[]{:S(2)}, u32[]{:S(2)}) collective-permute-start(f32[520,128]{1,0:T(8,128)S(1)} %shard_map.64.refs_0_), channel_id=1, source_target_pairs={{0,4},{2,6},{4,0},{6,2},{8,12},{10,14},{12,8},{14,10},{1,5},{3,7},... | collective-permute-start | bytes 798728 | tf_op jit(solution)/shard_map/ppermute | solution.py:20
  14.6 11.6 %collective-permute-start.5 = (f32[520,128]{1,0:T(8,128)S(1)}, f32[520,128]{1,0:T(8,128)S(1)}, u32[]{:S(2)}, u32[]{:S(2)}) collective-permute-start(f32[520,128]{1,0:T(8,128)S(1)} %collective-permute-done.3.refs_4_), channel_id=1, source_target_pairs={{0,4},{2,6},{4,0},{6,2},{8,12},{10,14},{12,8},{14,10},{1,5},{3,7},... | collective-permute-start | bytes 798728 | tf_op jit(solution)/shard_map/ppermute | solution.py:20
  20.6 6.6 %collective-permute-start.2 = (f32[520,128]{1,0:T(8,128)S(1)}, f32[520,128]{1,0:T(8,128)S(1)}, u32[]{:S(2)}, u32[]{:S(2)}) collective-permute-start(f32[520,128]{1,0:T(8,128)S(1)} %collective-permute-done.refs_2_), channel_id=1, source_target_pairs={{0,2},{2,0},{4,6},{6,4},{8,10},{10,8},{12,14},{14,12},{1,3},{3,1},... | collective-permute-start | bytes 798728 | tf_op jit(solution)/shard_map/ppermute | solution.py:20
  21.5 5.7 %collective-permute-start.4 = (f32[520,128]{1,0:T(8,128)S(1)}, f32[520,128]{1,0:T(8,128)S(1)}, u32[]{:S(2)}, u32[]{:S(2)}) collective-permute-start(f32[520,128]{1,0:T(8,128)S(1)} %collective-permute-done.3.refs_4_), channel_id=1, source_target_pairs={{0,2},{2,0},{4,6},{6,4},{8,10},{10,8},{12,14},{14,12},{1,3},{3,1},... | collective-permute-start | bytes 798728 | tf_op jit(solution)/shard_map/ppermute | solution.py:20
  26.1 2.3 %collective-permute-start.6 = (f32[520,128]{1,0:T(8,128)S(1)}, f32[520,128]{1,0:T(8,128)S(1)}, u32[]{:S(2)}, u32[]{:S(2)}) collective-permute-start(f32[520,128]{1,0:T(8,128)S(1)} %collective-permute-done.5.refs_6_), channel_id=1, source_target_pairs={{0,2},{2,0},{4,6},{6,4},{8,10},{10,8},{12,14},{14,12},{1,3},{3,1},... | collective-permute-start | bytes 798728 | tf_op jit(solution)/shard_map/ppermute | solution.py:20
  35.7 7.6 %collective-permute-start.8 = (f32[1,2,32,8,128]{4,3,2,1,0:T(8,128)S(1)}, f32[1,2,32,8,128]{4,3,2,1,0:T(8,128)S(1)}, u32[]{:S(2)}, u32[]{:S(2)}) collective-permute-start(f32[1,2,32,8,128]{4,3,2,1,0:T(8,128)S(1)} %get-tuple-element.37), channel_id=1, source_target_pairs={{0,16},{16,0},{1,17},{17,1},{2,18},{18,2},{3,19},{19,3},{4,20},{20... | collective-permute-start | bytes 786440 | tf_op jit(solution)/shard_map/ppermute | solution.py:20
  37.0 11.9 %collective-permute-start.12 = (f32[1,2,32,8,128]{4,3,2,1,0:T(8,128)S(1)}, f32[1,2,32,8,128]{4,3,2,1,0:T(8,128)S(1)}, u32[]{:S(2)}, u32[]{:S(2)}) collective-permute-start(f32[1,2,32,8,128]{4,3,2,1,0:T(8,128)S(1)} %get-tuple-element.43), channel_id=1, source_target_pairs={{0,16},{16,0},{1,17},{17,1},{2,18},{18,2},{3,19},{19,3},{4,20},{20... | collective-permute-start | bytes 786440 | tf_op jit(solution)/shard_map/ppermute | solution.py:20
  37.2 17.3 %collective-permute-start.15 = (f32[1,2,32,8,128]{4,3,2,1,0:T(8,128)S(1)}, f32[1,2,32,8,128]{4,3,2,1,0:T(8,128)S(1)}, u32[]{:S(2)}, u32[]{:S(2)}) collective-permute-start(f32[1,2,32,8,128]{4,3,2,1,0:T(8,128)S(1)} %get-tuple-element.47), channel_id=1, source_target_pairs={{0,16},{16,0},{1,17},{17,1},{2,18},{18,2},{3,19},{19,3},{4,20},{20... | collective-permute-start | bytes 786440 | tf_op jit(solution)/shard_map/ppermute | solution.py:20
  38.4 28.0 %collective-permute-start.19 = (f32[1,2,32,8,128]{4,3,2,1,0:T(8,128)S(1)}, f32[1,2,32,8,128]{4,3,2,1,0:T(8,128)S(1)}, u32[]{:S(2)}, u32[]{:S(2)}) collective-permute-start(f32[1,2,32,8,128]{4,3,2,1,0:T(8,128)S(1)} %get-tuple-element.54), channel_id=1, source_target_pairs={{0,16},{16,0},{1,17},{17,1},{2,18},{18,2},{3,19},{19,3},{4,20},{20... | collective-permute-start | bytes 786440 | tf_op jit(solution)/shard_map/ppermute | solution.py:20
  43.3 21.7 %collective-permute-start.9 = (f32[2,32,8,128]{3,2,1,0:T(8,128)S(1)}, f32[2,32,8,128]{3,2,1,0:T(8,128)S(1)}, u32[]{:S(2)}, u32[]{:S(2)}) collective-permute-start(f32[2,32,8,128]{3,2,1,0:T(8,128)S(1)} %add_bitcast_fusion.7), channel_id=1, source_target_pairs={{0,8},{2,10},{4,12},{6,14},{8,0},{10,2},{12,4},{14,6},{1,9},{3,11}... | collective-permute-start | bytes 786440 | tf_op jit(solution)/shard_map/ppermute | solution.py:20
  48.9 23.2 %collective-permute-start.13 = (f32[1,2,32,8,128]{4,3,2,1,0:T(8,128)S(1)}, f32[1,2,32,8,128]{4,3,2,1,0:T(8,128)S(1)}, u32[]{:S(2)}, u32[]{:S(2)}) collective-permute-start(f32[1,2,32,8,128]{4,3,2,1,0:T(8,128)S(1)} %get-tuple-element.44), channel_id=1, source_target_pairs={{0,16},{16,0},{1,17},{17,1},{2,18},{18,2},{3,19},{19,3},{4,20},{20... | collective-permute-start | bytes 786440 | tf_op jit(solution)/shard_map/ppermute | solution.py:20
  50.2 21.7 %collective-permute-start.16 = (f32[2,32,8,128]{3,2,1,0:T(8,128)S(1)}, f32[2,32,8,128]{3,2,1,0:T(8,128)S(1)}, u32[]{:S(2)}, u32[]{:S(2)}) collective-permute-start(f32[2,32,8,128]{3,2,1,0:T(8,128)S(1)} %add_bitcast_fusion.4), channel_id=1, source_target_pairs={{0,10},{2,8},{4,14},{6,12},{8,2},{10,0},{12,6},{14,4},{1,11},{3,9}... | collective-permute-start | bytes 786440 | tf_op jit(solution)/shard_map/ppermute | solution.py:20
  54.6 26.1 %collective-permute-start.20 = (f32[2,32,8,128]{3,2,1,0:T(8,128)S(1)}, f32[2,32,8,128]{3,2,1,0:T(8,128)S(1)}, u32[]{:S(2)}, u32[]{:S(2)}) collective-permute-start(f32[2,32,8,128]{3,2,1,0:T(8,128)S(1)} %add_bitcast_fusion.2), channel_id=1, source_target_pairs={{0,12},{2,14},{4,8},{6,10},{8,4},{10,6},{12,0},{14,2},{1,13},{3,15... | collective-permute-start | bytes 786440 | tf_op jit(solution)/shard_map/ppermute | solution.py:20
  65.0 16.9 %collective-permute-start.10 = (f32[1,2,32,8,128]{4,3,2,1,0:T(8,128)S(1)}, f32[1,2,32,8,128]{4,3,2,1,0:T(8,128)S(1)}, u32[]{:S(2)}, u32[]{:S(2)}) collective-permute-start(f32[1,2,32,8,128]{4,3,2,1,0:T(8,128)S(1)} %get-tuple-element.40), channel_id=1, source_target_pairs={{0,16},{16,0},{1,17},{17,1},{2,18},{18,2},{3,19},{19,3},{4,20},{20... | collective-permute-start | bytes 786440 | tf_op jit(solution)/shard_map/ppermute | solution.py:20
  66.5 21.5 %collective-permute-start.21 = (f32[2,32,8,128]{3,2,1,0:T(8,128)S(1)}, f32[2,32,8,128]{3,2,1,0:T(8,128)S(1)}, u32[]{:S(2)}, u32[]{:S(2)}) collective-permute-start(f32[2,32,8,128]{3,2,1,0:T(8,128)S(1)} %add_bitcast_fusion.1), channel_id=1, source_target_pairs={{0,4},{2,6},{4,0},{6,2},{8,12},{10,14},{12,8},{14,10},{1,5},{3,7},... | collective-permute-start | bytes 786440 | tf_op jit(solution)/shard_map/ppermute | solution.py:20
  71.9 10.1 %collective-permute-start.17 = (f32[1,2,32,8,128]{4,3,2,1,0:T(8,128)S(1)}, f32[1,2,32,8,128]{4,3,2,1,0:T(8,128)S(1)}, u32[]{:S(2)}, u32[]{:S(2)}) collective-permute-start(f32[1,2,32,8,128]{4,3,2,1,0:T(8,128)S(1)} %get-tuple-element.50), channel_id=1, source_target_pairs={{0,16},{16,0},{1,17},{17,1},{2,18},{18,2},{3,19},{19,3},{4,20},{20... | collective-permute-start | bytes 786440 | tf_op jit(solution)/shard_map/ppermute | solution.py:20
  72.2 18.6 %collective-permute-start.14 = (f32[2,32,8,128]{3,2,1,0:T(8,128)S(1)}, f32[2,32,8,128]{3,2,1,0:T(8,128)S(1)}, u32[]{:S(2)}, u32[]{:S(2)}) collective-permute-start(f32[2,32,8,128]{3,2,1,0:T(8,128)S(1)} %add_bitcast_fusion.5), channel_id=1, source_target_pairs={{0,6},{2,4},{4,2},{6,0},{8,14},{10,12},{12,10},{14,8},{1,7},{3,5},... | collective-permute-start | bytes 786440 | tf_op jit(solution)/shard_map/ppermute | solution.py:20
  80.6 7.4 %collective-permute-start.22 = (f32[1,2,32,8,128]{4,3,2,1,0:T(8,128)S(1)}, f32[1,2,32,8,128]{4,3,2,1,0:T(8,128)S(1)}, u32[]{:S(2)}, u32[]{:S(2)}) collective-permute-start(f32[1,2,32,8,128]{4,3,2,1,0:T(8,128)S(1)} %get-tuple-element.60), channel_id=1, source_target_pairs={{0,16},{16,0},{1,17},{17,1},{2,18},{18,2},{3,19},{19,3},{4,20},{20... | collective-permute-start | bytes 786440 | tf_op jit(solution)/shard_map/ppermute | solution.py:20
  81.9 13.6 %collective-permute-start.11 = (f32[2,32,8,128]{3,2,1,0:T(8,128)S(1)}, f32[2,32,8,128]{3,2,1,0:T(8,128)S(1)}, u32[]{:S(2)}, u32[]{:S(2)}) collective-permute-start(f32[2,32,8,128]{3,2,1,0:T(8,128)S(1)} %add_bitcast_fusion.6), channel_id=1, source_target_pairs={{0,14},{2,12},{4,10},{6,8},{8,6},{10,4},{12,2},{14,0},{1,15},{3,13... | collective-permute-start | bytes 786440 | tf_op jit(solution)/shard_map/ppermute | solution.py:20
  82.1 13.4 %collective-permute-start.18 = (f32[2,32,8,128]{3,2,1,0:T(8,128)S(1)}, f32[2,32,8,128]{3,2,1,0:T(8,128)S(1)}, u32[]{:S(2)}, u32[]{:S(2)}) collective-permute-start(f32[2,32,8,128]{3,2,1,0:T(8,128)S(1)} %add_bitcast_fusion.3), channel_id=1, source_target_pairs={{0,2},{2,0},{4,6},{6,4},{8,10},{10,8},{12,14},{14,12},{1,3},{3,1},... | collective-permute-start | bytes 786440 | tf_op jit(solution)/shard_map/ppermute | solution.py:20
